TPU v7x, 32 devices: a whole 2x2x4 slice. The times are simulated.
32 devices in a mesh: phase: 4 (over y, x), slab: 8 (over z, core).
Axes of the slice: x: 2, y: 2, z: 4, core: 2. Of those that a mesh axis runs over, the one named last changes fastest.
Arguments:
- normed: bfloat16 [16, 16, 128, 1024], P('phase', 'slab'), may hold values from -5 to 5
- block_list: int32 [16, 16, 5], P('phase', 'slab'), may hold values from 0 to 255, as said below
- registers: bfloat16 [256, 1024], replicated, may hold values from -5 to 5
- w_query: bfloat16 [1024, 1024], replicated, may hold values from -0.25 to 0.25
- w_key: bfloat16 [1024, 1024], replicated, may hold values from -0.25 to 0.25
- w_value: bfloat16 [1024, 1024], replicated, may hold values from -0.1875 to 0.1875
- w_out: bfloat16 [1024, 1024], replicated, may hold values from -0.1875 to 0.1875
Outputs:
- mixed: bfloat16 [16, 16, 128, 1024], P('phase', 'slab')
- register_out: bfloat16 [256, 1024], replicated
Inputs may be any that keep to these rules, and one draw needn't show every extreme that they name: Entry 0 of block_list[p, z] is p * 16 + z itself; the 5 entries of a list are distinct, and each names a block (p2, z2) with p2 one of p - 1, p, p + 1 taken modulo 16 and z2 one of z - 1, z, z + 1 within 0 to 15.
All inputs are finite; a program needn't handle non-finite values.
Results may differ from a plain program's by a relative error of at most 0.01.
Values may be sent and summed in bfloat16 or wider, within the bound.
No kernel may reach another device: no remote copies, remote signals or barrier semaphores. Data moves between devices by JAX's collectives and lax.ppermute only.
A program may use at most 192 MiB of HBM per device.

v0:
```python
import jax
import jax.numpy as jnp
from jax import lax
from jax.sharding import PartitionSpec as P

HEADS = 16
LIST = 5


def with_halo(cells, sides, width, closed):
    for axis, dim in sides:
        count = lax.axis_size(axis)
        ends = count if closed else count - 1
        head = lax.slice_in_dim(cells, 0, width, axis=dim)
        tail = lax.slice_in_dim(cells, cells.shape[dim] - width, cells.shape[dim], axis=dim)
        cells = jnp.concatenate(
            [
                lax.ppermute(tail, axis, [(i, (i + 1) % count) for i in range(ends)]),
                cells,
                lax.ppermute(head, axis, [((i + 1) % count, i) for i in range(ends)]),
            ],
            axis=dim,
        )
    return cells


def project(token_rows, weight):
    return jnp.dot(token_rows, weight, preferred_element_type=jnp.float32).astype(jnp.bfloat16)


def window_attend(group_queries, key_rows, value_rows, register_keys, register_values, score_scale):
    local_scores = (
        jnp.einsum("gqhe,gkhe->ghqk", group_queries, key_rows, preferred_element_type=jnp.float32)
        * score_scale
    )
    remote = (
        jnp.einsum(
            "gqhe,rhe->ghqr", group_queries, register_keys, preferred_element_type=jnp.float32
        )
        * score_scale
    )
    scores = jnp.concatenate([local_scores, remote], axis=-1)
    row_peak = jnp.max(scores, axis=-1, keepdims=True)
    shifted = jnp.exp(scores - row_peak)
    probabilities = (shifted / jnp.sum(shifted, axis=-1, keepdims=True)).astype(jnp.bfloat16)
    key_count = key_rows.shape[1]
    context = jnp.einsum(
        "ghqk,gkhe->gqhe",
        probabilities[..., :key_count],
        value_rows,
        preferred_element_type=jnp.float32,
    )
    context = context + jnp.einsum(
        "ghqr,rhe->gqhe",
        probabilities[..., key_count:],
        register_values,
        preferred_element_type=jnp.float32,
    )
    return context.astype(jnp.bfloat16)


def shards(normed, block_list, registers, w_query, w_key, w_value, w_out):
    own_phases, slab_blocks, block_len, model_width = normed.shape
    head_count = HEADS
    head_width = model_width // head_count
    score_scale = head_width ** (-0.5)
    block_count = own_phases * slab_blocks
    token_rows = normed.reshape(-1, model_width)
    both_weights = jnp.concatenate((w_key, w_value), axis=1)
    queries = project(token_rows, w_query).reshape(block_count, block_len, head_count, head_width)
    register_query = project(registers, w_query).reshape(-1, head_count, head_width)
    register_pair = project(registers, both_weights)
    register_keys = register_pair[:, :model_width].reshape(-1, head_count, head_width)
    register_values = register_pair[:, model_width:].reshape(-1, head_count, head_width)
    interior = project(token_rows, both_weights).reshape(
        own_phases, slab_blocks, block_len, 2 * model_width
    )
    key_value = with_halo(interior, (("phase", 0),), 1, True)
    key_value = with_halo(key_value, (("slab", 1),), 1, False)
    total_phases = own_phases * lax.axis_size("phase")
    depth_blocks = slab_blocks * lax.axis_size("slab")
    first_phase = lax.axis_index("phase") * own_phases
    first_depth = lax.axis_index("slab") * slab_blocks
    block_phase = block_list // depth_blocks
    block_depth = block_list % depth_blocks
    local_phase = (block_phase - first_phase + 1) % total_phases
    local_depth = block_depth - first_depth + 1
    local_index = (local_phase * (slab_blocks + 2) + local_depth).reshape(block_count, LIST)
    block_table = key_value.reshape(-1, block_len, 2 * model_width)
    per_group = min(block_count, max(1, 512 // block_len))
    while block_count % per_group:
        per_group -= 1
    group_total = block_count // per_group

    def one_group(inputs):
        group_queries, group_index = inputs
        chosen = block_table[group_index.reshape(-1)].reshape(
            per_group, LIST * block_len, 2 * model_width
        )
        key_rows = chosen[..., :model_width].reshape(
            per_group, LIST * block_len, head_count, head_width
        )
        value_rows = chosen[..., model_width:].reshape(
            per_group, LIST * block_len, head_count, head_width
        )
        context = window_attend(
            group_queries, key_rows, value_rows, register_keys, register_values, score_scale
        )
        return project(context.reshape(per_group * block_len, model_width), w_out)

    mixed = lax.map(
        one_group,
        (
            queries.reshape(group_total, per_group, block_len, head_count, head_width),
            local_index.reshape(group_total, per_group, LIST),
        ),
    )
    mixed = mixed.reshape(own_phases, slab_blocks, block_len, model_width)
    local_keys = interior[..., :model_width].reshape(-1, head_count, head_width)
    local_values = interior[..., model_width:].reshape(-1, head_count, head_width)
    scores = (
        jnp.einsum("rhe,the->hrt", register_query, local_keys, preferred_element_type=jnp.float32)
        * score_scale
    )
    row_peak = jnp.max(scores, axis=-1)
    weights = jnp.exp(scores - row_peak[:, :, None]).astype(jnp.bfloat16)
    weight_sum = jnp.sum(weights, axis=-1, dtype=jnp.float32)
    weighted = jnp.einsum("hrt,the->rhe", weights, local_values, preferred_element_type=jnp.float32)
    global_peak = lax.pmax(row_peak, ("phase", "slab"))
    factor = jnp.exp(row_peak - global_peak)
    register_sum, register_value = lax.psum(
        (weight_sum * factor, weighted * factor.T[:, :, None]), ("phase", "slab")
    )
    register_context = (
        (register_value / register_sum.T[:, :, None]).astype(jnp.bfloat16).reshape(-1, model_width)
    )
    register_out = project(register_context, w_out)
    return (mixed, register_out)


def solution(mesh):
    placed = (P("phase", "slab", None, None), P("phase", "slab", None), P(), P(), P(), P(), P())
    return jax.shard_map(
        shards,
        mesh=mesh,
        in_specs=placed,
        out_specs=(P("phase", "slab", None, None), P()),
        check_vma=False,
    )
```

profile of v0, /device:TPU:0, one launch (start us, length us, event | category | flops | bytes accessed | tf_op | source)
XLA Modules:
  0.0 443.4 jit_solution(18075583382627763853)
XLA Ops:
  10.0 4.8 %convolution_convert_fusion.1 = bf16[2048,1024]{0,1:T(8,128)(2,1)S(1)} fusion(bf16[1024,1024]{1,0:T(8,128)(2,1)S(1)} %bitcast.116, bf16[1024,2048]{1,0:T(8,128)(2,1)S(1)} %constant_dynamic-update-slice_fusion), kind=kOutput, calls=%fused_computation.35 | convolution fusion | flops 4297064448 | bytes 10485760 | tf_op jit(solution)/shard_map/dot_general | solution.py:28
  23.0 6.1 %copy.30 = bf16[4,2,128,1024]{2,1,0,3:T(2,128)(2,1)} copy(bf16[4,2,128,1024]{3,2,1,0:T(8,128)(2,1)} %get-tuple-element.85) | data formatting | bytes 4194304 | tf_op jit(solution)/shard_map/slice | solution.py:119
  29.2 4.4 reshape.97
  39.0 9.9 %multiply_reduce_fusion = (f32[16,256]{1,0:T(8,128)S(1)}, f32[16,256,1024]{2,1,0:T(8,128)}) fusion(bf16[256,16,64]{0,2,1:T(8,128)(2,1)} %bitcast.129, bf16[1024,16,64]{0,2,1:T(8,128)(2,1)} %reshape.97), kind=kOutput, calls=%fused_computation.32 | convolution fusion | flops 545255424 | bytes 19415040 | tf_op jit(solution)/shard_map/rhe,the->hrt/dot_general | solution.py:122
  48.8 52.0 %pmax.7 = f32[16,256]{1,0:T(8,128)S(1)} all-reduce(f32[16,256]{1,0:T(8,128)S(1)} %get-tuple-element.93), channel_id=1, replica_groups=mesh['phase'=4,'slab'=8] {'phase','slab'}, use_global_device_ids=true, to_apply=%region_6.7 | all-reduce | flops 4096 | bytes 32768 | tf_op jit(solution)/shard_map/pmax | solution.py:129
  100.8 7.8 %convert_reduce_fusion = f32[16,256]{1,0:T(8,128)S(1)} fusion(f32[16,256]{1,0:T(8,128)S(1)} %get-tuple-element.93, f32[16,256,1024]{2,1,0:T(8,128)} %get-tuple-element.94), kind=kLoop, calls=%fused_computation.30 | loop fusion | flops 20967424 | bytes 16809984 | tf_op jit(solution)/shard_map/reduce_sum | solution.py:127
  118.4 6.2 %copy.28 = bf16[4,2,128,1024]{2,1,0,3:T(2,128)(2,1)} copy(bf16[4,2,128,1024]{3,2,1,0:T(8,128)(2,1)} %get-tuple-element.86) | data formatting | bytes 4194304 | tf_op jit(solution)/shard_map/slice | solution.py:120
  124.6 4.5 %reshape.95 = bf16[1024,16,64]{0,2,1:T(8,128)(2,1)} reshape(bf16[4,2,128,1024]{2,1,0,3:T(2,128)(2,1)} %copy.28) | data formatting | bytes 4194304 | tf_op jit(solution)/shard_map/reshape | solution.py:120
  129.1 9.0 %fusion.23 = f32[256,16,64]{0,2,1:T(8,128)} fusion(bf16[1024,16,64]{0,2,1:T(8,128)(2,1)} %reshape.95, f32[16,256,1024]{2,1,0:T(8,128)} %get-tuple-element.94, f32[16,256]{1,0:T(8,128)S(1)} %get-tuple-element.93, f32[256,16]{0,1:T(8,128)S(1)} %get-tuple-element.92), kind=kOutput, calls=%fused_computation.40 | convolution fusion | flops 549715968 | bytes 19955712 | tf_op jit(solution)/shard_map/hrt,the->rhe/dot_general | solution.py:128
  138.1 5.4 %convolution_convert_fusion.3 = bf16[1024,1024]{1,0:T(8,128)(2,1)} fusion(bf16[1024,1024]{1,0:T(8,128)(2,1)S(1)} %bitcast.117, bf16[1024,1024]{1,0:T(8,128)(2,1)} %param.12), kind=kOutput, calls=%fused_computation.38 | convolution fusion | flops 2148532224 | bytes 6291456 | tf_op jit(solution)/shard_map/dot_general | solution.py:28
  145.9 4.0 reshape.109
  149.9 6.0 %copy.27 = bf16[2,4,128,16,64]{2,4,3,1,0:T(8,128)(2,1)} copy(bf16[2,4,128,16,64]{4,3,2,1,0:T(8,128)(2,1)} %reshape.109) | data formatting | bytes 4194304 | tf_op jit(solution)/shard_map/while | solution.py:111
  155.8 40.7 %psum.15 = f32[256,16]{0,1:T(8,128)S(1)} all-reduce(f32[256,16]{0,1:T(8,128)S(1)} %get-tuple-element.91), channel_id=1, replica_groups=mesh['phase'=4,'slab'=8] {'phase','slab'}, use_global_device_ids=true, to_apply=%region_9.10 | all-reduce | flops 4096 | bytes 32768 | tf_op jit(solution)/shard_map/psum | solution.py:131
  198.8 70.4 %all-reduce.2.cloned.1.call-done = f32[256,16,64]{0,2,1:T(8,128)} async-done(((f32[256,16,64]{0,2,1:T(8,128)}), f32[256,16,64]{0,2,1:T(8,128)}) %all-reduce.2.cloned.1.call-update) | async-done | bytes 1048592 | tf_op jit(solution)/shard_map/psum | solution.py:131
  272.3 10.6 %pad_maximum_fusion = bf16[6,4,128,2048]{3,2,1,0:T(8,128)(2,1)} fusion(bf16[6,1,128,2048]{3,2,1,0:T(8,128)(2,1)} %collective-permute-done.3, bf16[1,2,128,2048]{3,2,1,0:T(8,128)(2,1)} %collective-permute-done.1, bf16[4,2,128,2048]{3,2,1,0:T(8,128)(2,1)S(1)} %bitcast.125, bf16[1,2,128,2048]{3,2,1,0:T(8,128)(2,1)S(1)} %collective-permute-done, ...), kind=kLoop, calls=%fused_computation.33 | loop fusion | flops 25165824 | bytes 25165824 | tf_op jit(solution)/shard_map/concatenate | solution.py:16
  282.9 152.1 %while.10 = (s32[]{:T(128)}, bf16[2,512,1024]{2,1,0:T(8,128)(2,1)}, s32[2,4,5]{2,1,0:T(4,128)S(1)}, bf16[24,128,2048]{2,1,0:T(8,128)(2,1)}, bf16[2,4,128,16,64]{...) while((s32[]{:T(128)}, bf16[2,512,1024]{2,1,0:T(8,128)(2,1)}, ...), condition=%wide.region_4.5_spmd, body=%wide.region_0.4_spmd.sunk | while | flops 3020407808 | bytes 216308000 | solution.py:111
  283.0 10.0 %gather_fusion = bf16[20,128,2048]{2,1,0:T(8,128)(2,1)} fusion(bf16[24,128,2048]{2,1,0:T(8,128)(2,1)} %get-tuple-element.177, s32[1024]{0:T(1024)S(1)} %pad_clamp_fusion.2), kind=kCustom, calls=%fused_computation.clone.1 | custom fusion | bytes 20971600 | tf_op jit(solution)/shard_map/while/body/eval_jaxpr/gather | solution.py:97
  293.0 9.2 %fusion.76 = (bf16[4,640,1024]{2,1,0:T(8,128)(2,1)}, bf16[4,640,1024]{2,1,0:T(8,128)(2,1)}) fusion(bf16[4,640,2048]{2,1,0:T(8,128)(2,1)} %bitcast.118), kind=kLoop, calls=%fused_computation.62.clone.1 | loop fusion | bytes 20971520 | tf_op jit(solution)/shard_map/while/body/eval_jaxpr/slice | solution.py:100
  302.3 7.9 %copy.50 = bf16[4,640,1024]{1,2,0:T(8,128)(2,1)} copy(bf16[4,640,1024]{2,1,0:T(8,128)(2,1)} %get-tuple-element.152) | data formatting | bytes 10485760 | tf_op jit(solution)/shard_map/while
  310.1 5.9 %fusion.78 = (f32[4,16,128]{2,1,0:T(8,128)S(1)}, f32[4,16,128,640]{3,2,1,0:T(8,128)S(1)}) fusion(bf16[4,640,16,64]{1,3,2,0:T(8,128)(2,1)} %bitcast.119, bf16[2,4,128,16,64]{2,4,3,1,0:T(8,128)(2,1)} %get-tuple-element.178, s32[]{:T(128)} %get-tuple-element.165), kind=kOutput, calls=%fused_computation.63.clone.1 | convolution fusion | flops 681566208 | bytes 27296256 | tf_op jit(solution)/shard_map/while/body/eval_jaxpr/gqhe,gkhe->ghqk/dot_general | solution.py:33
  319.1 6.8 %fusion.79 = f32[4,16,128]{2,1,0:T(8,128)S(1)} fusion(f32[4,16,128,256]{3,2,1,0:T(8,128)S(1)} %get-tuple-element.151, f32[4,16,128,640]{3,2,1,0:T(8,128)S(1)} %get-tuple-element.153, f32[4,16,128]{2,1,0:T(8,128)S(1)} %reduce_max.38), kind=kLoop, calls=%fused_computation.4.clone.1 | loop fusion | flops 22011904 | bytes 29425664 | tf_op jit(solution)/shard_map/while/body/eval_jaxpr/reduce_sum | solution.py:45
  325.9 8.4 %divide_convert_fusion.3 = bf16[4,16,128,896]{3,2,1,0:T(8,128)(2,1)} fusion(f32[4,16,128,256]{3,2,1,0:T(8,128)S(1)} %get-tuple-element.151, f32[4,16,128,640]{3,2,1,0:T(8,128)S(1)} %get-tuple-element.153, f32[4,16,128]{2,1,0:T(8,128)S(1)} %fusion.79, f32[4,16,128]{2,1,0:T(8,128)S(1)} %reduce_max.38), kind=kLoop, calls=%fused_computation.3.clone.1 | loop fusion | flops 29360128 | bytes 44105728 | tf_op jit(solution)/shard_map/while/body/eval_jaxpr/convert_element_type | solution.py:45
  334.3 7.8 %copy.49 = bf16[4,640,1024]{1,2,0:T(8,128)(2,1)} copy(bf16[4,640,1024]{2,1,0:T(8,128)(2,1)} %get-tuple-element.150) | data formatting | bytes 10485760 | tf_op jit(solution)/shard_map/while
  342.2 9.8 %fusion.80 = f32[4,16,64,128]{3,2,1,0:T(8,128)S(1)} fusion(bf16[4,640,16,64]{1,3,2,0:T(8,128)(2,1)} %bitcast.121, bf16[4,16,128,896]{3,2,1,0:T(8,128)(2,1)} %divide_convert_fusion.3), kind=kOutput, calls=%fused_computation.5.clone.1 | convolution fusion | flops 671088640 | bytes 17825792 | tf_op jit(solution)/shard_map/while/body/eval_jaxpr/ghqk,gkhe->gqhe/dot_general | solution.py:47
  359.0 10.0 %gather_fusion = bf16[20,128,2048]{2,1,0:T(8,128)(2,1)} fusion(bf16[24,128,2048]{2,1,0:T(8,128)(2,1)} %get-tuple-element.177, s32[1024]{0:T(1024)S(1)} %pad_clamp_fusion.2), kind=kCustom, calls=%fused_computation.clone.1 | custom fusion | bytes 20971600 | tf_op jit(solution)/shard_map/while/body/eval_jaxpr/gather | solution.py:97
  369.1 9.2 %fusion.76 = (bf16[4,640,1024]{2,1,0:T(8,128)(2,1)}, bf16[4,640,1024]{2,1,0:T(8,128)(2,1)}) fusion(bf16[4,640,2048]{2,1,0:T(8,128)(2,1)} %bitcast.118), kind=kLoop, calls=%fused_computation.62.clone.1 | loop fusion | bytes 20971520 | tf_op jit(solution)/shard_map/while/body/eval_jaxpr/slice | solution.py:100
  378.3 7.9 %copy.50 = bf16[4,640,1024]{1,2,0:T(8,128)(2,1)} copy(bf16[4,640,1024]{2,1,0:T(8,128)(2,1)} %get-tuple-element.152) | data formatting | bytes 10485760 | tf_op jit(solution)/shard_map/while
  386.2 5.9 %fusion.78 = (f32[4,16,128]{2,1,0:T(8,128)S(1)}, f32[4,16,128,640]{3,2,1,0:T(8,128)S(1)}) fusion(bf16[4,640,16,64]{1,3,2,0:T(8,128)(2,1)} %bitcast.119, bf16[2,4,128,16,64]{2,4,3,1,0:T(8,128)(2,1)} %get-tuple-element.178, s32[]{:T(128)} %get-tuple-element.165), kind=kOutput, calls=%fused_computation.63.clone.1 | convolution fusion | flops 681566208 | bytes 27296256 | tf_op jit(solution)/shard_map/while/body/eval_jaxpr/gqhe,gkhe->ghqk/dot_general | solution.py:33
  395.1 6.8 %fusion.79 = f32[4,16,128]{2,1,0:T(8,128)S(1)} fusion(f32[4,16,128,256]{3,2,1,0:T(8,128)S(1)} %get-tuple-element.151, f32[4,16,128,640]{3,2,1,0:T(8,128)S(1)} %get-tuple-element.153, f32[4,16,128]{2,1,0:T(8,128)S(1)} %reduce_max.38), kind=kLoop, calls=%fused_computation.4.clone.1 | loop fusion | flops 22011904 | bytes 29425664 | tf_op jit(solution)/shard_map/while/body/eval_jaxpr/reduce_sum | solution.py:45
  402.0 8.4 %divide_convert_fusion.3 = bf16[4,16,128,896]{3,2,1,0:T(8,128)(2,1)} fusion(f32[4,16,128,256]{3,2,1,0:T(8,128)S(1)} %get-tuple-element.151, f32[4,16,128,640]{3,2,1,0:T(8,128)S(1)} %get-tuple-element.153, f32[4,16,128]{2,1,0:T(8,128)S(1)} %fusion.79, f32[4,16,128]{2,1,0:T(8,128)S(1)} %reduce_max.38), kind=kLoop, calls=%fused_computation.3.clone.1 | loop fusion | flops 29360128 | bytes 44105728 | tf_op jit(solution)/shard_map/while/body/eval_jaxpr/convert_element_type | solution.py:45
  410.4 7.8 %copy.49 = bf16[4,640,1024]{1,2,0:T(8,128)(2,1)} copy(bf16[4,640,1024]{2,1,0:T(8,128)(2,1)} %get-tuple-element.150) | data formatting | bytes 10485760 | tf_op jit(solution)/shard_map/while
  418.2 9.8 %fusion.80 = f32[4,16,64,128]{3,2,1,0:T(8,128)S(1)} fusion(bf16[4,640,16,64]{1,3,2,0:T(8,128)(2,1)} %bitcast.121, bf16[4,16,128,896]{3,2,1,0:T(8,128)(2,1)} %divide_convert_fusion.3), kind=kOutput, calls=%fused_computation.5.clone.1 | convolution fusion | flops 671088640 | bytes 17825792 | tf_op jit(solution)/shard_map/while/body/eval_jaxpr/ghqk,gkhe->gqhe/dot_general | solution.py:47
  (75 shorter events, 55.6 us)
Async XLA Ops:
  7.2 2.9 copy-start
  7.2 262.0 %all-reduce.2.cloned.1.call-start = ((), (), s32[]{:S(2)}) async-start(), calls=%async_computation | async-start | bytes 2097152 | tf_op jit(solution)/shard_map/psum | solution.py:131
  7.2 2.4 copy-start.9
  10.0 4.8 %copy-start.10 = (bf16[1024,2048]{1,0:T(8,128)(2,1)}, bf16[1024,2048]{1,0:T(8,128)(2,1)S(1)}, u32[]{:S(2)}) copy-start(bf16[1024,2048]{1,0:T(8,128)(2,1)S(1)} %constant_dynamic-update-slice_fusion) | copy-start | bytes 12582916
  14.8 8.2 %copy-start.2 = (bf16[2048,1024]{0,1:T(8,128)(2,1)}, bf16[2048,1024]{0,1:T(8,128)(2,1)S(1)}, u32[]{:S(2)}) copy-start(bf16[2048,1024]{0,1:T(8,128)(2,1)S(1)} %convolution_convert_fusion.1) | copy-start | bytes 12582916
  16.6 92.1 %collective-permute-start = (bf16[1,2,128,2048]{3,2,1,0:T(8,128)(2,1)}, bf16[1,2,128,2048]{3,2,1,0:T(8,128)(2,1)S(1)}, u32[]{:S(2)}, u32[]{:S(2)}) collective-permute-start(bf16[1,2,128,2048]{3,2,1,0:T(8,128)(2,1)} %bitcast.14), channel_id=1, source_target_pairs={{0,8},{8,16},{16,24},{24,0},{1,9},{9,17},{17,25},{25,1},{2,10},{10... | collective-permute-start | bytes 3145736 | tf_op jit(solution)/shard_map/ppermute | solution.py:18
  19.6 89.1 %collective-permute-start.1 = (bf16[1,2,128,2048]{3,2,1,0:T(8,128)(2,1)}, bf16[1,2,128,2048]{3,2,1,0:T(8,128)(2,1)}, u32[]{:S(2)}, u32[]{:S(2)}) collective-permute-start(bf16[1,2,128,2048]{3,2,1,0:T(8,128)(2,1)} %bitcast.16), channel_id=1, source_target_pairs={{8,0},{16,8},{24,16},{0,24},{9,1},{17,9},{25,17},{1,25},{10,2},{18... | collective-permute-start | bytes 3145736 | tf_op jit(solution)/shard_map/ppermute | solution.py:20
  100.8 7.9 %copy-start.3 = (bf16[2048,1024]{0,1:T(8,128)(2,1)S(1)}, bf16[2048,1024]{0,1:T(8,128)(2,1)}, u32[]{:S(2)}) copy-start(bf16[2048,1024]{0,1:T(8,128)(2,1)} %copy-done.2) | copy-start | bytes 12582916
  114.1 158.2 %collective-permute-start.2 = (bf16[6,1,128,2048]{3,2,1,0:T(8,128)(2,1)}, bf16[6,1,128,2048]{3,2,1,0:T(8,128)(2,1)}, u32[]{:S(2)}, u32[]{:S(2)}) collective-permute-start(bf16[6,1,128,2048]{3,2,1,0:T(8,128)(2,1)} %get-tuple-element.83), channel_id=1, source_target_pairs={{0,1},{1,2},{2,3},{3,4},{4,5},{5,6},{6,7},{8,9},{9,10},{10,11},{11... | collective-permute-start | bytes 9437192 | tf_op jit(solution)/shard_map/ppermute | solution.py:18
  117.0 155.3 %collective-permute-start.3 = (bf16[6,1,128,2048]{3,2,1,0:T(8,128)(2,1)}, bf16[6,1,128,2048]{3,2,1,0:T(8,128)(2,1)}, u32[]{:S(2)}, u32[]{:S(2)}) collective-permute-start(bf16[6,1,128,2048]{3,2,1,0:T(8,128)(2,1)} %get-tuple-element.84), channel_id=1, source_target_pairs={{1,0},{2,1},{3,2},{4,3},{5,4},{6,5},{7,6},{9,8},{10,9},{11,10},{12... | collective-permute-start | bytes 9437192 | tf_op jit(solution)/shard_map/ppermute | solution.py:20
  138.1 5.4 %copy-start.11 = (bf16[1024,2048]{1,0:T(8,128)(2,1)S(1)}, bf16[1024,2048]{1,0:T(8,128)(2,1)}, u32[]{:S(2)}) copy-start(bf16[1024,2048]{1,0:T(8,128)(2,1)} %copy-done.10) | copy-start | bytes 12582916
  138.1 5.4 %copy-start.13 = (bf16[256,1024]{1,0:T(8,128)(2,1)S(1)}, bf16[256,1024]{1,0:T(8,128)(2,1)}, u32[]{:S(2)}) copy-start(bf16[256,1024]{1,0:T(8,128)(2,1)} %param.11) | copy-start | bytes 1572868
  143.5 2.4 copy-start.6
  145.9 50.6 %copy-start.12 = (s32[4,2,5]{2,1,0:T(2,128)S(1)}, s32[4,2,5]{2,1,0:T(2,128)}, u32[]{:S(2)}) copy-start(s32[4,2,5]{2,1,0:T(2,128)} %param.10) | copy-start | bytes 484
  149.9 120.8 %copy-start.7 = (bf16[1024,1024]{1,0:T(8,128)(2,1)S(1)}, bf16[1024,1024]{1,0:T(8,128)(2,1)}, u32[]{:S(2)}) copy-start(bf16[1024,1024]{1,0:T(8,128)(2,1)} %param.15) | copy-start | bytes 6291460
  269.2 3.0 copy-start.4
  342.2 9.8 %copy-start.5 = (bf16[256,16,64]{0,2,1:T(8,128)(2,1)S(1)}, bf16[256,16,64]{0,2,1:T(8,128)(2,1)}, u32[]{:S(2)}) copy-start(bf16[256,16,64]{0,2,1:T(8,128)(2,1)} %get-tuple-element.180) | copy-start | bytes 1572868 | tf_op jit(solution)/shard_map/while
  352.0 4.7 %copy-start.8 = (bf16[1024,1024]{1,0:T(8,128)(2,1)S(1)}, bf16[1024,1024]{1,0:T(8,128)(2,1)}, u32[]{:S(2)}) copy-start(bf16[1024,1024]{1,0:T(8,128)(2,1)} %get-tuple-element.196) | copy-start | bytes 6291460 | tf_op jit(solution)/shard_map/while
  418.2 9.8 %copy-start.5 = (bf16[256,16,64]{0,2,1:T(8,128)(2,1)S(1)}, bf16[256,16,64]{0,2,1:T(8,128)(2,1)}, u32[]{:S(2)}) copy-start(bf16[256,16,64]{0,2,1:T(8,128)(2,1)} %get-tuple-element.180) | copy-start | bytes 1572868 | tf_op jit(solution)/shard_map/while
  428.0 4.7 %copy-start.8 = (bf16[1024,1024]{1,0:T(8,128)(2,1)S(1)}, bf16[1024,1024]{1,0:T(8,128)(2,1)}, u32[]{:S(2)}) copy-start(bf16[1024,1024]{1,0:T(8,128)(2,1)} %get-tuple-element.196) | copy-start | bytes 6291460 | tf_op jit(solution)/shard_map/while
  434.9 1.6 copy-start.1
Sparse Core Ops, SparseCore 0:
  138.2 130.9 all-reduce.1
where the time goes:
time: 445 us; the launch traced here: 443 us
  local copies, waits for them, and re-layouts  119 us (27%)
  blocking collectives  92.7 us (21%)
  matrix products  85.7 us (19%)
  waiting for transfers between devices  70.5 us (16%)
  other arithmetic  52.5 us (12%)
  between operations  14.2 us (3%)
  starting transfers between devices  8.29 us (2%)
    psum x1, waiting for transfers between devices, shards(): lax.psum((weight_sum * factor, weighted * factor.T[:, :, None]), ('phase'...  70.4 us
    pmax x1, blocking collectives, shards(): global_peak = lax.pmax(row_peak, ('phase', 'slab'))  52 us
    psum x1, blocking collectives, shards(): lax.psum((weight_sum * factor, weighted * factor.T[:, :, None]), ('phase'...  40.7 us
    while x12, local copies, waits for them, and re-layouts  31.4 us
    dot_general x7, matrix products, project(): jnp.dot(token_rows, weight, preferred_element_type=jnp.float32)  21.9 us
    gather x2, local copies, waits for them, and re-layouts, one_group(): block_table[group_index.reshape(-1)]  20.1 us
    dot_general x2, matrix products, window_attend(): jnp.einsum('ghqk,gkhe->gqhe', probabilities[..., :key_count], value_rows,...  19.6 us
    slice x2, local copies, waits for them, and re-layouts, one_group(): chosen[..., :model_width]  18.5 us
  transfers between devices with their start and end apart: 5, of which 1 were waited for; matrix products, arithmetic and copies ran while one was open for 18% of the time, Pallas kernels for 0%

commit v1 on v0

v1 whole, which is shorter than its diff:
```python
import functools

import jax
import jax.numpy as jnp
from jax import lax
from jax.experimental import pallas as pl
from jax.experimental.pallas import tpu as pltpu
from jax.sharding import PartitionSpec as P

HEADS = 16
LIST = 5
QUAD = 4
LOG2E = 1.4426950408889634
F32, BF16 = jnp.float32, jnp.bfloat16
VMEM_LIMIT = 56 * 1024 * 1024


def params():
    return pltpu.CompilerParams(vmem_limit_bytes=VMEM_LIMIT)


def cost(macs, size, exps=0):
    return pl.CostEstimate(flops=2 * macs, bytes_accessed=size, transcendentals=exps)


def matmul(a, b):
    return jnp.dot(a, b, preferred_element_type=F32)


def matmul_t(a, b):
    return lax.dot_general(a, b, (((1,), (1,)), ((), ())), preferred_element_type=F32)


def own_kernel(steps, scale, x_ref, reg_ref, wq_ref, wk_ref, wv_ref, q_ref, kv_ref):
    width = wq_ref.shape[1]

    def work(rows):
        q_ref[...] = (matmul(rows, wq_ref[...]) * scale).astype(BF16)
        blk = kv_ref.shape[1]
        for half in range(rows.shape[0] // blk):
            part = rows[half * blk : (half + 1) * blk]
            kv_ref[half, :, :width] = matmul(part, wk_ref[...]).astype(BF16)
            kv_ref[half, :, width:] = matmul(part, wv_ref[...]).astype(BF16)

    @pl.when(pl.program_id(0) == 0)
    def _():
        work(reg_ref[...])

    @pl.when(pl.program_id(0) > 0)
    def _():
        work(x_ref[...])


def own_project(rows, registers, w_query, w_key, w_value, slots, blk, scale):
    count, width = rows.shape
    tile = registers.shape[0]
    steps = count // tile
    whole = pl.BlockSpec((width, width), lambda i: (0, 0))
    per = tile // blk
    return pl.pallas_call(
        functools.partial(own_kernel, steps, scale),
        grid=(steps + 1,),
        in_specs=[
            pl.BlockSpec((tile, width), lambda i: (jnp.maximum(i - 1, 0), 0)),
            pl.BlockSpec((tile, width), lambda i: (0, 0)),
            whole,
            whole,
            whole,
        ],
        out_specs=[
            pl.BlockSpec((tile, width), lambda i: (i, 0)),
            pl.BlockSpec((per, blk, 2 * width), lambda i: (i, 0, 0)),
        ],
        out_shape=[
            jax.ShapeDtypeStruct((count + tile, width), BF16),
            jax.ShapeDtypeStruct((slots, blk, 2 * width), BF16),
        ],
        compiler_params=params(),
        cost_estimate=cost((count + tile) * width * width * 3, 18 << 20),
        name="own_project",
    )(rows, registers, w_query, w_key, w_value)


def halo_kernel(per_piece, pieces, *refs):
    xs, (wk_ref, wv_ref, _, kv_ref) = refs[:pieces], refs[pieces:]
    width = wk_ref.shape[1]
    for piece in range(pieces):

        @pl.when(pl.program_id(0) // per_piece == piece)
        def _():
            rows, blk, _ = kv_ref.shape
            x = xs[piece][...].reshape(rows * blk, width)
            kv_ref[:, :, :width] = matmul(x, wk_ref[...]).astype(BF16).reshape(rows, blk, width)
            kv_ref[:, :, width:] = matmul(x, wv_ref[...]).astype(BF16).reshape(rows, blk, width)


def halo_project(table, pieces, first_slot, w_key, w_value):
    slots, blk, _ = table.shape
    width = w_key.shape[0]
    each = pieces[0].shape[0]
    group = 2 if each % 2 == 0 and first_slot % 2 == 0 else 1
    per_piece = each // group
    whole = pl.BlockSpec((width, width), lambda i: (0, 0))

    def piece_map(piece):
        return lambda i: (jnp.clip(i - piece * per_piece, 0, per_piece - 1), 0, 0)

    first = first_slot // group
    return pl.pallas_call(
        functools.partial(halo_kernel, per_piece, len(pieces)),
        grid=(per_piece * len(pieces),),
        in_specs=[pl.BlockSpec((group, blk, width), piece_map(n)) for n in range(len(pieces))]
        + [whole, whole, pl.BlockSpec(memory_space=pl.ANY)],
        out_specs=pl.BlockSpec((group, blk, 2 * width), lambda i: (first + i, 0, 0)),
        out_shape=jax.ShapeDtypeStruct(table.shape, BF16),
        input_output_aliases={len(pieces) + 2: 0},
        compiler_params=params(),
        cost_estimate=cost(each * len(pieces) * blk * width * width * 2, 10 << 20),
        name="halo_project",
    )(*pieces, w_key, w_value, table)


def head_masks(rows, lanes, head_width):
    lane = lax.broadcasted_iota(jnp.int32, (rows, lanes), 1)
    return [lane // head_width == h for h in range(lanes // head_width)]


def attend(q, k, v, masks):
    rows = q.shape[0]
    stack = jnp.concatenate([jnp.where(m, q, jnp.zeros_like(q)) for m in masks], axis=0)
    s = matmul_t(stack, k)
    peak = jnp.max(s, axis=-1, keepdims=True)
    p = jnp.exp2(s - peak)
    total = jnp.sum(p, axis=-1, keepdims=True)
    o = matmul(p.astype(BF16), v) * (1.0 / total)
    out = o[:rows]
    for h in range(1, len(masks)):
        out = jnp.where(masks[h], o[h * rows : (h + 1) * rows], out)
    return out, peak, total


def window_kernel(head_width, idx_ref, q_ref, *refs):
    k_refs, (reg_ref, wo_ref) = refs[:LIST], refs[LIST : LIST + 2]
    o_ref, ctx_ref = refs[-2:]
    rows, width = q_ref.shape
    lanes = QUAD * head_width
    masks = head_masks(rows, lanes, head_width)
    for g in range(width // lanes):
        at = slice(g * lanes, (g + 1) * lanes)
        at_v = slice(width + g * lanes, width + (g + 1) * lanes)
        k = jnp.concatenate(
            [r[0, :, at] for r in k_refs] + [reg_ref[n, :, at] for n in range(reg_ref.shape[0])], axis=0
        )
        v = jnp.concatenate(
            [r[0, :, at_v] for r in k_refs] + [reg_ref[n, :, at_v] for n in range(reg_ref.shape[0])], axis=0
        )
        out, _, _ = attend(q_ref[:, at], k, v, masks)
        ctx_ref[:, at] = out.astype(BF16)
    o_ref[0] = matmul(ctx_ref[...], wo_ref[...]).astype(BF16)


def window_attend(queries, table, slots, order, w_out, blk, reg_slots, head_width, previous):
    total, width = queries.shape[0] // blk - reg_slots, w_out.shape[0]
    n = len(order)
    start, stride = order[0], (order[1] - order[0] if n > 1 else 1)
    run = 1
    while run < n and order[run] == order[run - 1] + 1:
        run += 1
    jump = order[run] - order[0] if run < n else 0

    def block(i):
        return start + (i // run) * jump + i % run

    def list_map(entry):
        return lambda i, idx: (idx[block(i) * LIST + entry], 0, 0)

    operands = [slots, queries] + [table] * LIST + [table, w_out]
    in_specs = (
        [pl.BlockSpec((blk, width), lambda i, idx: (reg_slots + block(i), 0))]
        + [pl.BlockSpec((1, blk, 2 * width), list_map(e)) for e in range(LIST)]
        + [
            pl.BlockSpec((reg_slots, blk, 2 * width), lambda i, idx: (0, 0, 0)),
            pl.BlockSpec((width, width), lambda i, idx: (0, 0)),
        ]
    )
    aliases = {}
    if previous is not None:
        aliases = {len(operands): 0}
        operands.append(previous)
        in_specs.append(pl.BlockSpec(memory_space=pl.ANY))
    keys = (LIST + reg_slots) * blk
    return pl.pallas_call(
        functools.partial(window_kernel, head_width),
        grid_spec=pltpu.PrefetchScalarGridSpec(
            num_scalar_prefetch=1,
            grid=(n,),
            in_specs=in_specs,
            out_specs=pl.BlockSpec((1, blk, width), lambda i, idx: (block(i), 0, 0)),
            scratch_shapes=[pltpu.VMEM((blk, width), BF16)],
        ),
        out_shape=jax.ShapeDtypeStruct((total, blk, width), BF16),
        input_output_aliases=aliases,
        compiler_params=params(),
        cost_estimate=cost(n * blk * width * (8 * keys + width), n * 3 << 20, n * blk * HEADS * keys),
        name="window_attend",
    )(*operands)


def pack_levels(level):
    hi = level.astype(BF16)
    rest = level - hi.astype(F32)
    mid = rest.astype(BF16)
    low = (rest - mid.astype(F32)).astype(BF16)
    pad = jnp.zeros((level.shape[0], 128 - 3 * level.shape[1]), BF16)
    return jnp.concatenate([hi, mid, low, pad], axis=1)


def unpack_levels(cols):
    wide = cols.astype(F32)
    return wide[:, :HEADS] + wide[:, HEADS : 2 * HEADS] + wide[:, 2 * HEADS : 3 * HEADS]


def register_kernel(head_width, q_ref, kv_ref, o_ref):
    slots, blk, width2 = kv_ref.shape
    rows, width = q_ref.shape
    lanes = QUAD * head_width
    masks = head_masks(rows, lanes, head_width)
    levels = []
    for g in range(width // lanes):
        at = slice(g * lanes, (g + 1) * lanes)
        at_v = slice(width + g * lanes, width + (g + 1) * lanes)
        k = kv_ref[:, :, at].reshape(slots * blk, lanes)
        v = kv_ref[:, :, at_v].reshape(slots * blk, lanes)
        out, peak, total = attend(q_ref[:, at], k, v, masks)
        o_ref[:, at] = out.astype(BF16)
        level = peak + jnp.log2(total)
        levels += [level[h * rows : (h + 1) * rows] for h in range(len(masks))]
    o_ref[:, width:] = pack_levels(jnp.concatenate(levels, axis=1))


def register_attend(queries, table, rows, own_slots, head_width):
    _, blk, width2 = table.shape
    width = width2 // 2
    reg_slots = rows // blk
    assert own_slots % reg_slots == 0
    keys = own_slots * blk

    def body(*refs):
        q_ref, kv_refs, o_ref, scratch = refs[0], refs[1:-2], refs[-2], refs[-1]
        for n, r in enumerate(kv_refs):
            scratch[n * reg_slots : (n + 1) * reg_slots] = r[...]
        register_kernel(head_width, q_ref, scratch, o_ref)

    parts = own_slots // reg_slots
    return pl.pallas_call(
        body,
        grid=(1,),
        in_specs=[pl.BlockSpec((rows, width), lambda i: (0, 0))]
        + [
            pl.BlockSpec((reg_slots, blk, width2), functools.partial(lambda n, i: (n + 1, 0, 0), n))
            for n in range(parts)
        ],
        out_specs=pl.BlockSpec((rows, width + 128), lambda i: (0, 0)),
        out_shape=jax.ShapeDtypeStruct((rows, width + 128), BF16),
        scratch_shapes=[pltpu.VMEM((own_slots, blk, width2), BF16)],
        compiler_params=params(),
        cost_estimate=cost(rows * keys * width * 8, 6 << 20, rows * keys * HEADS),
        name="register_attend",
    )(queries, *[table] * parts)


def merged(a_ref, b_ref, width):
    la, lb = unpack_levels(a_ref[:, width:]), unpack_levels(b_ref[:, width:])
    top = jnp.maximum(la, lb)
    ea, eb = jnp.exp2(la - top), jnp.exp2(lb - top)
    total = ea + eb
    fa = ea / total
    fb = eb / total
    rows = a_ref.shape[0]
    head_width = width // HEADS
    lower = lax.broadcasted_iota(jnp.int32, (rows, 2 * head_width), 1) < head_width
    cols = []
    for pair in range(HEADS // 2):
        at = slice(pair * 2 * head_width, (pair + 1) * 2 * head_width)

        def spread(f):
            return jnp.where(lower, f[:, 2 * pair : 2 * pair + 1], f[:, 2 * pair + 1 : 2 * pair + 2])

        mix = a_ref[:, at].astype(F32) * spread(fa) + b_ref[:, at].astype(F32) * spread(fb)
        cols.append(mix.astype(BF16))
    return jnp.concatenate(cols, axis=1), top + jnp.log2(total)


def split_kernel(chunk, bit_ref, x_ref, keep_ref, send_ref):
    bit = bit_ref[0]
    for j in range(keep_ref.shape[0] // chunk):
        at = slice(j * chunk, (j + 1) * chunk)
        keep_ref[at] = x_ref[pl.ds(pl.multiple_of((2 * j + bit) * chunk, chunk), chunk)]
        send_ref[at] = x_ref[pl.ds(pl.multiple_of((2 * j + 1 - bit) * chunk, chunk), chunk)]


def small_call(body, out_shape, scratch, name, *operands):
    vmem = pl.BlockSpec(memory_space=pltpu.VMEM)
    return pl.pallas_call(
        body,
        in_specs=[pl.BlockSpec(memory_space=pltpu.SMEM)] + [vmem] * (len(operands) - 1),
        out_specs=jax.tree.map(lambda _: vmem, out_shape),
        out_shape=out_shape,
        scratch_shapes=scratch,
        compiler_params=params(),
        cost_estimate=cost(1 << 20, 1 << 20),
        name=name,
    )(*operands)


def register_merge(partial, w_out):
    rows, wide = partial.shape
    width = w_out.shape[0]
    slabs, phases = lax.axis_size("slab"), lax.axis_size("phase")
    slab = lax.axis_index("slab")
    chunk = rows // slabs

    def half(n):
        return [jax.ShapeDtypeStruct((n // 2, wide), BF16)] * 2

    rounds = slabs.bit_length() - 1
    bits = [((slab >> r) & 1).astype(jnp.int32).reshape(1) for r in range(rounds)]
    keep, send = small_call(
        functools.partial(split_kernel, chunk), half(rows), [], "register_split", bits[0], partial
    )
    for r in range(rounds):
        got = lax.ppermute(send, "slab", [(i, i ^ (1 << r)) for i in range(slabs)])
        held = keep.shape[0]
        if r + 1 < rounds:

            def body(bit_ref, a_ref, b_ref, keep_ref, send_ref, full_ref):
                mix, level = merged(a_ref, b_ref, width)
                full_ref[:, :width] = mix
                full_ref[:, width:] = pack_levels(level)
                split_kernel(chunk, bit_ref, full_ref, keep_ref, send_ref)

            keep, send = small_call(
                body, half(held), [pltpu.VMEM((held, wide), BF16)], "register_merge", bits[r + 1], keep, got
            )
        else:

            def body_all(bit_ref, a_ref, b_ref, full_ref):
                mix, level = merged(a_ref, b_ref, width)
                full_ref[:, :width] = mix
                full_ref[:, width:] = pack_levels(level)

            keep = small_call(
                body_all, jax.ShapeDtypeStruct((held, wide), BF16), [], "register_merge", bits[0], keep, got
            )
    turns = phases.bit_length() - 1
    for r in range(turns):
        got = lax.ppermute(keep, "phase", [(i, i ^ (1 << r)) for i in range(phases)])
        held = keep.shape[0]
        if r + 1 < turns:
            keep = small_call(
                body_all, jax.ShapeDtypeStruct((held, wide), BF16), [], "register_merge", bits[0], keep, got
            )
        else:

            def body_out(bit_ref, a_ref, b_ref, w_ref, out_ref):
                mix, _ = merged(a_ref, b_ref, width)
                out_ref[...] = matmul(mix, w_ref[...]).astype(BF16)

            keep = small_call(
                body_out,
                jax.ShapeDtypeStruct((held, width), BF16),
                [],
                "register_out",
                bits[0],
                keep,
                got,
                w_out,
            )
    return lax.all_gather(keep, "slab", axis=0, tiled=True)


def shards(normed, block_list, registers, w_query, w_key, w_value, w_out):
    own_phases, slab_blocks, blk, width = normed.shape
    head_width = width // HEADS
    scale = head_width ** (-0.5) * LOG2E
    phases, slabs = lax.axis_size("phase"), lax.axis_size("slab")
    rows = registers.shape[0]
    reg_slots = rows // blk
    own = own_phases * slab_blocks

    def around(x, axis, step, closed):
        n = lax.axis_size(axis)
        return lax.ppermute(
            x, axis, [(i, (i + step) % n) for i in range(n) if closed or 0 <= i + step < n]
        )

    before = around(normed[-1], "phase", 1, True)
    after = around(normed[0], "phase", -1, True)
    left = around(normed[:, -1], "slab", 1, False)
    right = around(normed[:, 0], "slab", -1, False)
    corner_left = around(jnp.stack([before[-1], after[-1]]), "slab", 1, False)
    corner_right = around(jnp.stack([before[0], after[0]]), "slab", -1, False)

    at_left = reg_slots + own
    at_right = at_left + own_phases
    at_before = at_right + own_phases
    at_after = at_before + slab_blocks
    at_corner = at_after + slab_blocks
    slots = at_corner + 4

    total_phases, depth_blocks = own_phases * phases, slab_blocks * slabs
    p = (block_list // depth_blocks - lax.axis_index("phase") * own_phases + 1) % total_phases - 1
    z = block_list % depth_blocks - lax.axis_index("slab") * slab_blocks
    is_left, is_right = z < 0, z >= slab_blocks
    is_before, is_after = p < 0, p >= own_phases
    inner = jnp.where(
        is_left, at_left + p, jnp.where(is_right, at_right + p, reg_slots + p * slab_blocks + z)
    )
    outer = jnp.where(
        is_left | is_right,
        at_corner + jnp.where(is_right, 2, 0) + jnp.where(is_after, 1, 0),
        jnp.where(is_after, at_after, at_before) + z,
    )
    slot_list = jnp.where(is_before | is_after, outer, inner).astype(jnp.int32).reshape(-1)

    queries, table = own_project(
        normed.reshape(-1, width), registers, w_query, w_key, w_value, slots, blk, scale
    )
    partial = register_attend(queries, table, rows, own, head_width)
    register_out = register_merge(partial, w_out)

    table = halo_project(table, [left, right], at_left, w_key, w_value)
    middle = list(range(slab_blocks, own - slab_blocks))
    edge = list(range(slab_blocks)) + list(range(own - slab_blocks, own))
    mixed = window_attend(
        queries, table, slot_list, middle, w_out, blk, reg_slots, head_width, None
    )
    table = halo_project(table, [before, after], at_before, w_key, w_value)
    table = halo_project(table, [corner_left, corner_right], at_corner, w_key, w_value)
    mixed = window_attend(
        queries, table, slot_list, edge, w_out, blk, reg_slots, head_width, mixed
    )
    return mixed.reshape(own_phases, slab_blocks, blk, width), register_out


def solution(mesh):
    placed = (P("phase", "slab", None, None), P("phase", "slab", None), P(), P(), P(), P(), P())
    return jax.shard_map(
        shards,
        mesh=mesh,
        in_specs=placed,
        out_specs=(P("phase", "slab", None, None), P()),
        check_vma=False,
    )
```

time: 445 us -> 158 us (0.36)
  local copies, waits for them, and re-layouts: 119 us -> 11 us
  Pallas kernels: 0 us -> 95.4 us
  matrix products: 85.7 us -> 0 us
  blocking collectives: 92.7 us -> 15.1 us
  waiting for transfers between devices: 70.5 us -> 16.6 us
  other arithmetic: 52.5 us -> 0.15 us
  between operations: 14.2 us -> 0.78 us
  starting transfers between devices: 8.29 us -> 19 us
    pallas_call x0 -> x13, Pallas kernels: none -> 95.4 us  [the longest x2 37.7 us: window_attend(): pl.pallas_call(functools.partial(window_kernel, head_width), grid_spec=pl...]
    dot_general x17 -> x0, matrix products: 85.7 us -> none  [the longest x7 21.9 us: project(): jnp.dot(token_rows, weight, preferred_element_type=jnp.float32)]
    psum x1 -> x0, waiting for transfers between devices: 70.4 us -> none  [shards(): lax.psum((weight_sum * factor, weighted * factor.T[:, :, None]), ('phase'...]
    pmax x1 -> x0, blocking collectives: 52 us -> none  [shards(): global_peak = lax.pmax(row_peak, ('phase', 'slab'))]
    psum x1 -> x0, blocking collectives: 40.7 us -> none  [shards(): lax.psum((weight_sum * factor, weighted * factor.T[:, :, None]), ('phase'...]
    slice x8 -> x2, local copies, waits for them, and re-layouts: 40.7 us -> 0.07 us  [shards(): corner_right = around(jnp.stack([before[0], after[0]]), 'slab', -1, False)]
    while x13 -> x0, local copies, waits for them, and re-layouts: 37.4 us -> none
    reduce_sum x3 -> x0, other arithmetic: 21.5 us -> none  [the longest x2 13.7 us: window_attend(): jnp.sum(shifted, axis=-1, keepdims=True)]
  transfers between devices with their start and end apart: 5 -> 11, of which waited for: 1 -> 3; matrix products, arithmetic and copies ran while one was open for 18% -> 2% of each run, Pallas kernels for 0% -> 29%
where the time goes in v1:
time: 158 us
  Pallas kernels  95.4 us (60%)
  starting transfers between devices  19 us (12%)
  waiting for transfers between devices  16.6 us (11%)
  blocking collectives  15.1 us (10%)
  local copies, waits for them, and re-layouts  11 us (7%)
    pallas_call x2, Pallas kernels, window_attend(): pl.pallas_call(functools.partial(window_kernel, head_width), grid_spec=pl...  37.7 us
    pallas_call x3, Pallas kernels, halo_project(): pl.pallas_call(functools.partial(halo_kernel, per_piece, len(pieces)), gr...  21 us
    all_gather x1, blocking collectives, register_merge(): return lax.all_gather(keep, 'slab', axis=0, tiled=True)  15.1 us
    pallas_call x1, Pallas kernels, own_project(): pl.pallas_call(functools.partial(own_kernel, steps, scale), grid=(steps +...  13.6 us
    pallas_call x6, Pallas kernels, small_call(): pl.pallas_call(body, in_specs=[pl.BlockSpec(memory_space=pltpu.SMEM)] + [...  13.4 us
    ppermute x3, waiting for transfers between devices, register_merge(): got = lax.ppermute(send, 'slab', [(i, i ^ 1 << r) for i in range(slabs)])  12.4 us
    pallas_call x1, Pallas kernels, register_attend(): pl.pallas_call(body, grid=(1,), in_specs=[pl.BlockSpec((rows, width), lam...  9.66 us
    ppermute x6, starting transfers between devices, around(): lax.ppermute(x, axis, [(i, (i + step) % n) for i in range(n) if closed or...  9.16 us
  transfers between devices with their start and end apart: 11, of which 3 were waited for; matrix products, arithmetic and copies ran while one was open for 2% of the time, Pallas kernels for 29%

profile of v1, /device:TPU:0, one launch (start us, length us, event | category | flops | bytes accessed | tf_op | source)
XLA Modules:
  0.0 158.0 jit_solution(18427569885137387008)
XLA Ops:
  0.6 13.6 %own_project.1 = (bf16[1280,1024]{1,0:T(8,128)(2,1)}, bf16[26,128,2048]{2,1,0:T(8,128)(2,1)}) custom-call(bf16[1024,1024]{1,0:T(8,128)(2,1)} %bitcast.18, bf16[256,1024]{1,0:T(8,128)(2,1)} %reg_ref.1, bf16[1024,1024]{1,0:T(8,128)(2,1)} %wq_ref.1, bf16[1024,1024]{1,0:T(8,128)(2,1)} %refs_2_.5, bf16[1024,1024]{1,0:T(8,128)(2,1)} %refs_3_.5), custom_call_target="tpu_custom_call" | custom-call | flops 8053063680 | bytes 18874368 | tf_op jit(solution)/shard_map/own_project/pallas_call | solution.py:60
  14.2 9.7 %register_attend.1.x_ref = bf16[256,1152]{1,0:T(8,128)(2,1)} custom-call(bf16[1280,1024]{1,0:T(8,128)(2,1)} %get-tuple-element.10.q_ref.refs_0_, bf16[26,128,2048]{2,1,0:T(8,128)(2,1)} %get-tuple-element.11.refs_4_.refs_1_.refs_2_.refs_3_, bf16[26,128,2048]{2,1,0:T(8,128)(2,1)} %get-tuple-element.11.refs_4_.refs_1_.refs_2_.refs_3_, ...), custom_call_target="tpu_custom_call" | custom-call | flops 4294967296 | bytes 6291456 | tf_op jit(solution)/shard_map/register_attend/pallas_call | solution.py:255
  23.9 1.9 %register_split.1 = (bf16[128,1152]{1,0:T(8,128)(2,1)}, bf16[128,1152]{1,0:T(8,128)(2,1)}) custom-call(s32[1]{0:T(128)} %bitcast.6.bit_ref, bf16[256,1152]{1,0:T(8,128)(2,1)} %register_attend.1.x_ref), custom_call_target="tpu_custom_call" | custom-call | flops 2097152 | bytes 1048576 | tf_op jit(solution)/shard_map/register_split/pallas_call | solution.py:304
  26.3 1.1 slice_bitcast_fusion.3
  27.3 2.5 %collective-permute-start = (bf16[2,128,1024]{2,1,0:T(8,128)(2,1)}, bf16[2,128,1024]{2,1,0:T(8,128)(2,1)S(1)}, u32[]{:S(2)}, u32[]{:S(2)}) collective-permute-start(bf16[2,128,1024]{2,1,0:T(8,128)(2,1)} %get-tuple-element.20), channel_id=1, source_target_pairs={{0,8},{8,16},{16,24},{24,0},{1,9},{9,17},{17,25},{25,1},{2,10},{10... | collective-permute-start | bytes 1572872 | tf_op jit(solution)/shard_map/ppermute | solution.py:393
  29.8 1.0 collective-permute-start.1
  31.5 2.6 %register_merge.4 = (bf16[64,1152]{1,0:T(8,128)(2,1)}, bf16[64,1152]{1,0:T(8,128)(2,1)}) custom-call(s32[1]{0:T(128)} %bitcast.8.bit_ref, bf16[128,1152]{1,0:T(8,128)(2,1)} %get-tuple-element.12.a_ref, bf16[128,1152]{1,0:T(8,128)(2,1)} %copy-done.7), custom_call_target="tpu_custom_call" | custom-call | flops 2097152 | bytes 1048576 | tf_op jit(solution)/shard_map/register_merge/pallas_call | solution.py:304
  34.1 2.0 %collective-permute-start.7 = (bf16[64,1152]{1,0:T(8,128)(2,1)}, bf16[64,1152]{1,0:T(8,128)(2,1)S(1)}, u32[]{:S(2)}, u32[]{:S(2)}) collective-permute-start(bf16[64,1152]{1,0:T(8,128)(2,1)} %get-tuple-element.15), channel_id=1, source_target_pairs={{0,2},{1,3},{2,0},{3,1},{4,6},{5,7},{6,4},{7,5},{8,10},{9,11},{10,... | collective-permute-start | bytes 442376 | tf_op jit(solution)/shard_map/ppermute | solution.py:332
  36.1 1.6 %slice_bitcast_fusion = (bf16[4,128,1024]{2,1,0:T(8,128)(2,1)}, bf16[4,128,1024]{2,1,0:T(8,128)(2,1)}) fusion(bf16[4,2,128,1024]{3,2,1,0:T(8,128)(2,1)S(1)} %copy-done), kind=kLoop, calls=%fused_computation | loop fusion | bytes 4194304 | tf_op jit(solution)/shard_map/squeeze | solution.py:400
  37.8 1.6 %collective-permute-start.4 = (bf16[4,128,1024]{2,1,0:T(8,128)(2,1)}, bf16[4,128,1024]{2,1,0:T(8,128)(2,1)S(1)}, u32[]{:S(2)}, u32[]{:S(2)}) collective-permute-start(bf16[4,128,1024]{2,1,0:T(8,128)(2,1)} %get-tuple-element.19), channel_id=1, source_target_pairs={{0,1},{1,2},{2,3},{3,4},{4,5},{5,6},{6,7},{8,9},{9,10},{10,11},{11... | collective-permute-start | bytes 3145736 | tf_op jit(solution)/shard_map/ppermute | solution.py:393
  39.4 1.5 collective-permute-start.5
  41.6 2.1 %register_merge.5 = (bf16[32,1152]{1,0:T(8,128)(2,1)}, bf16[32,1152]{1,0:T(8,128)(2,1)}) custom-call(s32[1]{0:T(128)} %bitcast.7.bit_ref, bf16[64,1152]{1,0:T(8,128)(2,1)} %get-tuple-element.14.a_ref, bf16[64,1152]{1,0:T(8,128)(2,1)} %copy-done.8), custom_call_target="tpu_custom_call" | custom-call | flops 2097152 | bytes 1048576 | tf_op jit(solution)/shard_map/register_merge/pallas_call | solution.py:304
  43.7 5.2 %collective-permute-start.8 = (bf16[32,1152]{1,0:T(8,128)(2,1)}, bf16[32,1152]{1,0:T(8,128)(2,1)S(1)}, u32[]{:S(2)}, u32[]{:S(2)}) collective-permute-start(bf16[32,1152]{1,0:T(8,128)(2,1)} %get-tuple-element.17), channel_id=1, source_target_pairs={{0,4},{1,5},{2,6},{3,7},{4,0},{5,1},{6,2},{7,3},{8,12},{9,13},{10,... | collective-permute-start | bytes 221192 | tf_op jit(solution)/shard_map/ppermute | solution.py:332
  49.7 12.4 %collective-permute-done.8.b_ref = bf16[32,1152]{1,0:T(8,128)(2,1)S(1)} collective-permute-done((bf16[32,1152]{1,0:T(8,128)(2,1)}, bf16[32,1152]{1,0:T(8,128)(2,1)S(1)}, u32[]{:S(2)}, u32[]{:S(2)}) %collective-permute-start.8) | collective-permute-done | bytes 73760 | tf_op jit(solution)/shard_map/ppermute | solution.py:332
  62.7 1.9 %register_merge.6.a_ref = bf16[32,1152]{1,0:T(8,128)(2,1)} custom-call(s32[1]{0:T(128)} %bitcast.6.bit_ref, bf16[32,1152]{1,0:T(8,128)(2,1)} %get-tuple-element.16.a_ref, bf16[32,1152]{1,0:T(8,128)(2,1)} %copy-done.11), custom_call_target="tpu_custom_call" | custom-call | flops 2097152 | bytes 1048576 | tf_op jit(solution)/shard_map/register_merge/pallas_call | solution.py:304
  65.3 1.3 collective-permute-start.2
  66.7 2.5 %collective-permute-done.9.b_ref = bf16[32,1152]{1,0:T(8,128)(2,1)S(1)} collective-permute-done((bf16[32,1152]{1,0:T(8,128)(2,1)}, bf16[32,1152]{1,0:T(8,128)(2,1)S(1)}, u32[]{:S(2)}, u32[]{:S(2)}) %collective-permute-start.9) | collective-permute-done | bytes 73760 | tf_op jit(solution)/shard_map/ppermute | solution.py:357
  69.8 1.9 %register_merge.7.a_ref = bf16[32,1152]{1,0:T(8,128)(2,1)} custom-call(s32[1]{0:T(128)} %bitcast.6.bit_ref, bf16[32,1152]{1,0:T(8,128)(2,1)} %register_merge.6.a_ref, bf16[32,1152]{1,0:T(8,128)(2,1)} %copy-done.10), custom_call_target="tpu_custom_call" | custom-call | flops 2097152 | bytes 1048576 | tf_op jit(solution)/shard_map/register_merge/pallas_call | solution.py:304
  71.7 1.5 collective-permute-start.10
  73.2 1.3 collective-permute-start.3
  74.5 1.7 %collective-permute-done.10.b_ref = bf16[32,1152]{1,0:T(8,128)(2,1)S(1)} collective-permute-done((bf16[32,1152]{1,0:T(8,128)(2,1)}, bf16[32,1152]{1,0:T(8,128)(2,1)S(1)}, u32[]{:S(2)}, u32[]{:S(2)}) %collective-permute-start.10) | collective-permute-done | bytes 73760 | tf_op jit(solution)/shard_map/ppermute | solution.py:357
  76.8 2.9 %register_out.1 = bf16[32,1024]{1,0:T(8,128)(2,1)} custom-call(s32[1]{0:T(128)} %bitcast.6.bit_ref, bf16[32,1152]{1,0:T(8,128)(2,1)} %register_merge.7.a_ref, bf16[32,1152]{1,0:T(8,128)(2,1)} %copy-done.9, bf16[1024,1024]{1,0:T(8,128)(2,1)} %w_ref.1), custom_call_target="tpu_custom_call" | custom-call | flops 2097152 | bytes 1048576 | tf_op jit(solution)/shard_map/register_out/pallas_call | solution.py:304
  79.8 15.1 %all_gather.3 = bf16[256,1024]{1,0:T(8,128)(2,1)S(1)} all-gather(bf16[32,1024]{1,0:T(8,128)(2,1)} %register_out.1), channel_id=1, replica_groups=mesh['phase'=4,'slab'=8] {'slab'}, dimensions={0}, use_global_device_ids=true | all-gather | bytes 589824 | tf_op jit(solution)/shard_map/all_gather | solution.py:379
  94.9 1.0 copy-done.3
  95.9 1.0 copy-done.4
  96.8 8.8 %halo_project.3.refs_4_.refs_0_.refs_1_.refs_2_.refs_3_.refs_5_ = bf16[26,128,2048]{2,1,0:T(8,128)(2,1)} custom-call(bf16[4,128,1024]{2,1,0:T(8,128)(2,1)} %copy-done.3, bf16[4,128,1024]{2,1,0:T(8,128)(2,1)} %copy-done.4, bf16[1024,1024]{1,0:T(8,128)(2,1)} %refs_2_.5, bf16[1024,1024]{1,0:T(8,128)(2,1)} %refs_3_.5, ...), custom_call_target="tpu_custom_call", output_to_operand_aliasing={{}: (4, {})} | custom-call | flops 4294967296 | bytes 10485760 | tf_op jit(solution)/shard_map/halo_project/pallas_call | solution.py:109
  105.7 18.8 %window_attend.2.refs_7_ = bf16[8,128,1024]{2,1,0:T(8,128)(2,1)} custom-call(s32[40]{0:T(128)} %reshape.22.idx_ref, bf16[1280,1024]{1,0:T(8,128)(2,1)} %get-tuple-element.10.q_ref.refs_0_, bf16[26,128,2048]{2,1,0:T(8,128)(2,1)} %halo_project.3.refs_4_.refs_0_.refs_1_.refs_2_.refs_3_.refs_5_, ...), custom_call_target="tpu_custom_call" | custom-call | flops 8589934592 | bytes 12582912 | tf_op jit(solution)/shard_map/window_attend/pallas_call | solution.py:192
  124.5 6.1 %halo_project.4.refs_4_ = bf16[26,128,2048]{2,1,0:T(8,128)(2,1)} custom-call(bf16[2,128,1024]{2,1,0:T(8,128)(2,1)} %copy-done.1, bf16[2,128,1024]{2,1,0:T(8,128)(2,1)} %copy-done.2, bf16[1024,1024]{1,0:T(8,128)(2,1)} %refs_2_.5, bf16[1024,1024]{1,0:T(8,128)(2,1)} %refs_3_.5, ...), custom_call_target="tpu_custom_call", output_to_operand_aliasing={{}: (4, {})} | custom-call | flops 2147483648 | bytes 10485760 | tf_op jit(solution)/shard_map/halo_project/pallas_call | solution.py:109
  131.4 0.8 copy-done.6
  132.2 6.1 %halo_project.5.refs_0_.refs_1_.refs_2_.refs_3_.refs_4_.refs_5_ = bf16[26,128,2048]{2,1,0:T(8,128)(2,1)} custom-call(bf16[2,128,1024]{2,1,0:T(8,128)(2,1)} %copy-done.5, bf16[2,128,1024]{2,1,0:T(8,128)(2,1)} %copy-done.6, bf16[1024,1024]{1,0:T(8,128)(2,1)} %refs_2_.5, bf16[1024,1024]{1,0:T(8,128)(2,1)} %refs_3_.5, ...), custom_call_target="tpu_custom_call", output_to_operand_aliasing={{}: (4, {})} | custom-call | flops 2147483648 | bytes 10485760 | tf_op jit(solution)/shard_map/halo_project/pallas_call | solution.py:109
  138.3 18.9 %window_attend.3 = bf16[8,128,1024]{2,1,0:T(8,128)(2,1)} custom-call(s32[40]{0:T(128)} %reshape.22.idx_ref, bf16[1280,1024]{1,0:T(8,128)(2,1)} %get-tuple-element.10.q_ref.refs_0_, bf16[26,128,2048]{2,1,0:T(8,128)(2,1)} %halo_project.5.refs_0_.refs_1_.refs_2_.refs_3_.refs_4_.refs_5_, ...), custom_call_target="tpu_custom_call", output_to_operand_aliasing={{}: (9, {})} | custom-call | flops 8589934592 | bytes 12582912 | tf_op jit(solution)/shard_map/window_attend/pallas_call | solution.py:192
  157.2 0.8 copy.22
  (39 shorter events, 6.0 us)
Async XLA Ops:
  14.2 12.0 %copy-start = (bf16[4,2,128,1024]{3,2,1,0:T(8,128)(2,1)S(1)}, bf16[4,2,128,1024]{3,2,1,0:T(8,128)(2,1)}, u32[]{:S(2)}) copy-start(bf16[4,2,128,1024]{3,2,1,0:T(8,128)(2,1)} %param.7) | copy-start | bytes 6291460
  25.8 5.0 %collective-permute-start.6 = (bf16[128,1152]{1,0:T(8,128)(2,1)}, bf16[128,1152]{1,0:T(8,128)(2,1)S(1)}, u32[]{:S(2)}, u32[]{:S(2)}) collective-permute-start(bf16[128,1152]{1,0:T(8,128)(2,1)} %get-tuple-element.13), channel_id=1, source_target_pairs={{0,1},{1,0},{2,3},{3,2},{4,5},{5,4},{6,7},{7,6},{8,9},{9,8},{10,11... | collective-permute-start | bytes 884744 | tf_op jit(solution)/shard_map/ppermute | solution.py:332
  27.3 37.8 %collective-permute-start = (bf16[2,128,1024]{2,1,0:T(8,128)(2,1)}, bf16[2,128,1024]{2,1,0:T(8,128)(2,1)S(1)}, u32[]{:S(2)}, u32[]{:S(2)}) collective-permute-start(bf16[2,128,1024]{2,1,0:T(8,128)(2,1)} %get-tuple-element.20), channel_id=1, source_target_pairs={{0,8},{8,16},{16,24},{24,0},{1,9},{9,17},{17,25},{25,1},{2,10},{10... | collective-permute-start | bytes 1572872 | tf_op jit(solution)/shard_map/ppermute | solution.py:393
  29.8 35.4 %collective-permute-start.1 = (bf16[2,128,1024]{2,1,0:T(8,128)(2,1)}, bf16[2,128,1024]{2,1,0:T(8,128)(2,1)S(1)}, u32[]{:S(2)}, u32[]{:S(2)}) collective-permute-start(bf16[2,128,1024]{2,1,0:T(8,128)(2,1)} %get-tuple-element.21), channel_id=1, source_target_pairs={{0,24},{8,0},{16,8},{24,16},{1,25},{9,1},{17,9},{25,17},{2,26},{10... | collective-permute-start | bytes 1572872 | tf_op jit(solution)/shard_map/ppermute | solution.py:393
  30.8 0.7 copy-start.7
  34.1 14.9 %copy-start.12 = (s32[4,2,5]{2,1,0:T(2,128)S(1)}, s32[4,2,5]{2,1,0:T(2,128)}, u32[]{:S(2)}) copy-start(s32[4,2,5]{2,1,0:T(2,128)} %param.8) | copy-start | bytes 484
  34.1 6.8 %collective-permute-start.7 = (bf16[64,1152]{1,0:T(8,128)(2,1)}, bf16[64,1152]{1,0:T(8,128)(2,1)S(1)}, u32[]{:S(2)}, u32[]{:S(2)}) collective-permute-start(bf16[64,1152]{1,0:T(8,128)(2,1)} %get-tuple-element.15), channel_id=1, source_target_pairs={{0,2},{1,3},{2,0},{3,1},{4,6},{5,7},{6,4},{7,5},{8,10},{9,11},{10,... | collective-permute-start | bytes 442376 | tf_op jit(solution)/shard_map/ppermute | solution.py:332
  37.8 57.1 %collective-permute-start.4 = (bf16[4,128,1024]{2,1,0:T(8,128)(2,1)}, bf16[4,128,1024]{2,1,0:T(8,128)(2,1)S(1)}, u32[]{:S(2)}, u32[]{:S(2)}) collective-permute-start(bf16[4,128,1024]{2,1,0:T(8,128)(2,1)} %get-tuple-element.19), channel_id=1, source_target_pairs={{0,1},{1,2},{2,3},{3,4},{4,5},{5,6},{6,7},{8,9},{9,10},{10,11},{11... | collective-permute-start | bytes 3145736 | tf_op jit(solution)/shard_map/ppermute | solution.py:393
  39.4 55.5 %collective-permute-start.5 = (bf16[4,128,1024]{2,1,0:T(8,128)(2,1)}, bf16[4,128,1024]{2,1,0:T(8,128)(2,1)S(1)}, u32[]{:S(2)}, u32[]{:S(2)}) collective-permute-start(bf16[4,128,1024]{2,1,0:T(8,128)(2,1)} %get-tuple-element.18), channel_id=1, source_target_pairs={{1,0},{2,1},{3,2},{4,3},{5,4},{6,5},{7,6},{9,8},{10,9},{11,10},{12... | collective-permute-start | bytes 3145736 | tf_op jit(solution)/shard_map/ppermute | solution.py:393
  40.9 0.7 copy-start.8
  43.7 18.3 %collective-permute-start.8 = (bf16[32,1152]{1,0:T(8,128)(2,1)}, bf16[32,1152]{1,0:T(8,128)(2,1)S(1)}, u32[]{:S(2)}, u32[]{:S(2)}) collective-permute-start(bf16[32,1152]{1,0:T(8,128)(2,1)} %get-tuple-element.17), channel_id=1, source_target_pairs={{0,4},{1,5},{2,6},{3,7},{4,0},{5,1},{6,2},{7,3},{8,12},{9,13},{10,... | collective-permute-start | bytes 221192 | tf_op jit(solution)/shard_map/ppermute | solution.py:332
  62.0 0.6 copy-start.11
  64.6 4.6 %collective-permute-start.9 = (bf16[32,1152]{1,0:T(8,128)(2,1)}, bf16[32,1152]{1,0:T(8,128)(2,1)S(1)}, u32[]{:S(2)}, u32[]{:S(2)}) collective-permute-start(bf16[32,1152]{1,0:T(8,128)(2,1)} %register_merge.6.a_ref), channel_id=1, source_target_pairs={{0,8},{8,0},{16,24},{24,16},{1,9},{9,1},{17,25},{25,17},{2,10},{10... | collective-permute-start | bytes 221192 | tf_op jit(solution)/shard_map/ppermute | solution.py:357
  65.2 8.1 %copy-start.1 = (bf16[2,128,1024]{2,1,0:T(8,128)(2,1)}, bf16[2,128,1024]{2,1,0:T(8,128)(2,1)S(1)}, u32[]{:S(2)}) copy-start(bf16[2,128,1024]{2,1,0:T(8,128)(2,1)S(1)} %collective-permute-done.refs_0_) | copy-start | bytes 1572868
  65.2 14.6 %copy-start.2 = (bf16[2,128,1024]{2,1,0:T(8,128)(2,1)}, bf16[2,128,1024]{2,1,0:T(8,128)(2,1)S(1)}, u32[]{:S(2)}) copy-start(bf16[2,128,1024]{2,1,0:T(8,128)(2,1)S(1)} %collective-permute-done.1.refs_1_) | copy-start | bytes 1572868
  65.3 65.3 %collective-permute-start.2 = (bf16[2,128,1024]{2,1,0:T(8,128)(2,1)S(1)}, bf16[2,128,1024]{2,1,0:T(8,128)(2,1)S(1)}, u32[]{:S(2)}, u32[]{:S(2)}) collective-permute-start(bf16[2,128,1024]{2,1,0:T(8,128)(2,1)S(1)} %pad_maximum_fusion), channel_id=1, source_target_pairs={{0,1},{1,2},{2,3},{3,4},{4,5},{5,6},{6,7},{8,9},{9,10},{10,11},{11... | collective-permute-start | bytes 1572872 | tf_op jit(solution)/shard_map/ppermute | solution.py:393
  69.1 0.6 copy-start.10
  71.7 4.6 %collective-permute-start.10 = (bf16[32,1152]{1,0:T(8,128)(2,1)}, bf16[32,1152]{1,0:T(8,128)(2,1)S(1)}, u32[]{:S(2)}, u32[]{:S(2)}) collective-permute-start(bf16[32,1152]{1,0:T(8,128)(2,1)} %register_merge.7.a_ref), channel_id=1, source_target_pairs={{0,16},{8,24},{16,0},{24,8},{1,17},{9,25},{17,1},{25,9},{2,18},{10... | collective-permute-start | bytes 221192 | tf_op jit(solution)/shard_map/ppermute | solution.py:357
  73.2 57.4 %collective-permute-start.3 = (bf16[2,128,1024]{2,1,0:T(8,128)(2,1)S(1)}, bf16[2,128,1024]{2,1,0:T(8,128)(2,1)S(1)}, u32[]{:S(2)}, u32[]{:S(2)}) collective-permute-start(bf16[2,128,1024]{2,1,0:T(8,128)(2,1)S(1)} %pad_maximum_fusion.1), channel_id=1, source_target_pairs={{1,0},{2,1},{3,2},{4,3},{5,4},{6,5},{7,6},{9,8},{10,9},{11,10},{12... | collective-permute-start | bytes 1572872 | tf_op jit(solution)/shard_map/ppermute | solution.py:393
  76.2 0.6 copy-start.9
  94.9 1.0 copy-start.3
  95.9 1.0 copy-start.4
  130.6 0.8 copy-start.5
  131.4 0.8 copy-start.6

commit v2 on v0

v2 whole, which is shorter than its diff:
```python
import functools

import jax
import jax.numpy as jnp
from jax import lax
from jax.experimental import pallas as pl
from jax.experimental.pallas import tpu as pltpu
from jax.sharding import PartitionSpec as P

HEADS = 16
LIST = 5
QUAD = 4
LOG2E = 1.4426950408889634
F32, BF16 = jnp.float32, jnp.bfloat16
ANY = pl.BlockSpec(memory_space=pl.ANY)
TOKEN = jax.ShapeDtypeStruct((8, 128), jnp.float32)


def params(mib):
    return pltpu.CompilerParams(vmem_limit_bytes=mib << 20)


def cost():
    return pl.CostEstimate(flops=1 << 20, bytes_accessed=1 << 16, transcendentals=0)


def matmul(a, b):
    return jnp.dot(a, b, preferred_element_type=F32)


def matmul_t(a, b):
    return lax.dot_general(a, b, (((1,), (1,)), ((), ())), preferred_element_type=F32)


def t_matmul(a, b):
    return lax.dot_general(a, b, (((0,), (0,)), ((), ())), preferred_element_type=F32)


def spread_heads(q, head_width, heads):
    lane = lax.broadcasted_iota(jnp.int32, q.shape, 1) // head_width
    return jnp.concatenate([jnp.where(lane == h, q, jnp.zeros_like(q)) for h in heads], axis=0)


def soften(s):
    peak = jnp.max(s, axis=0, keepdims=True)
    p = jnp.exp2(s - peak)
    total = jnp.sum(p, axis=0, keepdims=True)
    return p.astype(BF16), peak, total


def pair_context(v, p, inverse, head_width):
    o = t_matmul(v, p)
    count = p.shape[1] // 2
    return [
        o[j * head_width : (j + 1) * head_width, j * count : (j + 1) * count]
        * inverse[:, j * count : (j + 1) * count]
        for j in range(2)
    ]


def pack_levels(level):
    hi = level.astype(BF16)
    rest = level - hi.astype(F32)
    mid = rest.astype(BF16)
    low = (rest - mid.astype(F32)).astype(BF16)
    pad = jnp.zeros((level.shape[0], 128 - 3 * level.shape[1]), BF16)
    return jnp.concatenate([hi, mid, low, pad], axis=1)


def unpack_levels(cols):
    wide = cols.astype(F32)
    return wide[:, :HEADS] + wide[:, HEADS : 2 * HEADS] + wide[:, 2 * HEADS : 3 * HEADS]


def own_kernel(scale, head_width, slabs, slab_ref, *refs):
    x_ref, reg_ref, wq_ref, wk_ref, wv_ref = refs[:5]
    q_ref, kv_ref, reg_kv_ref = refs[5:8]
    part_refs = refs[8 : 8 + slabs]
    rows_ref, ctx_ref, level_ref = refs[8 + slabs :]
    step = pl.program_id(0)
    count, width = x_ref.shape
    regs = reg_ref.shape[0]
    blk, lanes = kv_ref.shape[2:]

    @pl.when(step == 0)
    def _():
        rows_ref[:count] = x_ref[...]
        rows_ref[count:] = reg_ref[...]

    k = matmul(rows_ref[...], wk_ref[...]).astype(BF16)
    q_reg = (matmul(reg_ref[...], wq_ref[...]) * scale).astype(BF16)
    pairs = [(h, h + 1) for h in range(0, lanes // head_width, 2)]

    def score(pair):
        return matmul_t(k[:count], spread_heads(q_reg, head_width, pair))

    s = score(pairs[0])
    v = matmul(rows_ref[...], wv_ref[...]).astype(BF16)
    pending = None
    outs, levels = [], []
    for n, pair in enumerate(pairs):
        following = score(pairs[n + 1]) if n + 1 < len(pairs) else None
        p, peak, total = soften(s)
        at = slice(pair[0] * head_width, (pair[1] + 1) * head_width)
        if n == 0:
            q_ref[...] = (matmul(x_ref[...], wq_ref[...]) * scale).astype(BF16)
        outs += pair_context(v[:count, at], p, 1.0 / total, head_width)
        level = peak + jnp.log2(total)
        levels += [level[:, :regs], level[:, regs:]]
        s = following
    for n in range(kv_ref.shape[1]):
        kv_ref[0, n] = k[n * blk : (n + 1) * blk]
        kv_ref[1, n] = v[n * blk : (n + 1) * blk]
    for n in range(reg_kv_ref.shape[1]):
        kv_at = slice(count + n * blk, count + (n + 1) * blk)
        reg_kv_ref[0, n] = k[kv_at]
        reg_kv_ref[1, n] = v[kv_at]
    out = jnp.concatenate(outs, axis=0).astype(BF16).T
    level_block = jnp.concatenate(levels + [jnp.zeros((8 - len(levels), regs), F32)], axis=0)
    for g in range(width // lanes):

        @pl.when(step == g)
        def _():
            ctx_ref[:, g * lanes : (g + 1) * lanes] = out
            level_ref[g] = level_block

    @pl.when(step == width // lanes - 1)
    def _():
        each = lanes // head_width
        stacked = jnp.concatenate([level_ref[g][:each] for g in range(width // lanes)], axis=0)
        ctx_ref[:, width:] = pack_levels(stacked.T)
        chunk = regs // slabs
        for shift in range(slabs):
            target = lax.rem(slab_ref[0] + shift, slabs)
            part_refs[shift][...] = ctx_ref[pl.ds(pl.multiple_of(target * chunk, chunk), chunk)]


def own_project(slab, rows, registers, w_query, w_key, w_value, slots, blk, head_width, slabs):
    count, width = rows.shape
    regs = registers.shape[0]
    lanes = QUAD * head_width
    chunk = regs // slabs
    tile = pl.BlockSpec((width, lanes), lambda i, s: (0, i))
    outs = pl.pallas_call(
        functools.partial(own_kernel, head_width ** (-0.5) * LOG2E, head_width, slabs),
        grid_spec=pltpu.PrefetchScalarGridSpec(
            num_scalar_prefetch=1,
            grid=(width // lanes,),
            in_specs=[
                pl.BlockSpec((count, width), lambda i, s: (0, 0)),
                pl.BlockSpec((regs, width), lambda i, s: (0, 0)),
                tile,
                tile,
                tile,
            ],
            out_specs=[
                pl.BlockSpec((count, lanes), lambda i, s: (0, i)),
                pl.BlockSpec((2, count // blk, blk, lanes), lambda i, s: (0, 0, 0, i)),
                pl.BlockSpec((2, regs // blk, blk, lanes), lambda i, s: (0, 0, 0, i)),
            ]
            + [pl.BlockSpec((chunk, width + 128), lambda i, s: (0, 0))] * slabs,
            scratch_shapes=[
                pltpu.VMEM((count + regs, width), BF16),
                pltpu.VMEM((regs, width + 128), BF16),
                pltpu.VMEM((width // lanes, 8, regs), F32),
            ],
        ),
        out_shape=[
            jax.ShapeDtypeStruct((count, width), BF16),
            jax.ShapeDtypeStruct((2, slots, blk, width), BF16),
            jax.ShapeDtypeStruct((2, regs // blk, blk, width), BF16),
        ]
        + [jax.ShapeDtypeStruct((chunk, width + 128), BF16)] * slabs,
        compiler_params=params(48),
        cost_estimate=cost(),
        name="own_project",
    )(slab, rows, registers, w_query, w_key, w_value)
    return outs[0], outs[1], outs[2], outs[3:]


def halo_kernel(pieces, deps, *refs):
    xs, wk_ref, wv_ref = refs[:pieces], refs[pieces], refs[pieces + 1]
    kv_ref, _, rows_ref, sems = refs[pieces + 3 + deps :]
    blk = kv_ref.shape[2]

    @pl.when(pl.program_id(0) == 0)
    def _():
        copies, at = [], 0
        for n, x in enumerate(xs):
            copies.append(pltpu.make_async_copy(x, rows_ref.at[pl.ds(at, x.shape[0])], sems.at[n]))
            at += x.shape[0]
        for c in copies:
            c.start()
        for c in copies:
            c.wait()

    for side, w_ref in ((0, wk_ref), (1, wv_ref)):
        out = matmul(rows_ref[...], w_ref[...]).astype(BF16)
        for n in range(kv_ref.shape[1]):
            kv_ref[side, n] = out[n * blk : (n + 1) * blk]


def halo_project(table, pieces, index, w_key, w_value, lanes, deps):
    _, slots, blk, width = table.shape
    pieces = [x.reshape(-1, width) for x in pieces]
    rows = sum(x.shape[0] for x in pieces)
    tile = pl.BlockSpec((width, lanes), lambda i: (0, i))
    return pl.pallas_call(
        functools.partial(halo_kernel, len(pieces), len(deps)),
        grid=(width // lanes,),
        in_specs=[ANY] * len(pieces) + [tile, tile, ANY] + [ANY] * len(deps),
        out_specs=[pl.BlockSpec((2, rows // blk, blk, lanes), lambda i: (0, index, 0, i)), ANY],
        out_shape=[jax.ShapeDtypeStruct(table.shape, BF16), TOKEN],
        scratch_shapes=[pltpu.VMEM((rows, width), BF16), pltpu.SemaphoreType.DMA((len(pieces),))],
        input_output_aliases={len(pieces) + 2: 0},
        compiler_params=params(40),
        cost_estimate=cost(),
        name="halo_project",
    )(*pieces, w_key, w_value, table, *deps)


def window_kernel(head_width, idx_ref, q_ref, *refs):
    kv_refs, (reg_ref, wo_ref) = refs[:LIST], refs[LIST : LIST + 2]
    o_ref, _, ctx_ref = refs[-3:]
    width = q_ref.shape[1]
    lanes = QUAD * head_width
    groups = width // lanes

    def gathered(side, at):
        return jnp.concatenate(
            [r[side, 0, :, at] for r in kv_refs]
            + [reg_ref[side, n, :, at] for n in range(reg_ref.shape[1])],
            axis=0,
        )

    def score(g):
        at = slice(g * lanes, (g + 1) * lanes)
        return matmul_t(gathered(0, at), spread_heads(q_ref[:, at], head_width, range(QUAD)))

    def context(g, p, inverse):
        outs = []
        rows = q_ref.shape[0]
        for h in range(0, QUAD, 2):
            start = g * lanes + h * head_width
            at = slice(h * rows, (h + 2) * rows)
            outs += pair_context(
                gathered(1, slice(start, start + 2 * head_width)), p[:, at], inverse[:, at], head_width
            )
        ctx_ref[:, g * lanes : (g + 1) * lanes] = jnp.concatenate(outs, axis=0).astype(BF16).T

    following, pending = score(0), None
    for g in range(groups):
        s = following
        if g + 1 < groups:
            following = score(g + 1)
        if pending is not None:
            context(*pending)
        p, _, total = soften(s)
        pending = (g, p, 1.0 / total)
    context(*pending)
    o_ref[0] = matmul(ctx_ref[...], wo_ref[...]).astype(BF16)


def window_attend(queries, table, reg_kv, slot_list, block, n, w_out, head_width, previous, deps):
    _, _, blk, width = table.shape
    total = queries.shape[0] // blk

    def list_map(entry):
        return lambda i, idx: (0, idx[block(i) * LIST + entry], 0, 0)

    operands = [slot_list, queries] + [table] * LIST + [reg_kv, w_out]
    in_specs = (
        [pl.BlockSpec((blk, width), lambda i, idx: (block(i), 0))]
        + [pl.BlockSpec((2, 1, blk, width), list_map(e)) for e in range(LIST)]
        + [
            pl.BlockSpec(reg_kv.shape, lambda i, idx: (0, 0, 0, 0)),
            pl.BlockSpec((width, width), lambda i, idx: (0, 0)),
        ]
    )
    aliases = {}
    if previous is not None:
        aliases = {len(operands): 0}
        operands.append(previous)
        in_specs.append(ANY)
    operands += deps
    in_specs += [ANY] * len(deps)
    return pl.pallas_call(
        functools.partial(window_kernel, head_width),
        grid_spec=pltpu.PrefetchScalarGridSpec(
            num_scalar_prefetch=1,
            grid=(n,),
            in_specs=in_specs,
            out_specs=[pl.BlockSpec((1, blk, width), lambda i, idx: (block(i), 0, 0)), ANY],
            scratch_shapes=[pltpu.VMEM((blk, width), BF16)],
        ),
        out_shape=[jax.ShapeDtypeStruct((total, blk, width), BF16), TOKEN],
        input_output_aliases=aliases,
        compiler_params=params(48),
        cost_estimate=cost(),
        name="window_attend",
    )(*operands)


def merged(refs, width):
    levels = [unpack_levels(r[:, width:]) for r in refs]
    top = functools.reduce(jnp.maximum, levels)
    weights = [jnp.exp2(level - top) for level in levels]
    total = functools.reduce(jnp.add, weights)
    inverse = 1.0 / total
    weights = [w * inverse for w in weights]
    rows = refs[0].shape[0]
    head_width = width // HEADS
    lower = lax.broadcasted_iota(jnp.int32, (rows, 2 * head_width), 1) < head_width
    cols = []
    for pair in range(HEADS // 2):
        at = slice(pair * 2 * head_width, (pair + 1) * 2 * head_width)
        mix = jnp.zeros((rows, 2 * head_width), F32)
        for r, w in zip(refs, weights):
            spread = jnp.where(lower, w[:, 2 * pair : 2 * pair + 1], w[:, 2 * pair + 1 : 2 * pair + 2])
            mix = mix + r[:, at].astype(F32) * spread
        cols.append(mix.astype(BF16))
    return jnp.concatenate(cols, axis=1), top + jnp.log2(total)


def vmem_call(body, out_shape, name, operands, deps):
    vmem = pl.BlockSpec(memory_space=pltpu.VMEM)

    def wrapped(*refs):
        body(*refs[: len(operands)], *refs[len(operands) + len(deps) :])

    return pl.pallas_call(
        wrapped,
        in_specs=[vmem] * len(operands) + [ANY] * len(deps),
        out_specs=vmem,
        out_shape=out_shape,
        compiler_params=params(16),
        cost_estimate=cost(),
        name=name,
    )(*operands, *deps)


def shift_all(parts, axis):
    n = lax.axis_size(axis)
    return [parts[0]] + [
        lax.ppermute(parts[j], axis, [(i, (i + j) % n) for i in range(n)]) for j in range(1, n)
    ]


def merge_slab(parts, deps):
    rows, wide = parts[0].shape
    width = wide - 128

    def body(*refs):
        mix, level = merged(refs[:-1], width)
        refs[-1][:, :width] = mix
        refs[-1][:, width:] = pack_levels(level)

    return vmem_call(body, jax.ShapeDtypeStruct((rows, wide), BF16), "register_merge", parts, deps)


def merge_phase(parts, w_out, deps):
    rows, wide = parts[0].shape
    width = wide - 128

    def body(*refs):
        mix, _ = merged(refs[:-2], width)
        refs[-1][...] = matmul(mix, refs[-2][...]).astype(BF16)

    return vmem_call(
        body, jax.ShapeDtypeStruct((rows, width), BF16), "register_out", [*parts, w_out], deps
    )


def assemble(slab, parts, deps):
    rows, width = parts[0].shape
    slabs = len(parts)

    def body(slab_ref, *refs):
        out_ref = refs[-1]
        for j in range(slabs):
            source = lax.rem(slab_ref[0] + slabs - j, slabs)
            out_ref[pl.ds(pl.multiple_of(source * rows, rows), rows)] = refs[j][...]

    vmem = pl.BlockSpec(memory_space=pltpu.VMEM)
    return pl.pallas_call(
        body,
        in_specs=[pl.BlockSpec(memory_space=pltpu.SMEM)] + [vmem] * slabs + [ANY] * len(deps),
        out_specs=vmem,
        out_shape=jax.ShapeDtypeStruct((rows * slabs, width), BF16),
        compiler_params=params(16),
        cost_estimate=cost(),
        name="register_assemble",
    )(slab, *parts, *deps)


def shards(normed, block_list, registers, w_query, w_key, w_value, w_out):
    own_phases, slab_blocks, blk, width = normed.shape
    head_width = width // HEADS
    lanes = QUAD * head_width
    phases, slabs = lax.axis_size("phase"), lax.axis_size("slab")
    own = own_phases * slab_blocks
    slab = lax.axis_index("slab").astype(jnp.int32)

    def around(x, axis, step, closed):
        n = lax.axis_size(axis)
        return lax.ppermute(
            x, axis, [(i, (i + step) % n) for i in range(n) if closed or 0 <= i + step < n]
        )

    before = around(normed[-1], "phase", 1, True)
    after = around(normed[0], "phase", -1, True)
    left = around(normed[:, -1], "slab", 1, False)
    right = around(normed[:, 0], "slab", -1, False)
    corner_left = around(jnp.stack([before[-1], after[-1]]), "slab", 1, False)
    corner_right = around(jnp.stack([before[0], after[0]]), "slab", -1, False)

    at_left = own
    at_right = at_left + own_phases
    at_before = at_right + own_phases
    at_after = at_before + slab_blocks
    at_corner = at_after + slab_blocks
    slots = at_corner + 4
    assert own == at_before - at_left == slots - at_before

    total_phases, depth_blocks = own_phases * phases, slab_blocks * slabs
    p = (block_list // depth_blocks - lax.axis_index("phase") * own_phases + 1) % total_phases - 1
    z = block_list % depth_blocks - slab * slab_blocks
    is_left, is_right = z < 0, z >= slab_blocks
    is_before, is_after = p < 0, p >= own_phases
    inner = jnp.where(is_left, at_left + p, jnp.where(is_right, at_right + p, p * slab_blocks + z))
    outer = jnp.where(
        is_left | is_right,
        at_corner + jnp.where(is_right, 2, 0) + jnp.where(is_after, 1, 0),
        jnp.where(is_after, at_after, at_before) + z,
    )
    slot_list = jnp.where(is_before | is_after, outer, inner).astype(jnp.int32).reshape(-1)

    queries, table, reg_kv, parts = own_project(
        slab.reshape(1),
        normed.reshape(-1, width),
        registers,
        w_query,
        w_key,
        w_value,
        slots,
        blk,
        head_width,
        slabs,
    )
    parts = shift_all(parts, "slab")
    table, _ = halo_project(table, [left, right], 1, w_key, w_value, lanes, [])
    middle = own - 2 * slab_blocks
    mixed, token = window_attend(
        queries,
        table,
        reg_kv,
        slot_list,
        lambda i: i + slab_blocks,
        middle,
        w_out,
        head_width,
        None,
        [before, after],
    )
    one = merge_slab(parts, [token])
    ones = shift_all([one] * phases, "phase")
    table, token = halo_project(
        table, [before, after, corner_left, corner_right], 2, w_key, w_value, lanes, [one]
    )
    share = merge_phase(ones, w_out, [token])
    shares = shift_all([share] * slabs, "slab")
    mixed, token = window_attend(
        queries,
        table,
        reg_kv,
        slot_list,
        lambda i: i + jnp.where(i >= slab_blocks, middle, 0),
        own - middle,
        w_out,
        head_width,
        mixed,
        [share],
    )
    register_out = assemble(slab.reshape(1), shares, [token])
    return mixed.reshape(own_phases, slab_blocks, blk, width), register_out


def solution(mesh):
    placed = (P("phase", "slab", None, None), P("phase", "slab", None), P(), P(), P(), P(), P())
    return jax.shard_map(
        shards,
        mesh=mesh,
        in_specs=placed,
        out_specs=(P("phase", "slab", None, None), P()),
        check_vma=False,
    )
```

time: 445 us -> 131 us (0.29)
  local copies, waits for them, and re-layouts: 119 us -> 7.55 us
  blocking collectives: 92.7 us -> 0 us
  matrix products: 85.7 us -> 0 us
  Pallas kernels: 0 us -> 69.9 us
  waiting for transfers between devices: 70.5 us -> 16.3 us
  other arithmetic: 52.5 us -> 1.74 us
  starting transfers between devices: 8.29 us -> 34.8 us
  between operations: 14.2 us -> 0.88 us
    dot_general x17 -> x0, matrix products: 85.7 us -> none  [the longest x7 21.9 us: project(): jnp.dot(token_rows, weight, preferred_element_type=jnp.float32)]
    psum x1 -> x0, waiting for transfers between devices: 70.4 us -> none  [shards(): lax.psum((weight_sum * factor, weighted * factor.T[:, :, None]), ('phase'...]
    pallas_call x0 -> x8, Pallas kernels: none -> 69.9 us  [the longest x2 29.6 us: window_attend(): pl.pallas_call(functools.partial(window_kernel, head_width), grid_spec=pl...]
    pmax x1 -> x0, blocking collectives: 52 us -> none  [shards(): global_peak = lax.pmax(row_peak, ('phase', 'slab'))]
    psum x1 -> x0, blocking collectives: 40.7 us -> none  [shards(): lax.psum((weight_sum * factor, weighted * factor.T[:, :, None]), ('phase'...]
    slice x8 -> x2, local copies, waits for them, and re-layouts: 40.7 us -> 0.07 us  [shards(): corner_right = around(jnp.stack([before[0], after[0]]), 'slab', -1, False)]
    while x13 -> x0, local copies, waits for them, and re-layouts: 37.4 us -> none
    ppermute x4 -> x23, starting transfers between devices: 8.25 us -> 34.8 us  [the longest x17 20.4 us: shift_all(): lax.ppermute(parts[j], axis, [(i, (i + j) % n) for i in range(n)])]
  transfers between devices with their start and end apart: 5 -> 23, of which waited for: 1 -> 3; matrix products, arithmetic and copies ran while one was open for 18% -> 3% of each run, Pallas kernels for 0% -> 52%
where the time goes in v2:
time: 131 us
  Pallas kernels  69.9 us (53%)
  starting transfers between devices  34.8 us (27%)
  waiting for transfers between devices  16.3 us (12%)
  local copies, waits for them, and re-layouts  7.55 us (6%)
  other arithmetic  1.74 us (1%)
    pallas_call x2, Pallas kernels, window_attend(): pl.pallas_call(functools.partial(window_kernel, head_width), grid_spec=pl...  29.6 us
    ppermute x17, starting transfers between devices, shift_all(): lax.ppermute(parts[j], axis, [(i, (i + j) % n) for i in range(n)])  20.4 us
    pallas_call x1, Pallas kernels, own_project(): pl.pallas_call(functools.partial(own_kernel, head_width ** (-0.5) * LOG2E...  20.1 us
    pallas_call x2, Pallas kernels, halo_project(): pl.pallas_call(functools.partial(halo_kernel, len(pieces), len(deps)), gr...  16.6 us
    ppermute x17, waiting for transfers between devices, shift_all(): lax.ppermute(parts[j], axis, [(i, (i + j) % n) for i in range(n)])  16.3 us
    ppermute x6, starting transfers between devices, around(): lax.ppermute(x, axis, [(i, (i + step) % n) for i in range(n) if closed or...  14.4 us
    unnamed x28, local copies, waits for them, and re-layouts  3.51 us
    pallas_call x2, Pallas kernels, vmem_call(): pl.pallas_call(wrapped, in_specs=[vmem] * len(operands) + [ANY] * len(dep...  2.76 us
  transfers between devices with their start and end apart: 23, of which 3 were waited for; matrix products, arithmetic and copies ran while one was open for 3% of the time, Pallas kernels for 52%

profile of v2, /device:TPU:0, one launch (start us, length us, event | category | flops | bytes accessed | tf_op | source)
XLA Modules:
  0.0 131.2 jit_solution(4642341645901023844)
XLA Ops:
  0.6 2.4 %slice_bitcast_fusion.2 = (bf16[2,128,1024]{2,1,0:T(8,128)(2,1)}, bf16[2,128,1024]{2,1,0:T(8,128)(2,1)}) fusion(bf16[4,2,128,1024]{3,2,1,0:T(8,128)(2,1)} %param.7), kind=kLoop, calls=%fused_computation.4 | loop fusion | bytes 2097152 | tf_op jit(solution)/shard_map/squeeze | solution.py:411
  3.0 2.9 %collective-permute-start = (bf16[2,128,1024]{2,1,0:T(8,128)(2,1)}, bf16[2,128,1024]{2,1,0:T(8,128)(2,1)S(1)}, u32[]{:S(2)}, u32[]{:S(2)}) collective-permute-start(bf16[2,128,1024]{2,1,0:T(8,128)(2,1)} %get-tuple-element.41), channel_id=1, source_target_pairs={{0,8},{8,16},{16,24},{24,0},{1,9},{9,17},{17,25},{25,1},{2,10},{10... | collective-permute-start | bytes 1572872 | tf_op jit(solution)/shard_map/ppermute | solution.py:406
  6.0 1.0 collective-permute-start.1
  6.9 1.5 %slice_bitcast_fusion = (bf16[4,128,1024]{2,1,0:T(8,128)(2,1)}, bf16[4,128,1024]{2,1,0:T(8,128)(2,1)}) fusion(bf16[4,2,128,1024]{3,2,1,0:T(8,128)(2,1)S(1)} %copy-done.12), kind=kLoop, calls=%fused_computation | loop fusion | bytes 4194304 | tf_op jit(solution)/shard_map/squeeze | solution.py:413
  8.4 1.3 collective-permute-start.5
  9.7 4.0 %collective-permute-start.4 = (bf16[4,128,1024]{2,1,0:T(8,128)(2,1)}, bf16[4,128,1024]{2,1,0:T(8,128)(2,1)}, u32[]{:S(2)}, u32[]{:S(2)}) collective-permute-start(bf16[4,128,1024]{2,1,0:T(8,128)(2,1)} %get-tuple-element.39), channel_id=1, source_target_pairs={{0,1},{1,2},{2,3},{3,4},{4,5},{5,6},{6,7},{8,9},{9,10},{10,11},{11... | collective-permute-start | bytes 3145736 | tf_op jit(solution)/shard_map/ppermute | solution.py:406
  13.7 20.1 %own_project.1 = (bf16[1024,1024]{1,0:T(8,128)(2,1)S(1)}, bf16[2,24,128,1024]{3,2,1,0:T(8,128)(2,1)}, bf16[2,2,128,1024]{3,2,1,0:T(8,128)(2,1)S(1)}, bf16[32,115...) custom-call(s32[1]{0:T(128)} %bitcast.slab_ref, ...), custom_call_target="tpu_custom_call" | custom-call | flops 1048576 | bytes 65536 | tf_op jit(solution)/shard_map/own_project/pallas_call | solution.py:144
  34.5 0.6 copy-done.10
  35.7 3.0 %collective-permute-start.10 = (bf16[32,1152]{1,0:T(8,128)(2,1)S(1)}, bf16[32,1152]{1,0:T(8,128)(2,1)S(1)}, u32[]{:S(2)}, u32[]{:S(2)}) collective-permute-start(bf16[32,1152]{1,0:T(8,128)(2,1)S(1)} %get-tuple-element.28), channel_id=1, source_target_pairs={{0,5},{1,6},{2,7},{3,0},{4,1},{5,2},{6,3},{7,4},{8,13},{9,14},{10,... | collective-permute-start | bytes 221192 | tf_op jit(solution)/shard_map/ppermute | solution.py:345
  38.8 0.8 pad_maximum_fusion
  39.7 4.0 %collective-permute-start.2 = (bf16[2,128,1024]{2,1,0:T(8,128)(2,1)}, bf16[2,128,1024]{2,1,0:T(8,128)(2,1)}, u32[]{:S(2)}, u32[]{:S(2)}) collective-permute-start(bf16[2,128,1024]{2,1,0:T(8,128)(2,1)} %pad_maximum_fusion), channel_id=1, source_target_pairs={{0,1},{1,2},{2,3},{3,4},{4,5},{5,6},{6,7},{8,9},{9,10},{10,11},{11... | collective-permute-start | bytes 1572872 | tf_op jit(solution)/shard_map/ppermute | solution.py:406
  43.6 0.9 pad_maximum_fusion.1
  44.5 1.3 collective-permute-start.3
  45.8 2.0 %collective-permute-start.11 = (bf16[32,1152]{1,0:T(8,128)(2,1)S(1)}, bf16[32,1152]{1,0:T(8,128)(2,1)S(1)}, u32[]{:S(2)}, u32[]{:S(2)}) collective-permute-start(bf16[32,1152]{1,0:T(8,128)(2,1)S(1)} %get-tuple-element.29), channel_id=1, source_target_pairs={{0,6},{1,7},{2,0},{3,1},{4,2},{5,3},{6,4},{7,5},{8,14},{9,15},{10,... | collective-permute-start | bytes 221192 | tf_op jit(solution)/shard_map/ppermute | solution.py:345
  47.8 8.4 %collective-permute-done.11.refs_6_ = bf16[32,1152]{1,0:T(8,128)(2,1)S(1)} collective-permute-done((bf16[32,1152]{1,0:T(8,128)(2,1)S(1)}, bf16[32,1152]{1,0:T(8,128)(2,1)S(1)}, u32[]{:S(2)}, u32[]{:S(2)}) %collective-permute-start.11) | collective-permute-done | bytes 73760 | tf_op jit(solution)/shard_map/ppermute | solution.py:345
  56.2 2.0 %collective-permute-done.12.refs_7_ = bf16[32,1152]{1,0:T(8,128)(2,1)S(1)} collective-permute-done((bf16[32,1152]{1,0:T(8,128)(2,1)S(1)}, bf16[32,1152]{1,0:T(8,128)(2,1)S(1)}, u32[]{:S(2)}, u32[]{:S(2)}) %collective-permute-start.12) | collective-permute-done | bytes 73760 | tf_op jit(solution)/shard_map/ppermute | solution.py:345
  58.2 5.8 %collective-permute-done.6.refs_1_ = bf16[32,1152]{1,0:T(8,128)(2,1)S(1)} collective-permute-done((bf16[32,1152]{1,0:T(8,128)(2,1)}, bf16[32,1152]{1,0:T(8,128)(2,1)S(1)}, u32[]{:S(2)}, u32[]{:S(2)}) %collective-permute-start.6) | collective-permute-done | bytes 73760 | tf_op jit(solution)/shard_map/ppermute | solution.py:345
  64.3 1.6 %copy-done.1 = bf16[1024,1024]{1,0:T(8,128)(2,1)S(1)} copy-done((bf16[1024,1024]{1,0:T(8,128)(2,1)S(1)}, bf16[1024,1024]{1,0:T(8,128)(2,1)}, u32[]{:S(2)}) %copy-start.1) | copy-done | bytes 2097176
  65.9 8.4 %halo_project.2 = (bf16[2,24,128,1024]{3,2,1,0:T(8,128)(2,1)}, f32[8,128]{1,0:T(8,128)}) custom-call(bf16[512,1024]{1,0:T(8,128)(2,1)} %bitcast.9.refs_0_, bf16[512,1024]{1,0:T(8,128)(2,1)} %bitcast.11.refs_1_, bf16[1024,1024]{1,0:T(8,128)(2,1)S(1)} %copy-done, bf16[1024,1024]{1,0:T(8,128)(2,1)S(1)} %copy-done.1, ...), custom_call_target="tpu_custom_call", output_to_operand_aliasing={{0}: (4, {})} | custom-call | flops 1048576 | bytes 65536 | tf_op jit(solution)/shard_map/halo_project/pallas_call | solution.py:208
  74.3 15.0 %window_attend.2 = (bf16[8,128,1024]{2,1,0:T(8,128)(2,1)}, f32[8,128]{1,0:T(8,128)S(1)}) custom-call(s32[40]{0:T(128)S(1)} %reshape.35.idx_ref, bf16[1024,1024]{1,0:T(8,128)(2,1)S(1)} %copy-done.5, bf16[2,24,128,1024]{3,2,1,0:T(8,128)(2,1)} %get-tuple-element.22.refs_0_.refs_1_.refs_2_.refs_3_.refs_4_.refs_6_, ...), custom_call_target="tpu_custom_call" | custom-call | flops 1048576 | bytes 65536 | tf_op jit(solution)/shard_map/window_attend/pallas_call | solution.py:287
  89.3 1.9 %register_merge.1.refs_7_.refs_0_ = bf16[32,1152]{1,0:T(8,128)(2,1)S(1)} custom-call(bf16[32,1152]{1,0:T(8,128)(2,1)S(1)} %get-tuple-element.23.refs_0_, bf16[32,1152]{1,0:T(8,128)(2,1)S(1)} %collective-permute-done.6.refs_1_, bf16[32,1152]{1,0:T(8,128)(2,1)} %collective-permute-done.7.refs_2_, bf16[32,1152]{1,0:T(8,128)(2,1)} %collective-permute-done.8.refs_3_, ...), custom_call_target="tpu_custom_call" | custom-call | flops 1048576 | bytes 65536 | tf_op jit(solution)/shard_map/register_merge/pallas_call | solution.py:331
  91.2 0.6 collective-permute-start.13
  91.9 1.5 %collective-permute-start.14 = (bf16[32,1152]{1,0:T(8,128)(2,1)S(1)}, bf16[32,1152]{1,0:T(8,128)(2,1)S(1)}, u32[]{:S(2)}, u32[]{:S(2)}) collective-permute-start(bf16[32,1152]{1,0:T(8,128)(2,1)S(1)} %register_merge.1.refs_7_.refs_0_), channel_id=1, source_target_pairs={{0,16},{8,24},{16,0},{24,8},{1,17},{9,25},{17,1},{25,9},{2,18},{10... | collective-permute-start | bytes 221192 | tf_op jit(solution)/shard_map/ppermute | solution.py:345
  93.4 2.3 %collective-permute-start.15 = (bf16[32,1152]{1,0:T(8,128)(2,1)S(1)}, bf16[32,1152]{1,0:T(8,128)(2,1)S(1)}, u32[]{:S(2)}, u32[]{:S(2)}) collective-permute-start(bf16[32,1152]{1,0:T(8,128)(2,1)S(1)} %register_merge.1.refs_7_.refs_0_), channel_id=1, source_target_pairs={{0,24},{8,0},{16,8},{24,16},{1,25},{9,1},{17,9},{25,17},{2,26},{10... | collective-permute-start | bytes 221192 | tf_op jit(solution)/shard_map/ppermute | solution.py:345
  95.8 8.2 %halo_project.3 = (bf16[2,24,128,1024]{3,2,1,0:T(8,128)(2,1)}, f32[8,128]{1,0:T(8,128)S(1)}) custom-call(bf16[256,1024]{1,0:T(8,128)(2,1)S(1)} %bitcast.17, bf16[256,1024]{1,0:T(8,128)(2,1)S(1)} %bitcast.18, bf16[256,1024]{1,0:T(8,128)(2,1)} %bitcast.6.refs_2_, bf16[256,1024]{1,0:T(8,128)(2,1)} %bitcast.7.refs_3_, ...), custom_call_target="tpu_custom_call", output_to_operand_aliasing={{0}: (6, {})} | custom-call | flops 1048576 | bytes 65536 | tf_op jit(solution)/shard_map/halo_project/pallas_call | solution.py:208
  104.0 0.8 register_out.1.refs_8_.refs_0_
  104.9 1.8 %collective-permute-start.16 = (bf16[32,1024]{1,0:T(8,128)(2,1)S(1)}, bf16[32,1024]{1,0:T(8,128)(2,1)S(1)}, u32[]{:S(2)}, u32[]{:S(2)}) collective-permute-start(bf16[32,1024]{1,0:T(8,128)(2,1)S(1)} %register_out.1.refs_8_.refs_0_), channel_id=1, source_target_pairs={{0,1},{1,2},{2,3},{3,4},{4,5},{5,6},{6,7},{7,0},{8,9},{9,10},{10,1... | collective-permute-start | bytes 196616 | tf_op jit(solution)/shard_map/ppermute | solution.py:345
  106.7 2.6 %collective-permute-start.17 = (bf16[32,1024]{1,0:T(8,128)(2,1)S(1)}, bf16[32,1024]{1,0:T(8,128)(2,1)S(1)}, u32[]{:S(2)}, u32[]{:S(2)}) collective-permute-start(bf16[32,1024]{1,0:T(8,128)(2,1)S(1)} %register_out.1.refs_8_.refs_0_), channel_id=1, source_target_pairs={{0,2},{1,3},{2,4},{3,5},{4,6},{5,7},{6,0},{7,1},{8,10},{9,11},{10,... | collective-permute-start | bytes 196616 | tf_op jit(solution)/shard_map/ppermute | solution.py:345
  109.3 3.7 %collective-permute-start.19 = (bf16[32,1024]{1,0:T(8,128)(2,1)S(1)}, bf16[32,1024]{1,0:T(8,128)(2,1)S(1)}, u32[]{:S(2)}, u32[]{:S(2)}) collective-permute-start(bf16[32,1024]{1,0:T(8,128)(2,1)S(1)} %register_out.1.refs_8_.refs_0_), channel_id=1, source_target_pairs={{0,4},{1,5},{2,6},{3,7},{4,0},{5,1},{6,2},{7,3},{8,12},{9,13},{10,... | collective-permute-start | bytes 196616 | tf_op jit(solution)/shard_map/ppermute | solution.py:345
  113.5 1.7 %collective-permute-start.21 = (bf16[32,1024]{1,0:T(8,128)(2,1)S(1)}, bf16[32,1024]{1,0:T(8,128)(2,1)S(1)}, u32[]{:S(2)}, u32[]{:S(2)}) collective-permute-start(bf16[32,1024]{1,0:T(8,128)(2,1)S(1)} %register_out.1.refs_8_.refs_0_), channel_id=1, source_target_pairs={{0,6},{1,7},{2,0},{3,1},{4,2},{5,3},{6,4},{7,5},{8,14},{9,15},{10,... | collective-permute-start | bytes 196616 | tf_op jit(solution)/shard_map/ppermute | solution.py:345
  115.8 14.6 %window_attend.3 = (bf16[8,128,1024]{2,1,0:T(8,128)(2,1)}, f32[8,128]{1,0:T(8,128)S(1)}) custom-call(s32[40]{0:T(128)S(1)} %reshape.35.idx_ref, bf16[1024,1024]{1,0:T(8,128)(2,1)S(1)} %copy-done.5, bf16[2,24,128,1024]{3,2,1,0:T(8,128)(2,1)} %get-tuple-element.33.refs_0_.refs_1_.refs_2_.refs_3_.refs_4_, ...), custom_call_target="tpu_custom_call", output_to_operand_aliasing={{0}: (9, {})} | custom-call | flops 1048576 | bytes 65536 | tf_op jit(solution)/shard_map/window_attend/pallas_call | solution.py:287
  130.4 0.8 register_assemble.1
  (58 shorter events, 2.6 us)
Async XLA Ops:
  3.0 35.7 %collective-permute-start = (bf16[2,128,1024]{2,1,0:T(8,128)(2,1)}, bf16[2,128,1024]{2,1,0:T(8,128)(2,1)S(1)}, u32[]{:S(2)}, u32[]{:S(2)}) collective-permute-start(bf16[2,128,1024]{2,1,0:T(8,128)(2,1)} %get-tuple-element.41), channel_id=1, source_target_pairs={{0,8},{8,16},{16,24},{24,0},{1,9},{9,17},{17,25},{25,1},{2,10},{10... | collective-permute-start | bytes 1572872 | tf_op jit(solution)/shard_map/ppermute | solution.py:406
  6.0 7.8 %copy-start.8 = (bf16[256,1024]{1,0:T(8,128)(2,1)S(1)}, bf16[256,1024]{1,0:T(8,128)(2,1)}, u32[]{:S(2)}) copy-start(bf16[256,1024]{1,0:T(8,128)(2,1)} %refs_1_.1) | copy-start | bytes 1572868
  6.0 32.8 %collective-permute-start.1 = (bf16[2,128,1024]{2,1,0:T(8,128)(2,1)}, bf16[2,128,1024]{2,1,0:T(8,128)(2,1)S(1)}, u32[]{:S(2)}, u32[]{:S(2)}) collective-permute-start(bf16[2,128,1024]{2,1,0:T(8,128)(2,1)} %get-tuple-element.40), channel_id=1, source_target_pairs={{0,24},{8,0},{16,8},{24,16},{1,25},{9,1},{17,9},{25,17},{2,26},{10... | collective-permute-start | bytes 1572872 | tf_op jit(solution)/shard_map/ppermute | solution.py:406
  8.4 55.6 %collective-permute-start.5 = (bf16[4,128,1024]{2,1,0:T(8,128)(2,1)}, bf16[4,128,1024]{2,1,0:T(8,128)(2,1)}, u32[]{:S(2)}, u32[]{:S(2)}) collective-permute-start(bf16[4,128,1024]{2,1,0:T(8,128)(2,1)} %get-tuple-element.38), channel_id=1, source_target_pairs={{1,0},{2,1},{3,2},{4,3},{5,4},{6,5},{7,6},{9,8},{10,9},{11,10},{12... | collective-permute-start | bytes 3145736 | tf_op jit(solution)/shard_map/ppermute | solution.py:406
  9.7 54.3 %collective-permute-start.4 = (bf16[4,128,1024]{2,1,0:T(8,128)(2,1)}, bf16[4,128,1024]{2,1,0:T(8,128)(2,1)}, u32[]{:S(2)}, u32[]{:S(2)}) collective-permute-start(bf16[4,128,1024]{2,1,0:T(8,128)(2,1)} %get-tuple-element.39), channel_id=1, source_target_pairs={{0,1},{1,2},{2,3},{3,4},{4,5},{5,6},{6,7},{8,9},{9,10},{10,11},{11... | collective-permute-start | bytes 3145736 | tf_op jit(solution)/shard_map/ppermute | solution.py:406
  35.7 8.8 %copy-start.4 = (bf16[1024,1024]{1,0:T(8,128)(2,1)}, bf16[1024,1024]{1,0:T(8,128)(2,1)S(1)}, u32[]{:S(2)}) copy-start(bf16[1024,1024]{1,0:T(8,128)(2,1)S(1)} %get-tuple-element.20.q_ref) | copy-start | bytes 6291460
  35.7 8.8 %copy-start.6 = (bf16[2,2,128,1024]{3,2,1,0:T(8,128)(2,1)}, bf16[2,2,128,1024]{3,2,1,0:T(8,128)(2,1)S(1)}, u32[]{:S(2)}) copy-start(bf16[2,2,128,1024]{3,2,1,0:T(8,128)(2,1)S(1)} %get-tuple-element.31.refs_5_) | copy-start | bytes 3145732
  35.7 28.4 %copy-start.13 = (s32[4,2,5]{2,1,0:T(2,128)S(1)}, s32[4,2,5]{2,1,0:T(2,128)}, u32[]{:S(2)}) copy-start(s32[4,2,5]{2,1,0:T(2,128)} %param.8) | copy-start | bytes 484
  35.7 28.5 %copy-start = (bf16[1024,1024]{1,0:T(8,128)(2,1)S(1)}, bf16[1024,1024]{1,0:T(8,128)(2,1)}, u32[]{:S(2)}) copy-start(bf16[1024,1024]{1,0:T(8,128)(2,1)} %refs_4_.4) | copy-start | bytes 6291460
  35.7 10.0 %collective-permute-start.10 = (bf16[32,1152]{1,0:T(8,128)(2,1)S(1)}, bf16[32,1152]{1,0:T(8,128)(2,1)S(1)}, u32[]{:S(2)}, u32[]{:S(2)}) collective-permute-start(bf16[32,1152]{1,0:T(8,128)(2,1)S(1)} %get-tuple-element.28), channel_id=1, source_target_pairs={{0,5},{1,6},{2,7},{3,0},{4,1},{5,2},{6,3},{7,4},{8,13},{9,14},{10,... | collective-permute-start | bytes 221192 | tf_op jit(solution)/shard_map/ppermute | solution.py:345
  39.7 56.1 %collective-permute-start.2 = (bf16[2,128,1024]{2,1,0:T(8,128)(2,1)}, bf16[2,128,1024]{2,1,0:T(8,128)(2,1)}, u32[]{:S(2)}, u32[]{:S(2)}) collective-permute-start(bf16[2,128,1024]{2,1,0:T(8,128)(2,1)} %pad_maximum_fusion), channel_id=1, source_target_pairs={{0,1},{1,2},{2,3},{3,4},{4,5},{5,6},{6,7},{8,9},{9,10},{10,11},{11... | collective-permute-start | bytes 1572872 | tf_op jit(solution)/shard_map/ppermute | solution.py:406
  44.5 51.3 %collective-permute-start.3 = (bf16[2,128,1024]{2,1,0:T(8,128)(2,1)}, bf16[2,128,1024]{2,1,0:T(8,128)(2,1)}, u32[]{:S(2)}, u32[]{:S(2)}) collective-permute-start(bf16[2,128,1024]{2,1,0:T(8,128)(2,1)} %pad_maximum_fusion.1), channel_id=1, source_target_pairs={{1,0},{2,1},{3,2},{4,3},{5,4},{6,5},{7,6},{9,8},{10,9},{11,10},{12... | collective-permute-start | bytes 1572872 | tf_op jit(solution)/shard_map/ppermute | solution.py:406
  45.8 10.4 %collective-permute-start.11 = (bf16[32,1152]{1,0:T(8,128)(2,1)S(1)}, bf16[32,1152]{1,0:T(8,128)(2,1)S(1)}, u32[]{:S(2)}, u32[]{:S(2)}) collective-permute-start(bf16[32,1152]{1,0:T(8,128)(2,1)S(1)} %get-tuple-element.29), channel_id=1, source_target_pairs={{0,6},{1,7},{2,0},{3,1},{4,2},{5,3},{6,4},{7,5},{8,14},{9,15},{10,... | collective-permute-start | bytes 221192 | tf_op jit(solution)/shard_map/ppermute | solution.py:345
  56.2 2.0 %collective-permute-start.12 = (bf16[32,1152]{1,0:T(8,128)(2,1)S(1)}, bf16[32,1152]{1,0:T(8,128)(2,1)S(1)}, u32[]{:S(2)}, u32[]{:S(2)}) collective-permute-start(bf16[32,1152]{1,0:T(8,128)(2,1)S(1)} %get-tuple-element.30), channel_id=1, source_target_pairs={{0,7},{1,0},{2,1},{3,2},{4,3},{5,4},{6,5},{7,6},{8,15},{9,8},{10,9... | collective-permute-start | bytes 221192 | tf_op jit(solution)/shard_map/ppermute | solution.py:345
  58.2 5.8 %collective-permute-start.6 = (bf16[32,1152]{1,0:T(8,128)(2,1)}, bf16[32,1152]{1,0:T(8,128)(2,1)S(1)}, u32[]{:S(2)}, u32[]{:S(2)}) collective-permute-start(bf16[32,1152]{1,0:T(8,128)(2,1)} %get-tuple-element.24), channel_id=1, source_target_pairs={{0,1},{1,2},{2,3},{3,4},{4,5},{5,6},{6,7},{7,0},{8,9},{9,10},{10,1... | collective-permute-start | bytes 221192 | tf_op jit(solution)/shard_map/ppermute | solution.py:345
  64.0 25.3 %collective-permute-start.7 = (bf16[32,1152]{1,0:T(8,128)(2,1)}, bf16[32,1152]{1,0:T(8,128)(2,1)}, u32[]{:S(2)}, u32[]{:S(2)}) collective-permute-start(bf16[32,1152]{1,0:T(8,128)(2,1)} %copy-done.11), channel_id=1, source_target_pairs={{0,2},{1,3},{2,4},{3,5},{4,6},{5,7},{6,0},{7,1},{8,10},{9,11},{10,... | collective-permute-start | bytes 221192 | tf_op jit(solution)/shard_map/ppermute | solution.py:345
  64.0 25.3 %collective-permute-start.8 = (bf16[32,1152]{1,0:T(8,128)(2,1)}, bf16[32,1152]{1,0:T(8,128)(2,1)}, u32[]{:S(2)}, u32[]{:S(2)}) collective-permute-start(bf16[32,1152]{1,0:T(8,128)(2,1)} %copy-done.10), channel_id=1, source_target_pairs={{0,3},{1,4},{2,5},{3,6},{4,7},{5,0},{6,1},{7,2},{8,11},{9,12},{10,... | collective-permute-start | bytes 221192 | tf_op jit(solution)/shard_map/ppermute | solution.py:345
  64.0 25.3 %collective-permute-start.9 = (bf16[32,1152]{1,0:T(8,128)(2,1)}, bf16[32,1152]{1,0:T(8,128)(2,1)}, u32[]{:S(2)}, u32[]{:S(2)}) collective-permute-start(bf16[32,1152]{1,0:T(8,128)(2,1)} %copy-done.9), channel_id=1, source_target_pairs={{0,4},{1,5},{2,6},{3,7},{4,0},{5,1},{6,2},{7,3},{8,12},{9,13},{10,... | collective-permute-start | bytes 221192 | tf_op jit(solution)/shard_map/ppermute | solution.py:345
  65.8 8.4 %copy-start.5 = (bf16[1024,1024]{1,0:T(8,128)(2,1)S(1)}, bf16[1024,1024]{1,0:T(8,128)(2,1)}, u32[]{:S(2)}) copy-start(bf16[1024,1024]{1,0:T(8,128)(2,1)} %copy-done.4) | copy-start | bytes 6291460
  65.8 8.4 %copy-start.7 = (bf16[2,2,128,1024]{3,2,1,0:T(8,128)(2,1)S(1)}, bf16[2,2,128,1024]{3,2,1,0:T(8,128)(2,1)}, u32[]{:S(2)}) copy-start(bf16[2,2,128,1024]{3,2,1,0:T(8,128)(2,1)} %copy-done.6) | copy-start | bytes 3145732
  74.2 21.5 %copy-start.2 = (bf16[1024,1024]{1,0:T(8,128)(2,1)S(1)}, bf16[1024,1024]{1,0:T(8,128)(2,1)}, u32[]{:S(2)}) copy-start(bf16[1024,1024]{1,0:T(8,128)(2,1)} %refs_5_.1) | copy-start | bytes 6291460
  91.2 12.7 %collective-permute-start.13 = (bf16[32,1152]{1,0:T(8,128)(2,1)S(1)}, bf16[32,1152]{1,0:T(8,128)(2,1)S(1)}, u32[]{:S(2)}, u32[]{:S(2)}) collective-permute-start(bf16[32,1152]{1,0:T(8,128)(2,1)S(1)} %register_merge.1.refs_7_.refs_0_), channel_id=1, source_target_pairs={{0,8},{8,16},{16,24},{24,0},{1,9},{9,17},{17,25},{25,1},{2,10},{10... | collective-permute-start | bytes 221192 | tf_op jit(solution)/shard_map/ppermute | solution.py:345
  91.9 12.1 %collective-permute-start.14 = (bf16[32,1152]{1,0:T(8,128)(2,1)S(1)}, bf16[32,1152]{1,0:T(8,128)(2,1)S(1)}, u32[]{:S(2)}, u32[]{:S(2)}) collective-permute-start(bf16[32,1152]{1,0:T(8,128)(2,1)S(1)} %register_merge.1.refs_7_.refs_0_), channel_id=1, source_target_pairs={{0,16},{8,24},{16,0},{24,8},{1,17},{9,25},{17,1},{25,9},{2,18},{10... | collective-permute-start | bytes 221192 | tf_op jit(solution)/shard_map/ppermute | solution.py:345
  93.4 10.6 %collective-permute-start.15 = (bf16[32,1152]{1,0:T(8,128)(2,1)S(1)}, bf16[32,1152]{1,0:T(8,128)(2,1)S(1)}, u32[]{:S(2)}, u32[]{:S(2)}) collective-permute-start(bf16[32,1152]{1,0:T(8,128)(2,1)S(1)} %register_merge.1.refs_7_.refs_0_), channel_id=1, source_target_pairs={{0,24},{8,0},{16,8},{24,16},{1,25},{9,1},{17,9},{25,17},{2,26},{10... | collective-permute-start | bytes 221192 | tf_op jit(solution)/shard_map/ppermute | solution.py:345
  95.8 8.3 %copy-start.3 = (bf16[1024,1024]{1,0:T(8,128)(2,1)S(1)}, bf16[1024,1024]{1,0:T(8,128)(2,1)}, u32[]{:S(2)}) copy-start(bf16[1024,1024]{1,0:T(8,128)(2,1)} %refs_6_.3) | copy-start | bytes 6291460
  104.9 8.6 %collective-permute-start.16 = (bf16[32,1024]{1,0:T(8,128)(2,1)S(1)}, bf16[32,1024]{1,0:T(8,128)(2,1)S(1)}, u32[]{:S(2)}, u32[]{:S(2)}) collective-permute-start(bf16[32,1024]{1,0:T(8,128)(2,1)S(1)} %register_out.1.refs_8_.refs_0_), channel_id=1, source_target_pairs={{0,1},{1,2},{2,3},{3,4},{4,5},{5,6},{6,7},{7,0},{8,9},{9,10},{10,1... | collective-permute-start | bytes 196616 | tf_op jit(solution)/shard_map/ppermute | solution.py:345
  106.7 8.5 %collective-permute-start.17 = (bf16[32,1024]{1,0:T(8,128)(2,1)S(1)}, bf16[32,1024]{1,0:T(8,128)(2,1)S(1)}, u32[]{:S(2)}, u32[]{:S(2)}) collective-permute-start(bf16[32,1024]{1,0:T(8,128)(2,1)S(1)} %register_out.1.refs_8_.refs_0_), channel_id=1, source_target_pairs={{0,2},{1,3},{2,4},{3,5},{4,6},{5,7},{6,0},{7,1},{8,10},{9,11},{10,... | collective-permute-start | bytes 196616 | tf_op jit(solution)/shard_map/ppermute | solution.py:345
  109.3 21.0 %collective-permute-start.18 = (bf16[32,1024]{1,0:T(8,128)(2,1)S(1)}, bf16[32,1024]{1,0:T(8,128)(2,1)S(1)}, u32[]{:S(2)}, u32[]{:S(2)}) collective-permute-start(bf16[32,1024]{1,0:T(8,128)(2,1)S(1)} %register_out.1.refs_8_.refs_0_), channel_id=1, source_target_pairs={{0,3},{1,4},{2,5},{3,6},{4,7},{5,0},{6,1},{7,2},{8,11},{9,12},{10,... | collective-permute-start | bytes 196616 | tf_op jit(solution)/shard_map/ppermute | solution.py:345
  109.3 21.0 %collective-permute-start.19 = (bf16[32,1024]{1,0:T(8,128)(2,1)S(1)}, bf16[32,1024]{1,0:T(8,128)(2,1)S(1)}, u32[]{:S(2)}, u32[]{:S(2)}) collective-permute-start(bf16[32,1024]{1,0:T(8,128)(2,1)S(1)} %register_out.1.refs_8_.refs_0_), channel_id=1, source_target_pairs={{0,4},{1,5},{2,6},{3,7},{4,0},{5,1},{6,2},{7,3},{8,12},{9,13},{10,... | collective-permute-start | bytes 196616 | tf_op jit(solution)/shard_map/ppermute | solution.py:345
  113.1 17.3 %collective-permute-start.20 = (bf16[32,1024]{1,0:T(8,128)(2,1)S(1)}, bf16[32,1024]{1,0:T(8,128)(2,1)S(1)}, u32[]{:S(2)}, u32[]{:S(2)}) collective-permute-start(bf16[32,1024]{1,0:T(8,128)(2,1)S(1)} %register_out.1.refs_8_.refs_0_), channel_id=1, source_target_pairs={{0,5},{1,6},{2,7},{3,0},{4,1},{5,2},{6,3},{7,4},{8,13},{9,14},{10,... | collective-permute-start | bytes 196616 | tf_op jit(solution)/shard_map/ppermute | solution.py:345
  113.5 16.9 %collective-permute-start.21 = (bf16[32,1024]{1,0:T(8,128)(2,1)S(1)}, bf16[32,1024]{1,0:T(8,128)(2,1)S(1)}, u32[]{:S(2)}, u32[]{:S(2)}) collective-permute-start(bf16[32,1024]{1,0:T(8,128)(2,1)S(1)} %register_out.1.refs_8_.refs_0_), channel_id=1, source_target_pairs={{0,6},{1,7},{2,0},{3,1},{4,2},{5,3},{6,4},{7,5},{8,14},{9,15},{10,... | collective-permute-start | bytes 196616 | tf_op jit(solution)/shard_map/ppermute | solution.py:345
  115.2 15.2 %collective-permute-start.22 = (bf16[32,1024]{1,0:T(8,128)(2,1)S(1)}, bf16[32,1024]{1,0:T(8,128)(2,1)S(1)}, u32[]{:S(2)}, u32[]{:S(2)}) collective-permute-start(bf16[32,1024]{1,0:T(8,128)(2,1)S(1)} %register_out.1.refs_8_.refs_0_), channel_id=1, source_target_pairs={{0,7},{1,0},{2,1},{3,2},{4,3},{5,4},{6,5},{7,6},{8,15},{9,8},{10,9... | collective-permute-start | bytes 196616 | tf_op jit(solution)/shard_map/ppermute | solution.py:345
  (5 other events, 9.8 us)

commit v3 on v2

--- a/solution.py
+++ b/solution.py
@@ -13,6 +13,7 @@
 LOG2E = 1.4426950408889634
 F32, BF16 = jnp.float32, jnp.bfloat16
 ANY = pl.BlockSpec(memory_space=pl.ANY)
+VMEM = pl.BlockSpec(memory_space=pltpu.VMEM)
 TOKEN = jax.ShapeDtypeStruct((8, 128), jnp.float32)
 
 
@@ -72,42 +73,53 @@
     return wide[:, :HEADS] + wide[:, HEADS : 2 * HEADS] + wide[:, 2 * HEADS : 3 * HEADS]
 
 
-def own_kernel(scale, head_width, slabs, slab_ref, *refs):
+def own_kernel(scale, head_width, core_ref, *refs):
     x_ref, reg_ref, wq_ref, wk_ref, wv_ref = refs[:5]
-    q_ref, kv_ref, reg_kv_ref = refs[5:8]
-    part_refs = refs[8 : 8 + slabs]
-    rows_ref, ctx_ref, level_ref = refs[8 + slabs :]
+    q_ref, kv_ref, reg_kv_ref, keep_ref, send_ref = refs[5:10]
+    rows_ref, ctx_ref, level_ref = refs[10:]
     step = pl.program_id(0)
     count, width = x_ref.shape
     regs = reg_ref.shape[0]
     blk, lanes = kv_ref.shape[2:]
+    each = lanes // head_width
 
     @pl.when(step == 0)
     def _():
         rows_ref[:count] = x_ref[...]
         rows_ref[count:] = reg_ref[...]
 
+    tile = pl.ds(pl.multiple_of(step * lanes, lanes), lanes)
     k = matmul(rows_ref[...], wk_ref[...]).astype(BF16)
     q_reg = (matmul(reg_ref[...], wq_ref[...]) * scale).astype(BF16)
-    pairs = [(h, h + 1) for h in range(0, lanes // head_width, 2)]
+    pairs = [(h, h + 1) for h in range(0, each, 2)]
 
     def score(pair):
-        return matmul_t(k[:count], spread_heads(q_reg, head_width, pair))
-
-    s = score(pairs[0])
+        quad = pair[0] // QUAD * QUAD
+        at = slice(quad * head_width, (quad + QUAD) * head_width)
+        return matmul_t(
+            k[:count, at], spread_heads(q_reg[:, at], head_width, [h - quad for h in pair])
+        )
+
+    outs, levels = [], []
+
+    def context(pair, p, peak, total):
+        at = slice(pair[0] * head_width, (pair[1] + 1) * head_width)
+        outs.extend(pair_context(v[:count, at], p, 1.0 / total, head_width))
+        level = peak + jnp.log2(total)
+        levels.extend([level[:, :regs], level[:, regs:]])
+
+    following, pending = score(pairs[0]), None
     v = matmul(rows_ref[...], wv_ref[...]).astype(BF16)
-    pending = None
-    outs, levels = [], []
     for n, pair in enumerate(pairs):
-        following = score(pairs[n + 1]) if n + 1 < len(pairs) else None
-        p, peak, total = soften(s)
-        at = slice(pair[0] * head_width, (pair[1] + 1) * head_width)
-        if n == 0:
+        s = following
+        if n + 1 < len(pairs):
+            following = score(pairs[n + 1])
+        else:
             q_ref[...] = (matmul(x_ref[...], wq_ref[...]) * scale).astype(BF16)
-        outs += pair_context(v[:count, at], p, 1.0 / total, head_width)
-        level = peak + jnp.log2(total)
-        levels += [level[:, :regs], level[:, regs:]]
-        s = following
+        if pending is not None:
+            context(*pending)
+        pending = (pair, *soften(s))
+    context(*pending)
     for n in range(kv_ref.shape[1]):
         kv_ref[0, n] = k[n * blk : (n + 1) * blk]
         kv_ref[1, n] = v[n * blk : (n + 1) * blk]
@@ -115,67 +127,54 @@
         kv_at = slice(count + n * blk, count + (n + 1) * blk)
         reg_kv_ref[0, n] = k[kv_at]
         reg_kv_ref[1, n] = v[kv_at]
-    out = jnp.concatenate(outs, axis=0).astype(BF16).T
-    level_block = jnp.concatenate(levels + [jnp.zeros((8 - len(levels), regs), F32)], axis=0)
-    for g in range(width // lanes):
-
-        @pl.when(step == g)
-        def _():
-            ctx_ref[:, g * lanes : (g + 1) * lanes] = out
-            level_ref[g] = level_block
+    ctx_ref[:, tile] = jnp.concatenate(outs, axis=0).astype(BF16).T
+    level_ref[step] = jnp.concatenate(levels, axis=0)
 
     @pl.when(step == width // lanes - 1)
     def _():
-        each = lanes // head_width
-        stacked = jnp.concatenate([level_ref[g][:each] for g in range(width // lanes)], axis=0)
+        stacked = jnp.concatenate([level_ref[g] for g in range(width // lanes)], axis=0)
         ctx_ref[:, width:] = pack_levels(stacked.T)
-        chunk = regs // slabs
-        for shift in range(slabs):
-            target = lax.rem(slab_ref[0] + shift, slabs)
-            part_refs[shift][...] = ctx_ref[pl.ds(pl.multiple_of(target * chunk, chunk), chunk)]
-
-
-def own_project(slab, rows, registers, w_query, w_key, w_value, slots, blk, head_width, slabs):
+        half = regs // 2
+        core = core_ref[0]
+        keep_ref[...] = ctx_ref[pl.ds(pl.multiple_of(core * half, half), half)]
+        send_ref[...] = ctx_ref[pl.ds(pl.multiple_of((1 - core) * half, half), half)]
+
+
+def own_project(core, rows, registers, w_query, w_key, w_value, slots, blk, head_width, lanes):
     count, width = rows.shape
     regs = registers.shape[0]
-    lanes = QUAD * head_width
-    chunk = regs // slabs
-    tile = pl.BlockSpec((width, lanes), lambda i, s: (0, i))
-    outs = pl.pallas_call(
-        functools.partial(own_kernel, head_width ** (-0.5) * LOG2E, head_width, slabs),
+    half = jax.ShapeDtypeStruct((regs // 2, width + 128), BF16)
+    return pl.pallas_call(
+        functools.partial(own_kernel, head_width ** (-0.5) * LOG2E, head_width),
         grid_spec=pltpu.PrefetchScalarGridSpec(
             num_scalar_prefetch=1,
             grid=(width // lanes,),
-            in_specs=[
-                pl.BlockSpec((count, width), lambda i, s: (0, 0)),
-                pl.BlockSpec((regs, width), lambda i, s: (0, 0)),
-                tile,
-                tile,
-                tile,
-            ],
+            in_specs=[pl.BlockSpec((count, width), lambda i, s: (0, 0)), pl.BlockSpec((regs, width), lambda i, s: (0, 0))]
+            + [pl.BlockSpec((width, lanes), lambda i, s: (0, i))] * 3,
             out_specs=[
                 pl.BlockSpec((count, lanes), lambda i, s: (0, i)),
                 pl.BlockSpec((2, count // blk, blk, lanes), lambda i, s: (0, 0, 0, i)),
                 pl.BlockSpec((2, regs // blk, blk, lanes), lambda i, s: (0, 0, 0, i)),
-            ]
-            + [pl.BlockSpec((chunk, width + 128), lambda i, s: (0, 0))] * slabs,
+                pl.BlockSpec(half.shape, lambda i, s: (0, 0)),
+                pl.BlockSpec(half.shape, lambda i, s: (0, 0)),
+            ],
             scratch_shapes=[
                 pltpu.VMEM((count + regs, width), BF16),
                 pltpu.VMEM((regs, width + 128), BF16),
-                pltpu.VMEM((width // lanes, 8, regs), F32),
+                pltpu.VMEM((width // lanes, lanes // head_width, regs), F32),
             ],
         ),
         out_shape=[
             jax.ShapeDtypeStruct((count, width), BF16),
-            jax.ShapeDtypeStruct((2, slots, blk, width), BF16),
+            pltpu.HBM((2, slots, blk, width), BF16),
             jax.ShapeDtypeStruct((2, regs // blk, blk, width), BF16),
-        ]
-        + [jax.ShapeDtypeStruct((chunk, width + 128), BF16)] * slabs,
-        compiler_params=params(48),
+            half,
+            half,
+        ],
+        compiler_params=params(52),
         cost_estimate=cost(),
         name="own_project",
-    )(slab, rows, registers, w_query, w_key, w_value)
-    return outs[0], outs[1], outs[2], outs[3:]
+    )(core, rows, registers, w_query, w_key, w_value)
 
 
 def halo_kernel(pieces, deps, *refs):
@@ -210,10 +209,10 @@
         grid=(width // lanes,),
         in_specs=[ANY] * len(pieces) + [tile, tile, ANY] + [ANY] * len(deps),
         out_specs=[pl.BlockSpec((2, rows // blk, blk, lanes), lambda i: (0, index, 0, i)), ANY],
-        out_shape=[jax.ShapeDtypeStruct(table.shape, BF16), TOKEN],
+        out_shape=[pltpu.HBM(table.shape, BF16), TOKEN],
         scratch_shapes=[pltpu.VMEM((rows, width), BF16), pltpu.SemaphoreType.DMA((len(pieces),))],
         input_output_aliases={len(pieces) + 2: 0},
-        compiler_params=params(40),
+        compiler_params=params(52),
         cost_estimate=cost(),
         name="halo_project",
     )(*pieces, w_key, w_value, table, *deps)
@@ -272,10 +271,7 @@
     in_specs = (
         [pl.BlockSpec((blk, width), lambda i, idx: (block(i), 0))]
         + [pl.BlockSpec((2, 1, blk, width), list_map(e)) for e in range(LIST)]
-        + [
-            pl.BlockSpec(reg_kv.shape, lambda i, idx: (0, 0, 0, 0)),
-            pl.BlockSpec((width, width), lambda i, idx: (0, 0)),
-        ]
+        + [VMEM, VMEM]
     )
     aliases = {}
     if previous is not None:
@@ -295,102 +291,91 @@
         ),
         out_shape=[jax.ShapeDtypeStruct((total, blk, width), BF16), TOKEN],
         input_output_aliases=aliases,
-        compiler_params=params(48),
+        compiler_params=params(52),
         cost_estimate=cost(),
         name="window_attend",
     )(*operands)
 
 
-def merged(refs, width):
-    levels = [unpack_levels(r[:, width:]) for r in refs]
-    top = functools.reduce(jnp.maximum, levels)
+def merged(flag, mine_ref, got_ref, width):
+    first = jnp.where(flag == 0, mine_ref[...], got_ref[...])
+    second = jnp.where(flag == 0, got_ref[...], mine_ref[...])
+    levels = [unpack_levels(x[:, width:]) for x in (first, second)]
+    top = jnp.maximum(*levels)
     weights = [jnp.exp2(level - top) for level in levels]
-    total = functools.reduce(jnp.add, weights)
-    inverse = 1.0 / total
-    weights = [w * inverse for w in weights]
-    rows = refs[0].shape[0]
+    total = weights[0] + weights[1]
+    weights = [w / total for w in weights]
+    rows = first.shape[0]
     head_width = width // HEADS
     lower = lax.broadcasted_iota(jnp.int32, (rows, 2 * head_width), 1) < head_width
     cols = []
     for pair in range(HEADS // 2):
         at = slice(pair * 2 * head_width, (pair + 1) * 2 * head_width)
-        mix = jnp.zeros((rows, 2 * head_width), F32)
-        for r, w in zip(refs, weights):
-            spread = jnp.where(lower, w[:, 2 * pair : 2 * pair + 1], w[:, 2 * pair + 1 : 2 * pair + 2])
-            mix = mix + r[:, at].astype(F32) * spread
+
+        def spread(w):
+            return jnp.where(lower, w[:, 2 * pair : 2 * pair + 1], w[:, 2 * pair + 1 : 2 * pair + 2])
+
+        mix = first[:, at].astype(F32) * spread(weights[0]) + second[:, at].astype(F32) * spread(weights[1])
         cols.append(mix.astype(BF16))
     return jnp.concatenate(cols, axis=1), top + jnp.log2(total)
 
 
-def vmem_call(body, out_shape, name, operands, deps):
-    vmem = pl.BlockSpec(memory_space=pltpu.VMEM)
-
+def small_call(body, out_shape, name, flag, operands, deps):
     def wrapped(*refs):
-        body(*refs[: len(operands)], *refs[len(operands) + len(deps) :])
+        body(*refs[: 1 + len(operands)], refs[-2])
 
     return pl.pallas_call(
         wrapped,
-        in_specs=[vmem] * len(operands) + [ANY] * len(deps),
-        out_specs=vmem,
-        out_shape=out_shape,
+        in_specs=[pl.BlockSpec(memory_space=pltpu.SMEM)] + [VMEM] * len(operands) + [ANY] * len(deps),
+        out_specs=[VMEM, ANY],
+        out_shape=[out_shape, TOKEN],
         compiler_params=params(16),
         cost_estimate=cost(),
         name=name,
-    )(*operands, *deps)
-
-
-def shift_all(parts, axis):
-    n = lax.axis_size(axis)
-    return [parts[0]] + [
-        lax.ppermute(parts[j], axis, [(i, (i + j) % n) for i in range(n)]) for j in range(1, n)
-    ]
-
-
-def merge_slab(parts, deps):
-    rows, wide = parts[0].shape
+    )(flag, *operands, *deps)
+
+
+def register_rounds(slab, keep, send, w_out):
+    half, wide = keep.shape
     width = wide - 128
-
-    def body(*refs):
-        mix, level = merged(refs[:-1], width)
-        refs[-1][:, :width] = mix
-        refs[-1][:, width:] = pack_levels(level)
-
-    return vmem_call(body, jax.ShapeDtypeStruct((rows, wide), BF16), "register_merge", parts, deps)
-
-
-def merge_phase(parts, w_out, deps):
-    rows, wide = parts[0].shape
-    width = wide - 128
-
-    def body(*refs):
-        mix, _ = merged(refs[:-2], width)
-        refs[-1][...] = matmul(mix, refs[-2][...]).astype(BF16)
-
-    return vmem_call(
-        body, jax.ShapeDtypeStruct((rows, width), BF16), "register_out", [*parts, w_out], deps
-    )
-
-
-def assemble(slab, parts, deps):
-    rows, width = parts[0].shape
-    slabs = len(parts)
-
-    def body(slab_ref, *refs):
-        out_ref = refs[-1]
-        for j in range(slabs):
-            source = lax.rem(slab_ref[0] + slabs - j, slabs)
-            out_ref[pl.ds(pl.multiple_of(source * rows, rows), rows)] = refs[j][...]
-
-    vmem = pl.BlockSpec(memory_space=pltpu.VMEM)
-    return pl.pallas_call(
-        body,
-        in_specs=[pl.BlockSpec(memory_space=pltpu.SMEM)] + [vmem] * slabs + [ANY] * len(deps),
-        out_specs=vmem,
-        out_shape=jax.ShapeDtypeStruct((rows * slabs, width), BF16),
-        compiler_params=params(16),
-        cost_estimate=cost(),
-        name="register_assemble",
-    )(slab, *parts, *deps)
+    slabs, phases = lax.axis_size("slab"), lax.axis_size("phase")
+    phase = lax.axis_index("phase").astype(jnp.int32)
+    turns = [("slab", slab, b) for b in range(slabs.bit_length() - 1)]
+    turns += [("phase", phase, b) for b in range(phases.bit_length() - 1)]
+
+    def swap(x, axis, bit):
+        return lax.ppermute(x, axis, [(i, i ^ (1 << bit)) for i in range(lax.axis_size(axis))])
+
+    def merge_body(flag_ref, mine_ref, got_ref, out_ref):
+        mix, level = merged(flag_ref[0], mine_ref, got_ref, width)
+        out_ref[:, :width] = mix
+        out_ref[:, width:] = pack_levels(level)
+
+    def last_body(flag_ref, mine_ref, got_ref, w_ref, out_ref):
+        mix, _ = merged(flag_ref[0], mine_ref, got_ref, width)
+        out_ref[...] = matmul(mix, w_ref[...]).astype(BF16)
+
+    def join_body(core_ref, mine_ref, got_ref, out_ref):
+        core = core_ref[0]
+        out_ref[pl.ds(pl.multiple_of(core * half, half), half)] = mine_ref[...]
+        out_ref[pl.ds(pl.multiple_of((1 - core) * half, half), half)] = got_ref[...]
+
+    mine, token = keep, None
+    for n, (axis, place, bit) in enumerate(turns):
+        got = swap(send if n == 0 else mine, axis, bit)
+        token = yield token
+        flag = ((place >> bit) & 1).reshape(1)
+        if n + 1 < len(turns):
+            shape = jax.ShapeDtypeStruct((half, wide), BF16)
+            mine, token = small_call(merge_body, shape, "register_merge", flag, [mine, got], [token])
+        else:
+            shape = jax.ShapeDtypeStruct((half, width), BF16)
+            mine, token = small_call(last_body, shape, "register_out", flag, [mine, got, w_out], [token])
+    got = swap(mine, "slab", 0)
+    token = yield token
+    shape = jax.ShapeDtypeStruct((2 * half, width), BF16)
+    out, _ = small_call(join_body, shape, "register_join", (slab & 1).reshape(1), [mine, got], [token])
+    yield out
 
 
 def shards(normed, block_list, registers, w_query, w_key, w_value, w_out):
@@ -435,8 +420,8 @@
     )
     slot_list = jnp.where(is_before | is_after, outer, inner).astype(jnp.int32).reshape(-1)
 
-    queries, table, reg_kv, parts = own_project(
-        slab.reshape(1),
+    queries, table, reg_kv, keep, send = own_project(
+        (slab & 1).reshape(1),
         normed.reshape(-1, width),
         registers,
         w_query,
@@ -445,43 +430,42 @@
         slots,
         blk,
         head_width,
-        slabs,
+        2 * lanes,
     )
-    parts = shift_all(parts, "slab")
-    table, _ = halo_project(table, [left, right], 1, w_key, w_value, lanes, [])
-    middle = own - 2 * slab_blocks
-    mixed, token = window_attend(
-        queries,
-        table,
-        reg_kv,
-        slot_list,
-        lambda i: i + slab_blocks,
-        middle,
-        w_out,
-        head_width,
-        None,
-        [before, after],
+    rounds = register_rounds(slab, keep, send, w_out)
+    next(rounds)
+    count = (slabs * phases).bit_length()
+
+    def window(table, start, mixed, deps):
+        return window_attend(
+            queries,
+            table,
+            reg_kv,
+            slot_list,
+            lambda i: start + i,
+            slab_blocks,
+            w_out,
+            head_width,
+            mixed,
+            deps,
+        )
+
+    table, token = halo_project(table, [left, right], 1, w_key, w_value, 2 * lanes, [])
+    token = rounds.send(token)
+    mixed, starts = None, [n * slab_blocks for n in range(own_phases)]
+    for n, start in enumerate(starts[1:-1]):
+        deps = [token, before, after] if n == 0 else [token]
+        mixed, token = window(table, start, mixed, deps)
+        token = rounds.send(token)
+    table, token = halo_project(
+        table, [before, after, corner_left, corner_right], 2, w_key, w_value, 2 * lanes, [token]
     )
-    one = merge_slab(parts, [token])
-    ones = shift_all([one] * phases, "phase")
-    table, token = halo_project(
-        table, [before, after, corner_left, corner_right], 2, w_key, w_value, lanes, [one]
-    )
-    share = merge_phase(ones, w_out, [token])
-    shares = shift_all([share] * slabs, "slab")
-    mixed, token = window_attend(
-        queries,
-        table,
-        reg_kv,
-        slot_list,
-        lambda i: i + jnp.where(i >= slab_blocks, middle, 0),
-        own - middle,
-        w_out,
-        head_width,
-        mixed,
-        [share],
-    )
-    register_out = assemble(slab.reshape(1), shares, [token])
+    token = rounds.send(token)
+    mixed, token = window(table, starts[0], mixed, [token])
+    for _ in range(count - own_phases - 1):
+        token = rounds.send(token)
+    mixed, token = window(table, starts[-1], mixed, [token])
+    register_out = rounds.send(token)
     return mixed.reshape(own_phases, slab_blocks, blk, width), register_out
 
 

time: 131 us -> 112 us (0.85)
  waiting for transfers between devices: 16.3 us -> 2.17 us
  starting transfers between devices: 34.8 us -> 21.5 us
  Pallas kernels: 69.9 us -> 80.8 us
  local copies, waits for them, and re-layouts: 7.55 us -> 4.41 us
    ppermute x17 -> x6, waiting for transfers between devices: 16.3 us -> 2.16 us  [swap(): lax.ppermute(x, axis, [(i, i ^ 1 << bit) for i in range(lax.axis_size(axi...]
    ppermute x17 -> x6, starting transfers between devices: 20.4 us -> 10 us  [swap(): lax.ppermute(x, axis, [(i, i ^ 1 << bit) for i in range(lax.axis_size(axi...]
    pallas_call x2 -> x4, Pallas kernels: 29.6 us -> 38.5 us  [window_attend(): pl.pallas_call(functools.partial(window_kernel, head_width), grid_spec=pl...]
    unnamed x28 -> x10, local copies, waits for them, and re-layouts: 3.51 us -> 0.02 us
    ppermute x6, starting transfers between devices: 14.4 us -> 11.5 us  [around(): lax.ppermute(x, axis, [(i, (i + step) % n) for i in range(n) if closed or...]
    pallas_call x3 -> x6, Pallas kernels: 3.6 us -> 5.29 us  [small_call(): pl.pallas_call(wrapped, in_specs=[pl.BlockSpec(memory_space=pltpu.SMEM)]...]
    squeeze x1, local copies, waits for them, and re-layouts: 1.5 us -> 3.18 us  [shards(): right = around(normed[:, 0], 'slab', -1, False)]
    pallas_call x2, Pallas kernels: 16.6 us -> 18.1 us  [halo_project(): pl.pallas_call(functools.partial(halo_kernel, len(pieces), len(deps)), gr...]
  transfers between devices with their start and end apart: 23 -> 12, of which waited for: 3 -> 1; matrix products, arithmetic and copies ran while one was open for 3% -> 3% of each run, Pallas kernels for 52% -> 70%
where the time goes in v3:
time: 112 us; the launch traced here: 111 us
  Pallas kernels  80.8 us (72%)
  starting transfers between devices  21.5 us (19%)
  local copies, waits for them, and re-layouts  4.41 us (4%)
  waiting for transfers between devices  2.17 us (2%)
  other arithmetic  1.71 us (2%)
    pallas_call x4, Pallas kernels, window_attend(): pl.pallas_call(functools.partial(window_kernel, head_width), grid_spec=pl...  38.5 us
    pallas_call x1, Pallas kernels, own_project(): pl.pallas_call(functools.partial(own_kernel, head_width ** (-0.5) * LOG2E...  18.9 us
    pallas_call x2, Pallas kernels, halo_project(): pl.pallas_call(functools.partial(halo_kernel, len(pieces), len(deps)), gr...  18.1 us
    ppermute x6, starting transfers between devices, around(): lax.ppermute(x, axis, [(i, (i + step) % n) for i in range(n) if closed or...  11.5 us
    ppermute x6, starting transfers between devices, swap(): lax.ppermute(x, axis, [(i, i ^ 1 << bit) for i in range(lax.axis_size(axi...  10 us
    pallas_call x6, Pallas kernels, small_call(): pl.pallas_call(wrapped, in_specs=[pl.BlockSpec(memory_space=pltpu.SMEM)]...  5.29 us
    squeeze x1, local copies, waits for them, and re-layouts, shards(): right = around(normed[:, 0], 'slab', -1, False)  3.18 us
  transfers between devices with their start and end apart: 12, of which 1 were waited for; matrix products, arithmetic and copies ran while one was open for 3% of the time, Pallas kernels for 70%

profile of v3, /device:TPU:0, one launch (start us, length us, event | category | flops | bytes accessed | tf_op | source)
XLA Modules:
  0.0 111.4 jit_solution(17271135491485601250)
XLA Ops:
  0.6 0.0 copy-start.3
  0.6 3.2 %slice_bitcast_fusion = (bf16[4,128,1024]{2,1,0:T(8,128)(2,1)}, bf16[4,128,1024]{2,1,0:T(8,128)(2,1)}) fusion(bf16[4,2,128,1024]{3,2,1,0:T(8,128)(2,1)} %param.7), kind=kLoop, calls=%fused_computation | loop fusion | bytes 4194304 | tf_op jit(solution)/shard_map/squeeze | solution.py:398
  3.8 1.4 %collective-permute-start.5 = (bf16[4,128,1024]{2,1,0:T(8,128)(2,1)}, bf16[4,128,1024]{2,1,0:T(8,128)(2,1)}, u32[]{:S(2)}, u32[]{:S(2)}) collective-permute-start(bf16[4,128,1024]{2,1,0:T(8,128)(2,1)} %get-tuple-element.58), channel_id=1, source_target_pairs={{1,0},{2,1},{3,2},{4,3},{5,4},{6,5},{7,6},{9,8},{10,9},{11,10},{12... | collective-permute-start | bytes 3145736 | tf_op jit(solution)/shard_map/ppermute | solution.py:391
  5.2 3.1 %collective-permute-start.4 = (bf16[4,128,1024]{2,1,0:T(8,128)(2,1)}, bf16[4,128,1024]{2,1,0:T(8,128)(2,1)S(1)}, u32[]{:S(2)}, u32[]{:S(2)}) collective-permute-start(bf16[4,128,1024]{2,1,0:T(8,128)(2,1)} %get-tuple-element.59), channel_id=1, source_target_pairs={{0,1},{1,2},{2,3},{3,4},{4,5},{5,6},{6,7},{8,9},{9,10},{10,11},{11... | collective-permute-start | bytes 3145736 | tf_op jit(solution)/shard_map/ppermute | solution.py:391
  8.4 1.1 slice_bitcast_fusion.2
  9.4 2.9 %collective-permute-start = (bf16[2,128,1024]{2,1,0:T(8,128)(2,1)}, bf16[2,128,1024]{2,1,0:T(8,128)(2,1)S(1)}, u32[]{:S(2)}, u32[]{:S(2)}) collective-permute-start(bf16[2,128,1024]{2,1,0:T(8,128)(2,1)} %get-tuple-element.61), channel_id=1, source_target_pairs={{0,8},{8,16},{16,24},{24,0},{1,9},{9,17},{17,25},{25,1},{2,10},{10... | collective-permute-start | bytes 1572872 | tf_op jit(solution)/shard_map/ppermute | solution.py:391
  12.4 1.0 collective-permute-start.1
  13.3 18.9 %own_project.1 = (bf16[1024,1024]{1,0:T(8,128)(2,1)}, bf16[2,24,128,1024]{3,2,1,0:T(8,128)(2,1)}, bf16[2,2,128,1024]{3,2,1,0:T(8,128)(2,1)}, bf16[128,1152]{1,0:T(8,128)(2,1)S(1)}, bf16[128,1152]{1,0:T(8,128)(2,1)S(1)}) custom-call(s32[1]{0:T(128)} %bitcast.core_ref.refs_0_, bf16[1024,1024]{1,0:T(8,128)(2,1)} %bitcast.27, bf16[256,1024]{1,0:T(8,128)(2,1)S(1)} %copy-done.2, ...), custom_call_target="tpu_custom_call" | custom-call | flops 1048576 | bytes 65536 | tf_op jit(solution)/shard_map/own_project/pallas_call | solution.py:147
  32.3 1.0 collective-permute-start.6
  33.4 0.1 reshape.50.idx_ref
  33.5 9.1 %halo_project.2 = (bf16[2,24,128,1024]{3,2,1,0:T(8,128)(2,1)}, f32[8,128]{1,0:T(8,128)S(1)}) custom-call(bf16[512,1024]{1,0:T(8,128)(2,1)S(1)} %bitcast.24, bf16[512,1024]{1,0:T(8,128)(2,1)} %bitcast.11.refs_1_, bf16[1024,1024]{1,0:T(8,128)(2,1)} %refs_4_.3, bf16[1024,1024]{1,0:T(8,128)(2,1)} %refs_5_.1, ...), custom_call_target="tpu_custom_call", output_to_operand_aliasing={{0}: (4, {})} | custom-call | flops 1048576 | bytes 65536 | tf_op jit(solution)/shard_map/halo_project/pallas_call | solution.py:207
  42.6 0.8 register_merge.4
  43.4 1.6 %collective-permute-start.7 = (bf16[128,1152]{1,0:T(8,128)(2,1)S(1)}, bf16[128,1152]{1,0:T(8,128)(2,1)S(1)}, u32[]{:S(2)}, u32[]{:S(2)}) collective-permute-start(bf16[128,1152]{1,0:T(8,128)(2,1)S(1)} %get-tuple-element.36.refs_1_), channel_id=1, source_target_pairs={{0,2},{1,3},{2,0},{3,1},{4,6},{5,7},{6,4},{7,5},{8,10},{9,11},{10,... | collective-permute-start | bytes 884744 | tf_op jit(solution)/shard_map/ppermute | solution.py:347
  45.1 0.8 pad_maximum_fusion
  45.9 1.8 %collective-permute-start.2 = (bf16[2,128,1024]{2,1,0:T(8,128)(2,1)}, bf16[2,128,1024]{2,1,0:T(8,128)(2,1)S(1)}, u32[]{:S(2)}, u32[]{:S(2)}) collective-permute-start(bf16[2,128,1024]{2,1,0:T(8,128)(2,1)} %pad_maximum_fusion), channel_id=1, source_target_pairs={{0,1},{1,2},{2,3},{3,4},{4,5},{5,6},{6,7},{8,9},{9,10},{10,11},{11... | collective-permute-start | bytes 1572872 | tf_op jit(solution)/shard_map/ppermute | solution.py:391
  47.8 9.7 %window_attend.4 = (bf16[8,128,1024]{2,1,0:T(8,128)(2,1)}, f32[8,128]{1,0:T(8,128)S(1)}) custom-call(s32[40]{0:T(128)S(1)} %reshape.50.idx_ref, bf16[1024,1024]{1,0:T(8,128)(2,1)} %get-tuple-element.30.q_ref, bf16[2,24,128,1024]{3,2,1,0:T(8,128)(2,1)} %get-tuple-element.32.refs_0_.refs_1_.refs_2_.refs_3_.refs_4_.refs_6_, ...), custom_call_target="tpu_custom_call" | custom-call | flops 1048576 | bytes 65536 | tf_op jit(solution)/shard_map/window_attend/pallas_call | solution.py:283
  57.5 0.8 register_merge.5
  58.3 3.4 %collective-permute-start.8 = (bf16[128,1152]{1,0:T(8,128)(2,1)S(1)}, bf16[128,1152]{1,0:T(8,128)(2,1)S(1)}, u32[]{:S(2)}, u32[]{:S(2)}) collective-permute-start(bf16[128,1152]{1,0:T(8,128)(2,1)S(1)} %get-tuple-element.40.refs_1_), channel_id=1, source_target_pairs={{0,4},{1,5},{2,6},{3,7},{4,0},{5,1},{6,2},{7,3},{8,12},{9,13},{10,... | collective-permute-start | bytes 884744 | tf_op jit(solution)/shard_map/ppermute | solution.py:347
  61.8 0.8 pad_maximum_fusion.1
  62.6 1.3 %collective-permute-start.3 = (bf16[2,128,1024]{2,1,0:T(8,128)(2,1)}, bf16[2,128,1024]{2,1,0:T(8,128)(2,1)}, u32[]{:S(2)}, u32[]{:S(2)}) collective-permute-start(bf16[2,128,1024]{2,1,0:T(8,128)(2,1)} %pad_maximum_fusion.1), channel_id=1, source_target_pairs={{1,0},{2,1},{3,2},{4,3},{5,4},{6,5},{7,6},{9,8},{10,9},{11,10},{12... | collective-permute-start | bytes 1572872 | tf_op jit(solution)/shard_map/ppermute | solution.py:391
  63.9 9.4 %window_attend.5 = (bf16[8,128,1024]{2,1,0:T(8,128)(2,1)}, f32[8,128]{1,0:T(8,128)S(1)}) custom-call(s32[40]{0:T(128)S(1)} %reshape.50.idx_ref, bf16[1024,1024]{1,0:T(8,128)(2,1)} %get-tuple-element.30.q_ref, bf16[2,24,128,1024]{3,2,1,0:T(8,128)(2,1)} %get-tuple-element.32.refs_0_.refs_1_.refs_2_.refs_3_.refs_4_.refs_6_, ...), custom_call_target="tpu_custom_call", output_to_operand_aliasing={{0}: (9, {})} | custom-call | flops 1048576 | bytes 65536 | tf_op jit(solution)/shard_map/window_attend/pallas_call | solution.py:283
  73.3 2.1 %collective-permute-done.8.refs_2_ = bf16[128,1152]{1,0:T(8,128)(2,1)S(1)} collective-permute-done((bf16[128,1152]{1,0:T(8,128)(2,1)S(1)}, bf16[128,1152]{1,0:T(8,128)(2,1)S(1)}, u32[]{:S(2)}, u32[]{:S(2)}) %collective-permute-start.8) | collective-permute-done | bytes 294944 | tf_op jit(solution)/shard_map/ppermute | solution.py:347
  75.4 0.8 register_merge.6
  76.2 0.7 collective-permute-start.9
  76.9 9.0 %halo_project.3 = (bf16[2,24,128,1024]{3,2,1,0:T(8,128)(2,1)}, f32[8,128]{1,0:T(8,128)S(1)}) custom-call(bf16[256,1024]{1,0:T(8,128)(2,1)S(1)} %bitcast.22, bf16[256,1024]{1,0:T(8,128)(2,1)S(1)} %bitcast.23, bf16[256,1024]{1,0:T(8,128)(2,1)S(1)} %bitcast.25, bf16[256,1024]{1,0:T(8,128)(2,1)} %bitcast.7.refs_3_, ...), custom_call_target="tpu_custom_call", output_to_operand_aliasing={{0}: (6, {})} | custom-call | flops 1048576 | bytes 65536 | tf_op jit(solution)/shard_map/halo_project/pallas_call | solution.py:207
  85.9 0.8 register_merge.7
  86.7 1.6 %collective-permute-start.10 = (bf16[128,1152]{1,0:T(8,128)(2,1)S(1)}, bf16[128,1152]{1,0:T(8,128)(2,1)S(1)}, u32[]{:S(2)}, u32[]{:S(2)}) collective-permute-start(bf16[128,1152]{1,0:T(8,128)(2,1)S(1)} %get-tuple-element.51.refs_1_), channel_id=1, source_target_pairs={{0,16},{8,24},{16,0},{24,8},{1,17},{9,25},{17,1},{25,9},{2,18},{10... | collective-permute-start | bytes 884744 | tf_op jit(solution)/shard_map/ppermute | solution.py:347
  88.3 10.0 %window_attend.6 = (bf16[8,128,1024]{2,1,0:T(8,128)(2,1)}, f32[8,128]{1,0:T(8,128)S(1)}) custom-call(s32[40]{0:T(128)S(1)} %reshape.50.idx_ref, bf16[1024,1024]{1,0:T(8,128)(2,1)} %get-tuple-element.30.q_ref, bf16[2,24,128,1024]{3,2,1,0:T(8,128)(2,1)} %get-tuple-element.45.refs_0_.refs_1_.refs_2_.refs_3_.refs_4_, ...), custom_call_target="tpu_custom_call", output_to_operand_aliasing={{0}: (9, {})} | custom-call | flops 1048576 | bytes 65536 | tf_op jit(solution)/shard_map/window_attend/pallas_call | solution.py:283
  98.3 1.2 %register_out.1 = (bf16[128,1024]{1,0:T(8,128)(2,1)S(1)}, f32[8,128]{1,0:T(8,128)S(1)}) custom-call(s32[1]{0:T(128)} %bitcast.16.refs_0_, bf16[128,1152]{1,0:T(8,128)(2,1)S(1)} %get-tuple-element.51.refs_1_, bf16[128,1152]{1,0:T(8,128)(2,1)S(1)} %collective-permute-done.10.refs_2_, bf16[1024,1024]{1,0:T(8,128)(2,1)S(1)} %copy-done, ...), custom_call_target="tpu_custom_call" | custom-call | flops 1048576 | bytes 65536 | tf_op jit(solution)/shard_map/register_out/pallas_call | solution.py:327
  99.6 1.7 %collective-permute-start.11 = (bf16[128,1024]{1,0:T(8,128)(2,1)S(1)}, bf16[128,1024]{1,0:T(8,128)(2,1)S(1)}, u32[]{:S(2)}, u32[]{:S(2)}) collective-permute-start(bf16[128,1024]{1,0:T(8,128)(2,1)S(1)} %get-tuple-element.55.refs_1_), channel_id=1, source_target_pairs={{0,1},{1,0},{2,3},{3,2},{4,5},{5,4},{6,7},{7,6},{8,9},{9,8},{10,11... | collective-permute-start | bytes 786440 | tf_op jit(solution)/shard_map/ppermute | solution.py:347
  101.2 9.4 %window_attend.7 = (bf16[8,128,1024]{2,1,0:T(8,128)(2,1)}, f32[8,128]{1,0:T(8,128)S(1)}) custom-call(s32[40]{0:T(128)S(1)} %reshape.50.idx_ref, bf16[1024,1024]{1,0:T(8,128)(2,1)} %get-tuple-element.30.q_ref, bf16[2,24,128,1024]{3,2,1,0:T(8,128)(2,1)} %get-tuple-element.45.refs_0_.refs_1_.refs_2_.refs_3_.refs_4_, ...), custom_call_target="tpu_custom_call", output_to_operand_aliasing={{0}: (9, {})} | custom-call | flops 1048576 | bytes 65536 | tf_op jit(solution)/shard_map/window_attend/pallas_call | solution.py:283
  110.6 0.8 register_join.1
  (23 shorter events, 0.2 us)
Async XLA Ops:
  0.6 7.7 %copy-start.3 = (bf16[4,2,128,1024]{3,2,1,0:T(8,128)(2,1)S(1)}, bf16[4,2,128,1024]{3,2,1,0:T(8,128)(2,1)}, u32[]{:S(2)}) copy-start(bf16[4,2,128,1024]{3,2,1,0:T(8,128)(2,1)} %param.7) | copy-start | bytes 6291460
  3.8 9.5 %copy-start.2 = (bf16[256,1024]{1,0:T(8,128)(2,1)S(1)}, bf16[256,1024]{1,0:T(8,128)(2,1)}, u32[]{:S(2)}) copy-start(bf16[256,1024]{1,0:T(8,128)(2,1)} %refs_1_.1) | copy-start | bytes 1572868
  3.8 29.7 %collective-permute-start.5 = (bf16[4,128,1024]{2,1,0:T(8,128)(2,1)}, bf16[4,128,1024]{2,1,0:T(8,128)(2,1)}, u32[]{:S(2)}, u32[]{:S(2)}) collective-permute-start(bf16[4,128,1024]{2,1,0:T(8,128)(2,1)} %get-tuple-element.58), channel_id=1, source_target_pairs={{1,0},{2,1},{3,2},{4,3},{5,4},{6,5},{7,6},{9,8},{10,9},{11,10},{12... | collective-permute-start | bytes 3145736 | tf_op jit(solution)/shard_map/ppermute | solution.py:391
  5.2 28.3 %collective-permute-start.4 = (bf16[4,128,1024]{2,1,0:T(8,128)(2,1)}, bf16[4,128,1024]{2,1,0:T(8,128)(2,1)S(1)}, u32[]{:S(2)}, u32[]{:S(2)}) collective-permute-start(bf16[4,128,1024]{2,1,0:T(8,128)(2,1)} %get-tuple-element.59), channel_id=1, source_target_pairs={{0,1},{1,2},{2,3},{3,4},{4,5},{5,6},{6,7},{8,9},{9,10},{10,11},{11... | collective-permute-start | bytes 3145736 | tf_op jit(solution)/shard_map/ppermute | solution.py:391
  9.4 24.0 %collective-permute-start = (bf16[2,128,1024]{2,1,0:T(8,128)(2,1)}, bf16[2,128,1024]{2,1,0:T(8,128)(2,1)S(1)}, u32[]{:S(2)}, u32[]{:S(2)}) collective-permute-start(bf16[2,128,1024]{2,1,0:T(8,128)(2,1)} %get-tuple-element.61), channel_id=1, source_target_pairs={{0,8},{8,16},{16,24},{24,0},{1,9},{9,17},{17,25},{25,1},{2,10},{10... | collective-permute-start | bytes 1572872 | tf_op jit(solution)/shard_map/ppermute | solution.py:391
  12.4 32.7 %collective-permute-start.1 = (bf16[2,128,1024]{2,1,0:T(8,128)(2,1)}, bf16[2,128,1024]{2,1,0:T(8,128)(2,1)S(1)}, u32[]{:S(2)}, u32[]{:S(2)}) collective-permute-start(bf16[2,128,1024]{2,1,0:T(8,128)(2,1)} %get-tuple-element.60), channel_id=1, source_target_pairs={{0,24},{8,0},{16,8},{24,16},{1,25},{9,1},{17,9},{25,17},{2,26},{10... | collective-permute-start | bytes 1572872 | tf_op jit(solution)/shard_map/ppermute | solution.py:391
  13.3 20.0 %copy-start.4 = (s32[4,2,5]{2,1,0:T(2,128)S(1)}, s32[4,2,5]{2,1,0:T(2,128)}, u32[]{:S(2)}) copy-start(s32[4,2,5]{2,1,0:T(2,128)} %param.8) | copy-start | bytes 484
  32.3 10.3 %collective-permute-start.6 = (bf16[128,1152]{1,0:T(8,128)(2,1)S(1)}, bf16[128,1152]{1,0:T(8,128)(2,1)S(1)}, u32[]{:S(2)}, u32[]{:S(2)}) collective-permute-start(bf16[128,1152]{1,0:T(8,128)(2,1)S(1)} %get-tuple-element.34), channel_id=1, source_target_pairs={{0,1},{1,0},{2,3},{3,2},{4,5},{5,4},{6,7},{7,6},{8,9},{9,8},{10,11... | collective-permute-start | bytes 884744 | tf_op jit(solution)/shard_map/ppermute | solution.py:347
  43.4 14.1 %collective-permute-start.7 = (bf16[128,1152]{1,0:T(8,128)(2,1)S(1)}, bf16[128,1152]{1,0:T(8,128)(2,1)S(1)}, u32[]{:S(2)}, u32[]{:S(2)}) collective-permute-start(bf16[128,1152]{1,0:T(8,128)(2,1)S(1)} %get-tuple-element.36.refs_1_), channel_id=1, source_target_pairs={{0,2},{1,3},{2,0},{3,1},{4,6},{5,7},{6,4},{7,5},{8,10},{9,11},{10,... | collective-permute-start | bytes 884744 | tf_op jit(solution)/shard_map/ppermute | solution.py:347
  45.9 31.0 %collective-permute-start.2 = (bf16[2,128,1024]{2,1,0:T(8,128)(2,1)}, bf16[2,128,1024]{2,1,0:T(8,128)(2,1)S(1)}, u32[]{:S(2)}, u32[]{:S(2)}) collective-permute-start(bf16[2,128,1024]{2,1,0:T(8,128)(2,1)} %pad_maximum_fusion), channel_id=1, source_target_pairs={{0,1},{1,2},{2,3},{3,4},{4,5},{5,6},{6,7},{8,9},{9,10},{10,11},{11... | collective-permute-start | bytes 1572872 | tf_op jit(solution)/shard_map/ppermute | solution.py:391
  57.5 6.4 %copy-start.1 = (bf16[2,2,128,1024]{3,2,1,0:T(8,128)(2,1)S(1)}, bf16[2,2,128,1024]{3,2,1,0:T(8,128)(2,1)}, u32[]{:S(2)}) copy-start(bf16[2,2,128,1024]{3,2,1,0:T(8,128)(2,1)} %get-tuple-element.37.refs_5_) | copy-start | bytes 3145732
  58.3 17.1 %collective-permute-start.8 = (bf16[128,1152]{1,0:T(8,128)(2,1)S(1)}, bf16[128,1152]{1,0:T(8,128)(2,1)S(1)}, u32[]{:S(2)}, u32[]{:S(2)}) collective-permute-start(bf16[128,1152]{1,0:T(8,128)(2,1)S(1)} %get-tuple-element.40.refs_1_), channel_id=1, source_target_pairs={{0,4},{1,5},{2,6},{3,7},{4,0},{5,1},{6,2},{7,3},{8,12},{9,13},{10,... | collective-permute-start | bytes 884744 | tf_op jit(solution)/shard_map/ppermute | solution.py:347
  62.6 14.3 %collective-permute-start.3 = (bf16[2,128,1024]{2,1,0:T(8,128)(2,1)}, bf16[2,128,1024]{2,1,0:T(8,128)(2,1)}, u32[]{:S(2)}, u32[]{:S(2)}) collective-permute-start(bf16[2,128,1024]{2,1,0:T(8,128)(2,1)} %pad_maximum_fusion.1), channel_id=1, source_target_pairs={{1,0},{2,1},{3,2},{4,3},{5,4},{6,5},{7,6},{9,8},{10,9},{11,10},{12... | collective-permute-start | bytes 1572872 | tf_op jit(solution)/shard_map/ppermute | solution.py:391
  76.2 9.7 %collective-permute-start.9 = (bf16[128,1152]{1,0:T(8,128)(2,1)S(1)}, bf16[128,1152]{1,0:T(8,128)(2,1)S(1)}, u32[]{:S(2)}, u32[]{:S(2)}) collective-permute-start(bf16[128,1152]{1,0:T(8,128)(2,1)S(1)} %get-tuple-element.47.refs_1_), channel_id=1, source_target_pairs={{0,8},{8,0},{16,24},{24,16},{1,9},{9,1},{17,25},{25,17},{2,10},{10... | collective-permute-start | bytes 884744 | tf_op jit(solution)/shard_map/ppermute | solution.py:347
  86.7 11.6 %collective-permute-start.10 = (bf16[128,1152]{1,0:T(8,128)(2,1)S(1)}, bf16[128,1152]{1,0:T(8,128)(2,1)S(1)}, u32[]{:S(2)}, u32[]{:S(2)}) collective-permute-start(bf16[128,1152]{1,0:T(8,128)(2,1)S(1)} %get-tuple-element.51.refs_1_), channel_id=1, source_target_pairs={{0,16},{8,24},{16,0},{24,8},{1,17},{9,25},{17,1},{25,9},{2,18},{10... | collective-permute-start | bytes 884744 | tf_op jit(solution)/shard_map/ppermute | solution.py:347
  88.3 10.0 %copy-start = (bf16[1024,1024]{1,0:T(8,128)(2,1)S(1)}, bf16[1024,1024]{1,0:T(8,128)(2,1)}, u32[]{:S(2)}) copy-start(bf16[1024,1024]{1,0:T(8,128)(2,1)} %refs_6_.7) | copy-start | bytes 6291460
  99.6 11.1 %collective-permute-start.11 = (bf16[128,1024]{1,0:T(8,128)(2,1)S(1)}, bf16[128,1024]{1,0:T(8,128)(2,1)S(1)}, u32[]{:S(2)}, u32[]{:S(2)}) collective-permute-start(bf16[128,1024]{1,0:T(8,128)(2,1)S(1)} %get-tuple-element.55.refs_1_), channel_id=1, source_target_pairs={{0,1},{1,0},{2,3},{3,2},{4,5},{5,4},{6,7},{7,6},{8,9},{9,8},{10,11... | collective-permute-start | bytes 786440 | tf_op jit(solution)/shard_map/ppermute | solution.py:347

commit v4 on v3

v4 whole, which is shorter than its diff:
```python
import functools

import jax
import jax.numpy as jnp
from jax import lax
from jax.experimental import pallas as pl
from jax.experimental.pallas import tpu as pltpu
from jax.sharding import PartitionSpec as P

HEADS = 16
LIST = 5
QUAD = 4
LOG2E = 1.4426950408889634
F32, BF16 = jnp.float32, jnp.bfloat16
ANY = pl.BlockSpec(memory_space=pl.ANY)
VMEM = pl.BlockSpec(memory_space=pltpu.VMEM)
TOKEN = jax.ShapeDtypeStruct((8, 128), jnp.float32)


def params(mib):
    return pltpu.CompilerParams(vmem_limit_bytes=mib << 20)


def cost():
    return pl.CostEstimate(flops=1 << 20, bytes_accessed=1 << 16, transcendentals=0)


def matmul(a, b):
    return jnp.dot(a, b, preferred_element_type=F32)


def matmul_t(a, b):
    return lax.dot_general(a, b, (((1,), (1,)), ((), ())), preferred_element_type=F32)


def t_matmul(a, b):
    return lax.dot_general(a, b, (((0,), (0,)), ((), ())), preferred_element_type=F32)


def spread_heads(q, head_width, heads):
    lane = lax.broadcasted_iota(jnp.int32, q.shape, 1) // head_width
    return jnp.concatenate([jnp.where(lane == h, q, jnp.zeros_like(q)) for h in heads], axis=0)


def soften(s):
    peak = jnp.max(s, axis=0, keepdims=True)
    p = jnp.exp2(s - peak)
    total = jnp.sum(p, axis=0, keepdims=True)
    return p.astype(BF16), peak, total


def pair_context(v, p, inverse, head_width):
    o = t_matmul(v, p)
    count = p.shape[1] // 2
    return [
        o[j * head_width : (j + 1) * head_width, j * count : (j + 1) * count]
        * inverse[:, j * count : (j + 1) * count]
        for j in range(2)
    ]


def pack_levels(level):
    hi = level.astype(BF16)
    rest = level - hi.astype(F32)
    mid = rest.astype(BF16)
    low = (rest - mid.astype(F32)).astype(BF16)
    pad = jnp.zeros((level.shape[0], 128 - 3 * level.shape[1]), BF16)
    return jnp.concatenate([hi, mid, low, pad], axis=1)


def unpack_levels(cols):
    wide = cols.astype(F32)
    return wide[:, :HEADS] + wide[:, HEADS : 2 * HEADS] + wide[:, 2 * HEADS : 3 * HEADS]


def own_kernel(scale, head_width, core_ref, *refs):
    x_ref, reg_ref, wq_ref, wk_ref, wv_ref = refs[:5]
    kv_ref, reg_kv_ref, keep_ref, send_ref, rows_ref, ctx_ref, level_ref = refs[-7:]
    step = pl.program_id(0)
    count, width = x_ref.shape
    regs = reg_ref.shape[0]
    blk, lanes = kv_ref.shape[2:]
    each = lanes // head_width

    @pl.when(step == 0)
    def _():
        rows_ref[:count] = x_ref[...]
        rows_ref[count:] = reg_ref[...]

    tile = pl.ds(pl.multiple_of(step * lanes, lanes), lanes)
    k = matmul(rows_ref[...], wk_ref[...]).astype(BF16)
    q_reg = (matmul(reg_ref[...], wq_ref[...]) * scale).astype(BF16)
    pairs = [(h, h + 1) for h in range(0, each, 2)]

    def score(pair):
        quad = pair[0] // QUAD * QUAD
        at = slice(quad * head_width, (quad + QUAD) * head_width)
        return matmul_t(
            k[:count, at], spread_heads(q_reg[:, at], head_width, [h - quad for h in pair])
        )

    outs, levels = [], []

    def context(pair, p, peak, total):
        at = slice(pair[0] * head_width, (pair[1] + 1) * head_width)
        outs.extend(pair_context(v[:count, at], p, 1.0 / total, head_width))
        level = peak + jnp.log2(total)
        levels.extend([level[:, :regs], level[:, regs:]])

    following, pending = score(pairs[0]), None
    v = matmul(rows_ref[...], wv_ref[...]).astype(BF16)
    for n, pair in enumerate(pairs):
        s = following
        if n + 1 < len(pairs):
            following = score(pairs[n + 1])
        if pending is not None:
            context(*pending)
        pending = (pair, *soften(s))
    context(*pending)
    for n in range(kv_ref.shape[1]):
        kv_ref[0, n] = k[n * blk : (n + 1) * blk]
        kv_ref[1, n] = v[n * blk : (n + 1) * blk]
    for n in range(reg_kv_ref.shape[1]):
        kv_at = slice(count + n * blk, count + (n + 1) * blk)
        reg_kv_ref[0, n] = k[kv_at]
        reg_kv_ref[1, n] = v[kv_at]
    ctx_ref[:, tile] = jnp.concatenate(outs, axis=0).astype(BF16).T
    level_ref[step] = jnp.concatenate(levels, axis=0)

    @pl.when(step == width // lanes - 1)
    def _():
        stacked = jnp.concatenate([level_ref[g] for g in range(width // lanes)], axis=0)
        ctx_ref[:, width:] = pack_levels(stacked.T)
        half = regs // 2
        core = core_ref[0]
        keep_ref[...] = ctx_ref[pl.ds(pl.multiple_of(core * half, half), half)]
        send_ref[...] = ctx_ref[pl.ds(pl.multiple_of((1 - core) * half, half), half)]


def own_project(core, rows, registers, w_query, w_key, w_value, slots, blk, head_width, lanes, scale, deps):
    count, width = rows.shape
    regs = registers.shape[0]
    half = jax.ShapeDtypeStruct((regs // 2, width + 128), BF16)
    return pl.pallas_call(
        functools.partial(own_kernel, scale, head_width),
        grid_spec=pltpu.PrefetchScalarGridSpec(
            num_scalar_prefetch=1,
            grid=(width // lanes,),
            in_specs=[pl.BlockSpec((count, width), lambda i, s: (0, 0)), pl.BlockSpec((regs, width), lambda i, s: (0, 0))]
            + [pl.BlockSpec((width, lanes), lambda i, s: (0, i))] * 3
            + [ANY] * len(deps),
            out_specs=[
                pl.BlockSpec((2, count // blk, blk, lanes), lambda i, s: (0, 0, 0, i)),
                pl.BlockSpec((2, regs // blk, blk, lanes), lambda i, s: (0, 0, 0, i)),
                pl.BlockSpec(half.shape, lambda i, s: (0, 0)),
                pl.BlockSpec(half.shape, lambda i, s: (0, 0)),
            ],
            scratch_shapes=[
                pltpu.VMEM((count + regs, width), BF16),
                pltpu.VMEM((regs, width + 128), BF16),
                pltpu.VMEM((width // lanes, lanes // head_width, regs), F32),
            ],
        ),
        out_shape=[
            pltpu.HBM((2, slots, blk, width), BF16),
            jax.ShapeDtypeStruct((2, regs // blk, blk, width), BF16),
            half,
            half,
        ],
        compiler_params=params(52),
        cost_estimate=cost(),
        name="own_project",
    )(core, rows, registers, w_query, w_key, w_value, *deps)


def attend_kernel(head_width, start, loaded, pieces, skipped, idx_ref, *refs):
    refs = iter(refs)

    def take(count):
        return [next(refs) for _ in range(count)]

    q_ref, reg_ref = take(2)
    xs, w_refs = take(pieces), take(2 if pieces else 0)
    table_ref, wo_ref = take(2)
    take(skipped)
    (new_table_ref,) = take(1) if pieces else (None,)
    o_ref, _ = take(2)
    tabs = take(2)
    ctx_ref, wo_scratch, in_sems, wo_sem = take(4)
    if pieces:
        rows_ref, x_sems, out_sems = take(3)
    step, last = pl.program_id(0), pl.num_programs(0) - 1
    buf = lax.rem(step, 2)
    slots, blk, lanes = tabs[0].shape[1:]
    blocks = o_ref.shape[0]

    def columns(g):
        return pl.ds(pl.multiple_of(g * lanes, lanes), lanes)

    def bring(g, b):
        return [
            pltpu.make_async_copy(
                table_ref.at[side, pl.ds(0, loaded), :, columns(g)],
                tabs[side].at[b, pl.ds(0, loaded)],
                in_sems.at[side, b],
            )
            for side in range(2)
        ]

    def give(g, b):
        return [
            pltpu.make_async_copy(
                tabs[side].at[b, pl.ds(loaded, slots - loaded)],
                new_table_ref.at[side, pl.ds(loaded, slots - loaded), :, columns(g)],
                out_sems.at[side, b],
            )
            for side in range(2)
        ]

    def output_weight():
        return pltpu.make_async_copy(wo_ref, wo_scratch, wo_sem.at[0])

    @pl.when(step == 0)
    def _():
        copies, at = [], 0
        for n, x in enumerate(xs):
            copies.append(pltpu.make_async_copy(x, rows_ref.at[pl.ds(at, x.shape[0])], x_sems.at[n]))
            at += x.shape[0]
        for c in copies + bring(0, 0):
            c.start()
        output_weight().start()
        for c in copies:
            c.wait()

    @pl.when(step < last)
    def _():
        for c in bring(step + 1, 1 - buf):
            c.start()

    if pieces:

        @pl.when(step >= 2)
        def _():
            for c in give(step - 2, buf):
                c.wait()

    def project(side):
        if pieces:
            new = matmul(rows_ref[...], w_refs[side][...]).astype(BF16)
            for n in range(slots - loaded):
                tabs[side][buf, loaded + n] = new[n * blk : (n + 1) * blk]

    project(0)
    for c in bring(step, buf):
        c.wait()

    def gathered(side, block, at):
        listed = [idx_ref[(start + block) * LIST + e] for e in range(LIST)]
        return jnp.concatenate(
            [tabs[side][buf, slot, :, at] for slot in listed]
            + [reg_ref[side, n, :, at] for n in range(reg_ref.shape[1])],
            axis=0,
        )

    everything = slice(0, lanes)

    def score(block):
        q = q_ref[block * blk : (block + 1) * blk]
        return matmul_t(gathered(0, block, everything), spread_heads(q, head_width, range(QUAD)))

    def context(block, p, inverse):
        outs = []
        for h in range(0, QUAD, 2):
            at = slice(h * blk, (h + 2) * blk)
            v = gathered(1, block, slice(h * head_width, (h + 2) * head_width))
            outs += pair_context(v, p[:, at], inverse[:, at], head_width)
        ctx_ref[block * blk : (block + 1) * blk, columns(step)] = (
            jnp.concatenate(outs, axis=0).astype(BF16).T
        )

    following, pending = score(0), None
    project(1)
    for block in range(blocks):
        s = following
        if block + 1 < blocks:
            following = score(block + 1)
        if pending is not None:
            context(*pending)
        p, _, total = soften(s)
        pending = (block, p, 1.0 / total)
    context(*pending)
    if pieces:
        for c in give(step, buf):
            c.start()

    @pl.when(step == last)
    def _():
        output_weight().wait()
        out = matmul(ctx_ref[...], wo_scratch[...]).astype(BF16)
        for block in range(blocks):
            o_ref[block] = out[block * blk : (block + 1) * blk]
        if pieces:
            for c in give(step - 1, 1 - buf) + give(step, buf):
                c.wait()


def attend(
    queries, table, reg_kv, slot_list, start, blocks, loaded, pieces, w_key, w_value, w_out, head_width, previous, deps
):
    _, all_slots, blk, width = table.shape
    lanes = QUAD * head_width
    rows = blocks * blk
    pieces = [x.reshape(-1, width) for x in pieces]
    new_rows = sum(x.shape[0] for x in pieces)
    slots = loaded + new_rows // blk
    assert start % blocks == 0 and width // lanes >= 2
    operands = [slot_list, queries, reg_kv, *pieces]
    in_specs = [
        pl.BlockSpec((rows, lanes), lambda i, idx: (start // blocks, i)),
        pl.BlockSpec((*reg_kv.shape[:3], lanes), lambda i, idx: (0, 0, 0, i)),
    ] + [ANY] * len(pieces)
    if pieces:
        operands += [w_key, w_value]
        in_specs += [pl.BlockSpec((width, lanes), lambda i, idx: (0, i))] * 2
    aliases, out_specs, out_shape = {}, [], []
    if pieces:
        aliases[len(operands)] = 0
        out_specs.append(pl.BlockSpec(memory_space=pltpu.HBM))
        out_shape.append(pltpu.HBM(table.shape, BF16))
    operands += [table, w_out]
    in_specs += [pl.BlockSpec(memory_space=pltpu.HBM), ANY]
    if previous is not None:
        aliases[len(operands)] = len(out_specs)
        operands.append(previous)
        in_specs.append(ANY)
    operands += deps
    in_specs += [ANY] * len(deps)
    skipped = len(deps) + (previous is not None)
    out_specs += [pl.BlockSpec((blocks, blk, width), lambda i, idx: (start // blocks, 0, 0)), ANY]
    out_shape += [jax.ShapeDtypeStruct((queries.shape[0] // blk, blk, width), BF16), TOKEN]
    tab = pltpu.VMEM((2, slots, blk, lanes), BF16)
    sems = pltpu.SemaphoreType.DMA
    scratch = [tab, tab, pltpu.VMEM((rows, width), BF16), pltpu.VMEM((width, width), BF16), sems((2, 2)), sems((1,))]
    if pieces:
        scratch += [pltpu.VMEM((new_rows, width), BF16), sems((len(pieces),)), sems((2, 2))]
    out = pl.pallas_call(
        functools.partial(attend_kernel, head_width, start, loaded, len(pieces), skipped),
        grid_spec=pltpu.PrefetchScalarGridSpec(
            num_scalar_prefetch=1,
            grid=(width // lanes,),
            in_specs=in_specs,
            out_specs=out_specs,
            scratch_shapes=scratch,
        ),
        out_shape=out_shape,
        input_output_aliases=aliases,
        compiler_params=params(52),
        cost_estimate=cost(),
        name="attend",
    )(*operands)
    return out if pieces else [table, *out]


def tree(values):
    while len(values) > 1:
        values = [values[n] + values[n + 1] for n in range(0, len(values), 2)]
    return values[0]


def merged(place, refs, all_ref, width):
    for n, r in enumerate(refs):
        all_ref[place ^ n] = r[...]
    count, rows, _ = all_ref.shape
    levels = [unpack_levels(all_ref[n, :, width:]) for n in range(count)]
    top = functools.reduce(jnp.maximum, levels)
    weights = [jnp.exp2(level - top) for level in levels]
    total = tree(weights)
    weights = [w / total for w in weights]
    head_width = width // HEADS
    lower = lax.broadcasted_iota(jnp.int32, (rows, 2 * head_width), 1) < head_width
    cols = []
    for pair in range(HEADS // 2):
        at = slice(pair * 2 * head_width, (pair + 1) * 2 * head_width)

        def spread(w):
            return jnp.where(lower, w[:, 2 * pair : 2 * pair + 1], w[:, 2 * pair + 1 : 2 * pair + 2])

        mix = tree([all_ref[n, :, at].astype(F32) * spread(weights[n]) for n in range(count)])
        cols.append(mix.astype(BF16))
    return jnp.concatenate(cols, axis=1), top + jnp.log2(total)


def small_call(body, out_shape, scratch, name, flag, operands, deps):
    def wrapped(*refs):
        ins, outs = refs[: 1 + len(operands)], refs[1 + len(operands) + len(deps) :]
        body(*ins, outs[0], *outs[2:])

    return pl.pallas_call(
        wrapped,
        in_specs=[pl.BlockSpec(memory_space=pltpu.SMEM)] + [VMEM] * len(operands) + [ANY] * len(deps),
        out_specs=[VMEM, ANY],
        out_shape=[out_shape, TOKEN],
        scratch_shapes=scratch,
        compiler_params=params(16),
        cost_estimate=cost(),
        name=name,
    )(flag, *operands, *deps)


def register_rounds(slab, keep, send, w_out):
    half, wide = keep.shape
    width = wide - 128
    slabs, phases = lax.axis_size("slab"), lax.axis_size("phase")
    phase = lax.axis_index("phase").astype(jnp.int32)
    turns = [("slab", slab & 1, 0, 2), ("slab", slab >> 1, 1, slabs // 2)]
    turns += [("phase", phase, 0, phases)]

    def swap(x, axis, bit, n):
        return lax.ppermute(x, axis, [(i, i ^ (n << bit)) for i in range(lax.axis_size(axis))])

    def merge_body(place_ref, *refs):
        mix, level = merged(place_ref[0], refs[:-2], refs[-1], width)
        refs[-2][:, :width] = mix
        refs[-2][:, width:] = pack_levels(level)

    def last_body(place_ref, *refs):
        mix, _ = merged(place_ref[0], refs[:-3], refs[-1], width)
        refs[-2][...] = matmul(mix, refs[-3][...]).astype(BF16)

    def join_body(core_ref, mine_ref, got_ref, out_ref):
        core = core_ref[0]
        out_ref[pl.ds(pl.multiple_of(core * half, half), half)] = mine_ref[...]
        out_ref[pl.ds(pl.multiple_of((1 - core) * half, half), half)] = got_ref[...]

    mine, token = keep, None
    for n, (axis, place, bit, size) in enumerate(turns):
        got = [swap(send if n == 0 else mine, axis, bit, j) for j in range(1, size)]
        deps = yield token
        scratch = [pltpu.VMEM((size, half, wide), BF16)]
        place = place.reshape(1)
        if n + 1 < len(turns):
            shape = jax.ShapeDtypeStruct((half, wide), BF16)
            mine, token = small_call(merge_body, shape, scratch, "register_merge", place, [mine, *got], deps)
        else:
            shape = jax.ShapeDtypeStruct((half, width), BF16)
            mine, token = small_call(
                last_body, shape, scratch, "register_out", place, [mine, *got, w_out], deps
            )
    got = swap(mine, "slab", 0, 1)
    deps = yield token
    shape = jax.ShapeDtypeStruct((2 * half, width), BF16)
    out, _ = small_call(join_body, shape, [], "register_join", (slab & 1).reshape(1), [mine, got], deps)
    yield out


def shards(normed, block_list, registers, w_query, w_key, w_value, w_out):
    own_phases, slab_blocks, blk, width = normed.shape
    head_width = width // HEADS
    lanes = QUAD * head_width
    phases, slabs = lax.axis_size("phase"), lax.axis_size("slab")
    own = own_phases * slab_blocks
    slab = lax.axis_index("slab").astype(jnp.int32)
    scale = head_width ** (-0.5) * LOG2E

    def around(x, axis, step, closed):
        n = lax.axis_size(axis)
        return lax.ppermute(
            x, axis, [(i, (i + step) % n) for i in range(n) if closed or 0 <= i + step < n]
        )

    before = around(normed[-1], "phase", 1, True)
    after = around(normed[0], "phase", -1, True)
    left = around(normed[:, -1], "slab", 1, False)
    right = around(normed[:, 0], "slab", -1, False)
    corner_left = around(jnp.stack([before[-1], after[-1]]), "slab", 1, False)
    corner_right = around(jnp.stack([before[0], after[0]]), "slab", -1, False)

    at_left = own
    at_right = at_left + own_phases
    at_before = at_right + own_phases
    at_after = at_before + slab_blocks
    at_corner = at_after + slab_blocks
    slots = at_corner + 4
    assert own == at_before - at_left == slots - at_before

    total_phases, depth_blocks = own_phases * phases, slab_blocks * slabs
    p = (block_list // depth_blocks - lax.axis_index("phase") * own_phases + 1) % total_phases - 1
    z = block_list % depth_blocks - slab * slab_blocks
    is_left, is_right = z < 0, z >= slab_blocks
    is_before, is_after = p < 0, p >= own_phases
    inner = jnp.where(is_left, at_left + p, jnp.where(is_right, at_right + p, p * slab_blocks + z))
    outer = jnp.where(
        is_left | is_right,
        at_corner + jnp.where(is_right, 2, 0) + jnp.where(is_after, 1, 0),
        jnp.where(is_after, at_after, at_before) + z,
    )
    slot_list = jnp.where(is_before | is_after, outer, inner).astype(jnp.int32).reshape(-1)

    rows = normed.reshape(-1, width)
    queries = (matmul(rows, w_query) * scale).astype(BF16)
    table, reg_kv, keep, send = own_project(
        (slab & 1).reshape(1),
        rows,
        registers,
        w_query,
        w_key,
        w_value,
        slots,
        blk,
        head_width,
        2 * lanes,
        scale,
        [queries],
    )
    rounds = register_rounds(slab, keep, send, w_out)
    next(rounds)

    def windows(table, phase, loaded, pieces, mixed, deps):
        return attend(
            queries,
            table,
            reg_kv,
            slot_list,
            phase * slab_blocks,
            slab_blocks,
            loaded,
            pieces,
            w_key,
            w_value,
            w_out,
            head_width,
            mixed,
            deps,
        )

    order = [*range(1, own_phases - 1), 0, own_phases - 1]
    assert len(order) == 4
    mixed, deps = None, []
    for n, at in enumerate(order):
        pieces, loaded = [], at_before if n < 3 else slots
        if n == 0:
            pieces, loaded = [left, right], at_left
        if n == 1:
            deps = [*deps, before, after]
        if n == 2:
            pieces = [before, after, corner_left, corner_right]
        table, mixed, token = windows(table, at, loaded, pieces, mixed, deps)
        token = rounds.send([token])
        deps = [token]
    return mixed.reshape(own_phases, slab_blocks, blk, width), token


def solution(mesh):
    placed = (P("phase", "slab", None, None), P("phase", "slab", None), P(), P(), P(), P(), P())
    return jax.shard_map(
        shards,
        mesh=mesh,
        in_specs=placed,
        out_specs=(P("phase", "slab", None, None), P()),
        check_vma=False,
    )
```

time: 112 us -> 131 us (1.17)
  the two profiles are of different devices: /device:TPU:0 before, /device:TPU:11 now
where the time goes in v4:
time: 131 us
  Pallas kernels  84.5 us (65%)
  starting transfers between devices  18.3 us (14%)
  waiting for transfers between devices  17.8 us (14%)
  local copies, waits for them, and re-layouts  4.22 us (3%)
  matrix products  3.66 us (3%)
  other arithmetic  1.71 us (1%)
    pallas_call x4, Pallas kernels, attend(): pl.pallas_call(functools.partial(attend_kernel, head_width, start, loaded...  62.7 us
    pallas_call x1, Pallas kernels, own_project(): pl.pallas_call(functools.partial(own_kernel, scale, head_width), grid_spe...  16.7 us
    ppermute x6, starting transfers between devices, around(): lax.ppermute(x, axis, [(i, (i + step) % n) for i in range(n) if closed or...  12.8 us
    ppermute x8, waiting for transfers between devices, swap(): lax.ppermute(x, axis, [(i, i ^ n << bit) for i in range(lax.axis_size(axi...  12.8 us
    ppermute x8, starting transfers between devices, swap(): lax.ppermute(x, axis, [(i, i ^ n << bit) for i in range(lax.axis_size(axi...  5.5 us
    pallas_call x4, Pallas kernels, small_call(): pl.pallas_call(wrapped, in_specs=[pl.BlockSpec(memory_space=pltpu.SMEM)]...  5.18 us
    ppermute x6, waiting for transfers between devices, around(): lax.ppermute(x, axis, [(i, (i + step) % n) for i in range(n) if closed or...  5.02 us
    dot_general x1, matrix products, matmul(): return jnp.dot(a, b, preferred_element_type=F32)  3.66 us
  transfers between devices with their start and end apart: 14, of which 4 were waited for; matrix products, arithmetic and copies ran while one was open for 5% of the time, Pallas kernels for 62%

profile of v4, /device:TPU:11, one launch (start us, length us, event | category | flops | bytes accessed | tf_op | source)
XLA Modules:
  0.0 131.1 jit_solution(17264480217548738281)
XLA Ops:
  0.6 3.2 %slice_bitcast_fusion = (bf16[4,128,1024]{2,1,0:T(8,128)(2,1)}, bf16[4,128,1024]{2,1,0:T(8,128)(2,1)}) fusion(bf16[4,2,128,1024]{3,2,1,0:T(8,128)(2,1)} %param.7), kind=kLoop, calls=%fused_computation.1 | loop fusion | bytes 4194304 | tf_op jit(solution)/shard_map/squeeze | solution.py:474
  3.8 2.7 %collective-permute-start.5 = (bf16[4,128,1024]{2,1,0:T(8,128)(2,1)}, bf16[4,128,1024]{2,1,0:T(8,128)(2,1)}, u32[]{:S(2)}, u32[]{:S(2)}) collective-permute-start(bf16[4,128,1024]{2,1,0:T(8,128)(2,1)} %get-tuple-element.44), channel_id=1, source_target_pairs={{1,0},{2,1},{3,2},{4,3},{5,4},{6,5},{7,6},{9,8},{10,9},{11,10},{12... | collective-permute-start | bytes 3145736 | tf_op jit(solution)/shard_map/ppermute | solution.py:467
  6.5 3.1 %collective-permute-start.4 = (bf16[4,128,1024]{2,1,0:T(8,128)(2,1)}, bf16[4,128,1024]{2,1,0:T(8,128)(2,1)}, u32[]{:S(2)}, u32[]{:S(2)}) collective-permute-start(bf16[4,128,1024]{2,1,0:T(8,128)(2,1)} %get-tuple-element.45), channel_id=1, source_target_pairs={{0,1},{1,2},{2,3},{3,4},{4,5},{5,6},{6,7},{8,9},{9,10},{10,11},{11... | collective-permute-start | bytes 3145736 | tf_op jit(solution)/shard_map/ppermute | solution.py:467
  9.7 0.9 slice_bitcast_fusion.2
  10.5 1.2 collective-permute-start
  11.7 0.3 collective-permute-start.1
  12.0 3.7 %multiply_convert_fusion.refs_5_.refs_0_ = bf16[1024,1024]{1,0:T(8,128)(2,1)} fusion(bf16[1024,1024]{1,0:T(8,128)(2,1)S(1)} %bitcast.26, bf16[1024,1024]{1,0:T(8,128)(2,1)S(1)} %copy-done.5), kind=kOutput, calls=%fused_computation | convolution fusion | flops 2149580800 | bytes 6291456 | tf_op jit(solution)/shard_map/dot_general | solution.py:29
  15.7 16.7 %own_project.1 = (bf16[2,24,128,1024]{3,2,1,0:T(8,128)(2,1)}, bf16[2,2,128,1024]{3,2,1,0:T(8,128)(2,1)}, bf16[128,1152]{1,0:T(8,128)(2,1)S(1)}, bf16[128,1152]{1,0:T(8,128)(2,1)S(1)}) custom-call(s32[1]{0:T(128)} %bitcast.1.core_ref.refs_0_, bf16[1024,1024]{1,0:T(8,128)(2,1)} %bitcast.25, bf16[256,1024]{1,0:T(8,128)(2,1)S(1)} %copy-done.3, ...), custom_call_target="tpu_custom_call" | custom-call | flops 1048576 | bytes 65536 | tf_op jit(solution)/shard_map/own_project/pallas_call | solution.py:144
  32.4 0.1 reshape.42.idx_ref
  32.5 3.7 %collective-permute-done.1.refs_7_ = bf16[2,128,1024]{2,1,0:T(8,128)(2,1)S(1)} collective-permute-done((bf16[2,128,1024]{2,1,0:T(8,128)(2,1)}, bf16[2,128,1024]{2,1,0:T(8,128)(2,1)S(1)}, u32[]{:S(2)}, u32[]{:S(2)}) %collective-permute-start.1) | collective-permute-done | bytes 524320 | tf_op jit(solution)/shard_map/ppermute | solution.py:467
  36.2 0.8 pad_maximum_fusion
  37.1 3.7 %collective-permute-start.2 = (bf16[2,128,1024]{2,1,0:T(8,128)(2,1)}, bf16[2,128,1024]{2,1,0:T(8,128)(2,1)S(1)}, u32[]{:S(2)}, u32[]{:S(2)}) collective-permute-start(bf16[2,128,1024]{2,1,0:T(8,128)(2,1)} %pad_maximum_fusion), channel_id=1, source_target_pairs={{0,1},{1,2},{2,3},{3,4},{4,5},{5,6},{6,7},{8,9},{9,10},{10,11},{11... | collective-permute-start | bytes 1572872 | tf_op jit(solution)/shard_map/ppermute | solution.py:467
  40.8 20.2 %attend.4 = (bf16[2,24,128,1024]{3,2,1,0:T(8,128)(2,1)}, bf16[8,128,1024]{2,1,0:T(8,128)(2,1)}, f32[8,128]{1,0:T(8,128)S(1)}) custom-call(s32[40]{0:T(128)S(1)} %reshape.42.idx_ref, bf16[1024,1024]{1,0:T(8,128)(2,1)} %multiply_convert_fusion.refs_5_.refs_0_, bf16[2,2,128,1024]{3,2,1,0:T(8,128)(2,1)S(1)} %copy-done.1, ...), custom_call_target="tpu_custom_call", output_to_operand_aliasing={{0}: (7, {})} | custom-call | flops 1048576 | bytes 65536 | tf_op jit(solution)/shard_map/attend/pallas_call | solution.py:346
  61.0 0.9 register_merge.2
  61.9 0.2 collective-permute-start.7
  62.1 1.9 %collective-permute-start.8 = (bf16[128,1152]{1,0:T(8,128)(2,1)S(1)}, bf16[128,1152]{1,0:T(8,128)(2,1)S(1)}, u32[]{:S(2)}, u32[]{:S(2)}) collective-permute-start(bf16[128,1152]{1,0:T(8,128)(2,1)S(1)} %get-tuple-element.32.refs_1_), channel_id=1, source_target_pairs={{0,4},{1,5},{2,6},{3,7},{4,0},{5,1},{6,2},{7,3},{8,12},{9,13},{10,... | collective-permute-start | bytes 884744 | tf_op jit(solution)/shard_map/ppermute | solution.py:419
  64.0 0.6 collective-permute-start.9
  64.6 0.8 pad_maximum_fusion.1
  65.4 1.9 %collective-permute-start.3 = (bf16[2,128,1024]{2,1,0:T(8,128)(2,1)}, bf16[2,128,1024]{2,1,0:T(8,128)(2,1)}, u32[]{:S(2)}, u32[]{:S(2)}) collective-permute-start(bf16[2,128,1024]{2,1,0:T(8,128)(2,1)} %pad_maximum_fusion.1), channel_id=1, source_target_pairs={{1,0},{2,1},{3,2},{4,3},{5,4},{6,5},{7,6},{9,8},{10,9},{11,10},{12... | collective-permute-start | bytes 1572872 | tf_op jit(solution)/shard_map/ppermute | solution.py:467
  67.3 10.8 %attend.5 = (bf16[8,128,1024]{2,1,0:T(8,128)(2,1)}, f32[8,128]{1,0:T(8,128)S(1)}) custom-call(s32[40]{0:T(128)S(1)} %reshape.42.idx_ref, bf16[1024,1024]{1,0:T(8,128)(2,1)} %multiply_convert_fusion.refs_5_.refs_0_, bf16[2,2,128,1024]{3,2,1,0:T(8,128)(2,1)} %get-tuple-element.23.refs_1_, ...), custom_call_target="tpu_custom_call", output_to_operand_aliasing={{0}: (5, {})} | custom-call | flops 1048576 | bytes 65536 | tf_op jit(solution)/shard_map/attend/pallas_call | solution.py:346
  78.2 5.3 %collective-permute-done.8.refs_3_ = bf16[128,1152]{1,0:T(8,128)(2,1)S(1)} collective-permute-done((bf16[128,1152]{1,0:T(8,128)(2,1)S(1)}, bf16[128,1152]{1,0:T(8,128)(2,1)S(1)}, u32[]{:S(2)}, u32[]{:S(2)}) %collective-permute-start.8) | collective-permute-done | bytes 294944 | tf_op jit(solution)/shard_map/ppermute | solution.py:419
  83.5 7.4 %collective-permute-done.9.refs_4_ = bf16[128,1152]{1,0:T(8,128)(2,1)S(1)} collective-permute-done((bf16[128,1152]{1,0:T(8,128)(2,1)S(1)}, bf16[128,1152]{1,0:T(8,128)(2,1)S(1)}, u32[]{:S(2)}, u32[]{:S(2)}) %collective-permute-start.9) | collective-permute-done | bytes 294944 | tf_op jit(solution)/shard_map/ppermute | solution.py:419
  90.9 1.6 %register_merge.3 = (bf16[128,1152]{1,0:T(8,128)(2,1)S(1)}, f32[8,128]{1,0:T(8,128)S(1)}) custom-call(s32[1]{0:T(128)} %bitcast.12.refs_0_, bf16[128,1152]{1,0:T(8,128)(2,1)S(1)} %get-tuple-element.32.refs_1_, bf16[128,1152]{1,0:T(8,128)(2,1)S(1)} %collective-permute-done.7.refs_2_, bf16[128,1152]{1,0:T(8,128)(2,1)S(1)} %collective-permute-done.8.refs_3_, ...), custom_call_target="tpu_custom_call" | custom-call | flops 1048576 | bytes 65536 | tf_op jit(solution)/shard_map/register_merge/pallas_call | solution.py:398
  92.5 0.3 collective-permute-start.10
  92.8 0.2 collective-permute-start.11
  93.0 2.2 %collective-permute-start.12 = (bf16[128,1152]{1,0:T(8,128)(2,1)S(1)}, bf16[128,1152]{1,0:T(8,128)(2,1)S(1)}, u32[]{:S(2)}, u32[]{:S(2)}) collective-permute-start(bf16[128,1152]{1,0:T(8,128)(2,1)S(1)} %get-tuple-element.37.refs_1_), channel_id=1, source_target_pairs={{0,24},{8,16},{16,8},{24,0},{1,25},{9,17},{17,9},{25,1},{2,26},{10... | collective-permute-start | bytes 884744 | tf_op jit(solution)/shard_map/ppermute | solution.py:419
  95.2 1.3 %collective-permute-done.3 = bf16[2,128,1024]{2,1,0:T(8,128)(2,1)} collective-permute-done((bf16[2,128,1024]{2,1,0:T(8,128)(2,1)}, bf16[2,128,1024]{2,1,0:T(8,128)(2,1)}, u32[]{:S(2)}, u32[]{:S(2)}) %collective-permute-start.3) | collective-permute-done | bytes 524320 | tf_op jit(solution)/shard_map/ppermute | solution.py:467
  96.5 20.2 %attend.6 = (bf16[2,24,128,1024]{3,2,1,0:T(8,128)(2,1)}, bf16[8,128,1024]{2,1,0:T(8,128)(2,1)}, f32[8,128]{1,0:T(8,128)S(1)}) custom-call(s32[40]{0:T(128)S(1)} %reshape.42.idx_ref, bf16[1024,1024]{1,0:T(8,128)(2,1)} %multiply_convert_fusion.refs_5_.refs_0_, ...), custom_call_target="tpu_custom_call", output_to_operand_aliasing={{0}: (9, {}), {1}: (11, {})} | custom-call | flops 1048576 | bytes 65536 | tf_op jit(solution)/shard_map/attend/pallas_call | solution.py:346
  116.7 1.9 %register_out.1 = (bf16[128,1024]{1,0:T(8,128)(2,1)S(1)}, f32[8,128]{1,0:T(8,128)S(1)}) custom-call(s32[1]{0:T(128)} %bitcast.13.refs_0_, bf16[128,1152]{1,0:T(8,128)(2,1)S(1)} %get-tuple-element.37.refs_1_, bf16[128,1152]{1,0:T(8,128)(2,1)S(1)} %collective-permute-done.10.refs_2_, bf16[128,1152]{1,0:T(8,128)(2,1)S(1)} %collective-permute-done.11.refs_3_, ...), custom_call_target="tpu_custom_call" | custom-call | flops 1048576 | bytes 65536 | tf_op jit(solution)/shard_map/register_out/pallas_call | solution.py:398
  118.7 0.1 collective-permute-start.13
  118.8 11.5 %attend.7 = (bf16[8,128,1024]{2,1,0:T(8,128)(2,1)}, f32[8,128]{1,0:T(8,128)S(1)}) custom-call(s32[40]{0:T(128)S(1)} %reshape.42.idx_ref, bf16[1024,1024]{1,0:T(8,128)(2,1)} %multiply_convert_fusion.refs_5_.refs_0_, bf16[2,2,128,1024]{3,2,1,0:T(8,128)(2,1)S(1)} %copy-done.2, ...), custom_call_target="tpu_custom_call", output_to_operand_aliasing={{0}: (5, {})} | custom-call | flops 1048576 | bytes 65536 | tf_op jit(solution)/shard_map/attend/pallas_call | solution.py:346
  130.3 0.8 register_join.1
  (28 shorter events, 0.2 us)
Async XLA Ops:
  0.6 9.0 %copy-start.4 = (bf16[4,2,128,1024]{3,2,1,0:T(8,128)(2,1)S(1)}, bf16[4,2,128,1024]{3,2,1,0:T(8,128)(2,1)}, u32[]{:S(2)}) copy-start(bf16[4,2,128,1024]{3,2,1,0:T(8,128)(2,1)} %param.7) | copy-start | bytes 6291460
  3.8 8.2 %copy-start.5 = (bf16[1024,1024]{1,0:T(8,128)(2,1)S(1)}, bf16[1024,1024]{1,0:T(8,128)(2,1)}, u32[]{:S(2)}) copy-start(bf16[1024,1024]{1,0:T(8,128)(2,1)} %refs_2_.1) | copy-start | bytes 6291460
  3.8 36.9 %collective-permute-start.5 = (bf16[4,128,1024]{2,1,0:T(8,128)(2,1)}, bf16[4,128,1024]{2,1,0:T(8,128)(2,1)}, u32[]{:S(2)}, u32[]{:S(2)}) collective-permute-start(bf16[4,128,1024]{2,1,0:T(8,128)(2,1)} %get-tuple-element.44), channel_id=1, source_target_pairs={{1,0},{2,1},{3,2},{4,3},{5,4},{6,5},{7,6},{9,8},{10,9},{11,10},{12... | collective-permute-start | bytes 3145736 | tf_op jit(solution)/shard_map/ppermute | solution.py:467
  6.5 34.2 %collective-permute-start.4 = (bf16[4,128,1024]{2,1,0:T(8,128)(2,1)}, bf16[4,128,1024]{2,1,0:T(8,128)(2,1)}, u32[]{:S(2)}, u32[]{:S(2)}) collective-permute-start(bf16[4,128,1024]{2,1,0:T(8,128)(2,1)} %get-tuple-element.45), channel_id=1, source_target_pairs={{0,1},{1,2},{2,3},{3,4},{4,5},{5,6},{6,7},{8,9},{9,10},{10,11},{11... | collective-permute-start | bytes 3145736 | tf_op jit(solution)/shard_map/ppermute | solution.py:467
  10.5 22.0 %collective-permute-start = (bf16[2,128,1024]{2,1,0:T(8,128)(2,1)S(1)}, bf16[2,128,1024]{2,1,0:T(8,128)(2,1)S(1)}, u32[]{:S(2)}, u32[]{:S(2)}) collective-permute-start(bf16[2,128,1024]{2,1,0:T(8,128)(2,1)S(1)} %get-tuple-element.47), channel_id=1, source_target_pairs={{0,8},{8,16},{16,24},{24,0},{1,9},{9,17},{17,25},{25,1},{2,10},{10... | collective-permute-start | bytes 1572872 | tf_op jit(solution)/shard_map/ppermute | solution.py:467
  11.7 24.5 %collective-permute-start.1 = (bf16[2,128,1024]{2,1,0:T(8,128)(2,1)}, bf16[2,128,1024]{2,1,0:T(8,128)(2,1)S(1)}, u32[]{:S(2)}, u32[]{:S(2)}) collective-permute-start(bf16[2,128,1024]{2,1,0:T(8,128)(2,1)} %get-tuple-element.46), channel_id=1, source_target_pairs={{0,24},{8,0},{16,8},{24,16},{1,25},{9,1},{17,9},{25,17},{2,26},{10... | collective-permute-start | bytes 1572872 | tf_op jit(solution)/shard_map/ppermute | solution.py:467
  12.0 3.7 %copy-start.3 = (bf16[256,1024]{1,0:T(8,128)(2,1)S(1)}, bf16[256,1024]{1,0:T(8,128)(2,1)}, u32[]{:S(2)}) copy-start(bf16[256,1024]{1,0:T(8,128)(2,1)} %refs_1_.1) | copy-start | bytes 1572868
  15.6 16.7 %copy-start.6 = (s32[4,2,5]{2,1,0:T(2,128)S(1)}, s32[4,2,5]{2,1,0:T(2,128)}, u32[]{:S(2)}) copy-start(s32[4,2,5]{2,1,0:T(2,128)} %param.8) | copy-start | bytes 484
  32.3 8.5 %copy-start.1 = (bf16[2,2,128,1024]{3,2,1,0:T(8,128)(2,1)S(1)}, bf16[2,2,128,1024]{3,2,1,0:T(8,128)(2,1)}, u32[]{:S(2)}) copy-start(bf16[2,2,128,1024]{3,2,1,0:T(8,128)(2,1)} %get-tuple-element.23.refs_1_) | copy-start | bytes 3145732
  32.3 28.7 %collective-permute-start.6 = (bf16[128,1152]{1,0:T(8,128)(2,1)S(1)}, bf16[128,1152]{1,0:T(8,128)(2,1)S(1)}, u32[]{:S(2)}, u32[]{:S(2)}) collective-permute-start(bf16[128,1152]{1,0:T(8,128)(2,1)S(1)} %get-tuple-element.28), channel_id=1, source_target_pairs={{0,1},{1,0},{2,3},{3,2},{4,5},{5,4},{6,7},{7,6},{8,9},{9,8},{10,11... | collective-permute-start | bytes 884744 | tf_op jit(solution)/shard_map/ppermute | solution.py:419
  37.1 58.1 %collective-permute-start.2 = (bf16[2,128,1024]{2,1,0:T(8,128)(2,1)}, bf16[2,128,1024]{2,1,0:T(8,128)(2,1)S(1)}, u32[]{:S(2)}, u32[]{:S(2)}) collective-permute-start(bf16[2,128,1024]{2,1,0:T(8,128)(2,1)} %pad_maximum_fusion), channel_id=1, source_target_pairs={{0,1},{1,2},{2,3},{3,4},{4,5},{5,6},{6,7},{8,9},{9,10},{10,11},{11... | collective-permute-start | bytes 1572872 | tf_op jit(solution)/shard_map/ppermute | solution.py:467
  61.9 16.3 %collective-permute-start.7 = (bf16[128,1152]{1,0:T(8,128)(2,1)S(1)}, bf16[128,1152]{1,0:T(8,128)(2,1)S(1)}, u32[]{:S(2)}, u32[]{:S(2)}) collective-permute-start(bf16[128,1152]{1,0:T(8,128)(2,1)S(1)} %get-tuple-element.32.refs_1_), channel_id=1, source_target_pairs={{0,2},{1,3},{2,0},{3,1},{4,6},{5,7},{6,4},{7,5},{8,10},{9,11},{10,... | collective-permute-start | bytes 884744 | tf_op jit(solution)/shard_map/ppermute | solution.py:419
  62.1 21.3 %collective-permute-start.8 = (bf16[128,1152]{1,0:T(8,128)(2,1)S(1)}, bf16[128,1152]{1,0:T(8,128)(2,1)S(1)}, u32[]{:S(2)}, u32[]{:S(2)}) collective-permute-start(bf16[128,1152]{1,0:T(8,128)(2,1)S(1)} %get-tuple-element.32.refs_1_), channel_id=1, source_target_pairs={{0,4},{1,5},{2,6},{3,7},{4,0},{5,1},{6,2},{7,3},{8,12},{9,13},{10,... | collective-permute-start | bytes 884744 | tf_op jit(solution)/shard_map/ppermute | solution.py:419
  64.0 26.9 %collective-permute-start.9 = (bf16[128,1152]{1,0:T(8,128)(2,1)S(1)}, bf16[128,1152]{1,0:T(8,128)(2,1)S(1)}, u32[]{:S(2)}, u32[]{:S(2)}) collective-permute-start(bf16[128,1152]{1,0:T(8,128)(2,1)S(1)} %get-tuple-element.32.refs_1_), channel_id=1, source_target_pairs={{0,6},{1,7},{2,4},{3,5},{4,2},{5,3},{6,0},{7,1},{8,14},{9,15},{10,... | collective-permute-start | bytes 884744 | tf_op jit(solution)/shard_map/ppermute | solution.py:419
  65.4 31.1 %collective-permute-start.3 = (bf16[2,128,1024]{2,1,0:T(8,128)(2,1)}, bf16[2,128,1024]{2,1,0:T(8,128)(2,1)}, u32[]{:S(2)}, u32[]{:S(2)}) collective-permute-start(bf16[2,128,1024]{2,1,0:T(8,128)(2,1)} %pad_maximum_fusion.1), channel_id=1, source_target_pairs={{1,0},{2,1},{3,2},{4,3},{5,4},{6,5},{7,6},{9,8},{10,9},{11,10},{12... | collective-permute-start | bytes 1572872 | tf_op jit(solution)/shard_map/ppermute | solution.py:467
  92.5 24.2 %collective-permute-start.10 = (bf16[128,1152]{1,0:T(8,128)(2,1)S(1)}, bf16[128,1152]{1,0:T(8,128)(2,1)S(1)}, u32[]{:S(2)}, u32[]{:S(2)}) collective-permute-start(bf16[128,1152]{1,0:T(8,128)(2,1)S(1)} %get-tuple-element.37.refs_1_), channel_id=1, source_target_pairs={{0,8},{8,0},{16,24},{24,16},{1,9},{9,1},{17,25},{25,17},{2,10},{10... | collective-permute-start | bytes 884744 | tf_op jit(solution)/shard_map/ppermute | solution.py:419
  92.8 23.9 %collective-permute-start.11 = (bf16[128,1152]{1,0:T(8,128)(2,1)S(1)}, bf16[128,1152]{1,0:T(8,128)(2,1)S(1)}, u32[]{:S(2)}, u32[]{:S(2)}) collective-permute-start(bf16[128,1152]{1,0:T(8,128)(2,1)S(1)} %get-tuple-element.37.refs_1_), channel_id=1, source_target_pairs={{0,16},{8,24},{16,0},{24,8},{1,17},{9,25},{17,1},{25,9},{2,18},{10... | collective-permute-start | bytes 884744 | tf_op jit(solution)/shard_map/ppermute | solution.py:419
  93.0 23.7 %collective-permute-start.12 = (bf16[128,1152]{1,0:T(8,128)(2,1)S(1)}, bf16[128,1152]{1,0:T(8,128)(2,1)S(1)}, u32[]{:S(2)}, u32[]{:S(2)}) collective-permute-start(bf16[128,1152]{1,0:T(8,128)(2,1)S(1)} %get-tuple-element.37.refs_1_), channel_id=1, source_target_pairs={{0,24},{8,16},{16,8},{24,0},{1,25},{9,17},{17,9},{25,1},{2,26},{10... | collective-permute-start | bytes 884744 | tf_op jit(solution)/shard_map/ppermute | solution.py:419
  96.5 20.2 %copy-start = (bf16[1024,1024]{1,0:T(8,128)(2,1)S(1)}, bf16[1024,1024]{1,0:T(8,128)(2,1)}, u32[]{:S(2)}) copy-start(bf16[1024,1024]{1,0:T(8,128)(2,1)} %refs_3_.5) | copy-start | bytes 6291460
  116.7 2.1 %copy-start.2 = (bf16[2,2,128,1024]{3,2,1,0:T(8,128)(2,1)S(1)}, bf16[2,2,128,1024]{3,2,1,0:T(8,128)(2,1)}, u32[]{:S(2)}) copy-start(bf16[2,2,128,1024]{3,2,1,0:T(8,128)(2,1)} %get-tuple-element.23.refs_1_) | copy-start | bytes 3145732
  118.7 11.6 %collective-permute-start.13 = (bf16[128,1024]{1,0:T(8,128)(2,1)S(1)}, bf16[128,1024]{1,0:T(8,128)(2,1)S(1)}, u32[]{:S(2)}, u32[]{:S(2)}) collective-permute-start(bf16[128,1024]{1,0:T(8,128)(2,1)S(1)} %get-tuple-element.41.refs_1_), channel_id=1, source_target_pairs={{0,1},{1,0},{2,3},{3,2},{4,5},{5,4},{6,7},{7,6},{8,9},{9,8},{10,11... | collective-permute-start | bytes 786440 | tf_op jit(solution)/shard_map/ppermute | solution.py:419

commit v5 on v4

--- a/solution.py
+++ b/solution.py
@@ -10,6 +10,7 @@
 HEADS = 16
 LIST = 5
 QUAD = 4
+TILE_QUADS = 2
 LOG2E = 1.4426950408889634
 F32, BF16 = jnp.float32, jnp.bfloat16
 ANY = pl.BlockSpec(memory_space=pl.ANY)
@@ -75,7 +76,7 @@
 
 def own_kernel(scale, head_width, core_ref, *refs):
     x_ref, reg_ref, wq_ref, wk_ref, wv_ref = refs[:5]
-    kv_ref, reg_kv_ref, keep_ref, send_ref, rows_ref, ctx_ref, level_ref = refs[-7:]
+    kv_ref, reg_kv_ref, keep_ref, send_ref, _, rows_ref, ctx_ref, level_ref = refs[-8:]
     step = pl.program_id(0)
     count, width = x_ref.shape
     regs = reg_ref.shape[0]
@@ -154,6 +155,7 @@
                 pl.BlockSpec((2, regs // blk, blk, lanes), lambda i, s: (0, 0, 0, i)),
                 pl.BlockSpec(half.shape, lambda i, s: (0, 0)),
                 pl.BlockSpec(half.shape, lambda i, s: (0, 0)),
+                ANY,
             ],
             scratch_shapes=[
                 pltpu.VMEM((count + regs, width), BF16),
@@ -166,6 +168,7 @@
             jax.ShapeDtypeStruct((2, regs // blk, blk, width), BF16),
             half,
             half,
+            TOKEN,
         ],
         compiler_params=params(52),
         cost_estimate=cost(),
@@ -173,26 +176,50 @@
     )(core, rows, registers, w_query, w_key, w_value, *deps)
 
 
-def attend_kernel(head_width, start, loaded, pieces, skipped, idx_ref, *refs):
+def query_kernel(scale, x_ref, w_ref, *refs):
+    refs[-2][...] = (matmul(x_ref[...], w_ref[...]) * scale).astype(BF16)
+
+
+def query_project(rows, w_query, lanes, scale, deps):
+    count, width = rows.shape
+    return pl.pallas_call(
+        functools.partial(query_kernel, scale),
+        grid=(width // lanes,),
+        in_specs=[
+            pl.BlockSpec((count, width), lambda i: (0, 0)),
+            pl.BlockSpec((width, lanes), lambda i: (0, i)),
+        ]
+        + [ANY] * len(deps),
+        out_specs=[pl.BlockSpec((count, lanes), lambda i: (0, i)), ANY],
+        out_shape=[jax.ShapeDtypeStruct((count, width), BF16), TOKEN],
+        compiler_params=params(52),
+        cost_estimate=cost(),
+        name="query_project",
+    )(rows, w_query, *deps)
+
+
+def attend_kernel(head_width, phases, loaded, pieces, skipped, idx_ref, *refs):
     refs = iter(refs)
 
     def take(count):
         return [next(refs) for _ in range(count)]
 
-    q_ref, reg_ref = take(2)
+    q_refs = take(len(phases))
+    (reg_ref,) = take(1)
     xs, w_refs = take(pieces), take(2 if pieces else 0)
     table_ref, wo_ref = take(2)
     take(skipped)
     (new_table_ref,) = take(1) if pieces else (None,)
     o_ref, _ = take(2)
     tabs = take(2)
-    ctx_ref, wo_scratch, in_sems, wo_sem = take(4)
+    ctx_ref, wo_scratch, in_sems, wo_sem, o_sems = take(5)
     if pieces:
         rows_ref, x_sems, out_sems = take(3)
     step, last = pl.program_id(0), pl.num_programs(0) - 1
     buf = lax.rem(step, 2)
     slots, blk, lanes = tabs[0].shape[1:]
-    blocks = o_ref.shape[0]
+    each = q_refs[0].shape[0] // blk
+    blocks = each * len(phases)
 
     def columns(g):
         return pl.ds(pl.multiple_of(g * lanes, lanes), lanes)
@@ -255,39 +282,44 @@
         c.wait()
 
     def gathered(side, block, at):
-        listed = [idx_ref[(start + block) * LIST + e] for e in range(LIST)]
+        place = phases[block // each] * each + block % each
+        listed = [idx_ref[place * LIST + e] for e in range(LIST)]
         return jnp.concatenate(
             [tabs[side][buf, slot, :, at] for slot in listed]
             + [reg_ref[side, n, :, at] for n in range(reg_ref.shape[1])],
             axis=0,
         )
 
-    everything = slice(0, lanes)
-
-    def score(block):
-        q = q_ref[block * blk : (block + 1) * blk]
-        return matmul_t(gathered(0, block, everything), spread_heads(q, head_width, range(QUAD)))
-
-    def context(block, p, inverse):
+    quad = QUAD * head_width
+
+    def score(block, group):
+        at = slice(group * quad, (group + 1) * quad)
+        inner = block % each * blk
+        q = q_refs[block // each][inner : inner + blk, at]
+        return matmul_t(gathered(0, block, at), spread_heads(q, head_width, range(QUAD)))
+
+    def context(unit, p, inverse):
+        block, group = unit
         outs = []
         for h in range(0, QUAD, 2):
             at = slice(h * blk, (h + 2) * blk)
-            v = gathered(1, block, slice(h * head_width, (h + 2) * head_width))
+            first = group * quad + h * head_width
+            v = gathered(1, block, slice(first, first + 2 * head_width))
             outs += pair_context(v, p[:, at], inverse[:, at], head_width)
-        ctx_ref[block * blk : (block + 1) * blk, columns(step)] = (
-            jnp.concatenate(outs, axis=0).astype(BF16).T
-        )
-
-    following, pending = score(0), None
+        at = pl.ds(pl.multiple_of(step * lanes + group * quad, quad), quad)
+        ctx_ref[block * blk : (block + 1) * blk, at] = jnp.concatenate(outs, axis=0).astype(BF16).T
+
+    units = [(block, group) for group in range(lanes // quad) for block in range(blocks)]
+    following, pending = score(*units[0]), None
     project(1)
-    for block in range(blocks):
+    for n, unit in enumerate(units):
         s = following
-        if block + 1 < blocks:
-            following = score(block + 1)
+        if n + 1 < len(units):
+            following = score(*units[n + 1])
         if pending is not None:
             context(*pending)
         p, _, total = soften(s)
-        pending = (block, p, 1.0 / total)
+        pending = (unit, p, 1.0 / total)
     context(*pending)
     if pieces:
         for c in give(step, buf):
@@ -296,27 +328,44 @@
     @pl.when(step == last)
     def _():
         output_weight().wait()
-        out = matmul(ctx_ref[...], wo_scratch[...]).astype(BF16)
-        for block in range(blocks):
-            o_ref[block] = out[block * blk : (block + 1) * blk]
+        ctx_ref[...] = matmul(ctx_ref[...], wo_scratch[...]).astype(BF16)
+        rows = each * blk
+        copies = [
+            pltpu.make_async_copy(
+                ctx_ref.at[pl.ds(n * rows, rows)], o_ref.at[pl.ds(phase * rows, rows)], o_sems.at[n]
+            )
+            for n, phase in enumerate(phases)
+        ]
+        for c in copies:
+            c.start()
+        for c in copies:
+            c.wait()
         if pieces:
-            for c in give(step - 1, 1 - buf) + give(step, buf):
+            for c in give(step, buf):
                 c.wait()
 
+    if pieces:
+
+        @pl.when((step == last) & (last > 0))
+        def _():
+            for c in give(step - 1, 1 - buf):
+                c.wait()
+
 
 def attend(
-    queries, table, reg_kv, slot_list, start, blocks, loaded, pieces, w_key, w_value, w_out, head_width, previous, deps
+    queries, table, reg_kv, slot_list, each, phases, loaded, pieces, w_key, w_value, w_out, head_width, previous, deps
 ):
     _, all_slots, blk, width = table.shape
-    lanes = QUAD * head_width
-    rows = blocks * blk
+    lanes = TILE_QUADS * QUAD * head_width
+    rows = each * blk
     pieces = [x.reshape(-1, width) for x in pieces]
     new_rows = sum(x.shape[0] for x in pieces)
     slots = loaded + new_rows // blk
-    assert start % blocks == 0 and width // lanes >= 2
-    operands = [slot_list, queries, reg_kv, *pieces]
+    assert width % lanes == 0
+    operands = [slot_list, *[queries] * len(phases), reg_kv, *pieces]
     in_specs = [
-        pl.BlockSpec((rows, lanes), lambda i, idx: (start // blocks, i)),
+        pl.BlockSpec((rows, lanes), functools.partial(lambda p, i, idx: (p, i), phase)) for phase in phases
+    ] + [
         pl.BlockSpec((*reg_kv.shape[:3], lanes), lambda i, idx: (0, 0, 0, i)),
     ] + [ANY] * len(pieces)
     if pieces:
@@ -336,15 +385,16 @@
     operands += deps
     in_specs += [ANY] * len(deps)
     skipped = len(deps) + (previous is not None)
-    out_specs += [pl.BlockSpec((blocks, blk, width), lambda i, idx: (start // blocks, 0, 0)), ANY]
-    out_shape += [jax.ShapeDtypeStruct((queries.shape[0] // blk, blk, width), BF16), TOKEN]
+    out_specs += [pl.BlockSpec(memory_space=pltpu.HBM), ANY]
+    out_shape += [pltpu.HBM(queries.shape, BF16), TOKEN]
     tab = pltpu.VMEM((2, slots, blk, lanes), BF16)
     sems = pltpu.SemaphoreType.DMA
-    scratch = [tab, tab, pltpu.VMEM((rows, width), BF16), pltpu.VMEM((width, width), BF16), sems((2, 2)), sems((1,))]
+    scratch = [tab, tab, pltpu.VMEM((rows * len(phases), width), BF16), pltpu.VMEM((width, width), BF16)]
+    scratch += [sems((2, 2)), sems((1,)), sems((len(phases),))]
     if pieces:
         scratch += [pltpu.VMEM((new_rows, width), BF16), sems((len(pieces),)), sems((2, 2))]
     out = pl.pallas_call(
-        functools.partial(attend_kernel, head_width, start, loaded, len(pieces), skipped),
+        functools.partial(attend_kernel, head_width, phases, loaded, len(pieces), skipped),
         grid_spec=pltpu.PrefetchScalarGridSpec(
             num_scalar_prefetch=1,
             grid=(width // lanes,),
@@ -497,8 +547,7 @@
     slot_list = jnp.where(is_before | is_after, outer, inner).astype(jnp.int32).reshape(-1)
 
     rows = normed.reshape(-1, width)
-    queries = (matmul(rows, w_query) * scale).astype(BF16)
-    table, reg_kv, keep, send = own_project(
+    table, reg_kv, keep, send, token = own_project(
         (slab & 1).reshape(1),
         rows,
         registers,
@@ -510,19 +559,23 @@
         head_width,
         2 * lanes,
         scale,
-        [queries],
+        [],
     )
     rounds = register_rounds(slab, keep, send, w_out)
     next(rounds)
-
-    def windows(table, phase, loaded, pieces, mixed, deps):
+    queries, token = query_project(
+        rows, w_query, 2 * lanes, scale, [token, left, right, before, after]
+    )
+    token = rounds.send([token])
+
+    def windows(table, at, loaded, pieces, mixed, deps):
         return attend(
             queries,
             table,
             reg_kv,
             slot_list,
-            phase * slab_blocks,
             slab_blocks,
+            at,
             loaded,
             pieces,
             w_key,
@@ -533,20 +586,13 @@
             deps,
         )
 
-    order = [*range(1, own_phases - 1), 0, own_phases - 1]
-    assert len(order) == 4
-    mixed, deps = None, []
-    for n, at in enumerate(order):
-        pieces, loaded = [], at_before if n < 3 else slots
-        if n == 0:
-            pieces, loaded = [left, right], at_left
-        if n == 1:
-            deps = [*deps, before, after]
-        if n == 2:
-            pieces = [before, after, corner_left, corner_right]
-        table, mixed, token = windows(table, at, loaded, pieces, mixed, deps)
-        token = rounds.send([token])
-        deps = [token]
+    inner, outer = list(range(1, own_phases - 1)), [0, own_phases - 1]
+    table, mixed, token = windows(table, inner, at_left, [left, right], None, [token])
+    token = rounds.send([token])
+    corners = [before, after, corner_left, corner_right]
+    _, mixed, token = windows(table, outer, at_before, corners, mixed, [token])
+    token = rounds.send([token])
+    token = rounds.send([])
     return mixed.reshape(own_phases, slab_blocks, blk, width), token
 
 

time: 131 us -> 102 us (0.78)
  the two profiles are of different devices: /device:TPU:11 before, /device:TPU:0 now
where the time goes in v5:
time: 102 us; the launch traced here: 100 us
  Pallas kernels  71.2 us (70%)
  starting transfers between devices  22.1 us (22%)
  local copies, waits for them, and re-layouts  3.12 us (3%)
  other arithmetic  1.72 us (2%)
  waiting for transfers between devices  1.21 us (1%)
    pallas_call x2, Pallas kernels, attend(): pl.pallas_call(functools.partial(attend_kernel, head_width, phases, loade...  42.9 us
    pallas_call x1, Pallas kernels, own_project(): pl.pallas_call(functools.partial(own_kernel, scale, head_width), grid_spe...  16.7 us
    ppermute x6, starting transfers between devices, around(): lax.ppermute(x, axis, [(i, (i + step) % n) for i in range(n) if closed or...  11.8 us
    ppermute x8, starting transfers between devices, swap(): lax.ppermute(x, axis, [(i, i ^ n << bit) for i in range(lax.axis_size(axi...  10.3 us
    pallas_call x4, Pallas kernels, small_call(): pl.pallas_call(wrapped, in_specs=[pl.BlockSpec(memory_space=pltpu.SMEM)]...  6.14 us
    pallas_call x1, Pallas kernels, query_project(): pl.pallas_call(functools.partial(query_kernel, scale), grid=(width // lan...  5.5 us
  transfers between devices with their start and end apart: 14, of which 1 were waited for; matrix products, arithmetic and copies ran while one was open for 3% of the time, Pallas kernels for 68%

profile of v5, /device:TPU:0, one launch (start us, length us, event | category | flops | bytes accessed | tf_op | source)
XLA Modules:
  0.0 100.2 jit_solution(17989352801089197180)
XLA Ops:
  0.6 0.0 copy-start.3
  0.6 1.4 %slice_bitcast_fusion.2 = (bf16[2,128,1024]{2,1,0:T(8,128)(2,1)S(1)}, bf16[2,128,1024]{2,1,0:T(8,128)(2,1)S(1)}) fusion(bf16[4,2,128,1024]{3,2,1,0:T(8,128)(2,1)} %param.7), kind=kLoop, calls=%fused_computation.4 | loop fusion | bytes 2097152 | tf_op jit(solution)/shard_map/squeeze | solution.py:522
  2.1 0.0 copy-start.2
  2.1 3.0 %collective-permute-start.2 = (bf16[2,128,1024]{2,1,0:T(8,128)(2,1)S(1)}, bf16[2,128,1024]{2,1,0:T(8,128)(2,1)S(1)}, u32[]{:S(2)}, u32[]{:S(2)}) collective-permute-start(bf16[2,128,1024]{2,1,0:T(8,128)(2,1)S(1)} %get-tuple-element.39), channel_id=1, source_target_pairs={{0,8},{8,16},{16,24},{24,0},{1,9},{9,17},{17,25},{25,1},{2,10},{10... | collective-permute-start | bytes 1572872 | tf_op jit(solution)/shard_map/ppermute | solution.py:517
  5.1 1.5 %slice_bitcast_fusion = (bf16[4,128,1024]{2,1,0:T(8,128)(2,1)}, bf16[4,128,1024]{2,1,0:T(8,128)(2,1)}) fusion(bf16[4,2,128,1024]{3,2,1,0:T(8,128)(2,1)S(1)} %copy-done.3), kind=kLoop, calls=%fused_computation | loop fusion | bytes 4194304 | tf_op jit(solution)/shard_map/squeeze | solution.py:524
  6.6 2.5 %collective-permute-start = (bf16[4,128,1024]{2,1,0:T(8,128)(2,1)}, bf16[4,128,1024]{2,1,0:T(8,128)(2,1)}, u32[]{:S(2)}, u32[]{:S(2)}) collective-permute-start(bf16[4,128,1024]{2,1,0:T(8,128)(2,1)} %get-tuple-element.41), channel_id=1, source_target_pairs={{0,1},{1,2},{2,3},{3,4},{4,5},{5,6},{6,7},{8,9},{9,10},{10,11},{11... | collective-permute-start | bytes 3145736 | tf_op jit(solution)/shard_map/ppermute | solution.py:517
  9.1 1.3 %collective-permute-start.1 = (bf16[4,128,1024]{2,1,0:T(8,128)(2,1)}, bf16[4,128,1024]{2,1,0:T(8,128)(2,1)}, u32[]{:S(2)}, u32[]{:S(2)}) collective-permute-start(bf16[4,128,1024]{2,1,0:T(8,128)(2,1)} %get-tuple-element.40), channel_id=1, source_target_pairs={{1,0},{2,1},{3,2},{4,3},{5,4},{6,5},{7,6},{9,8},{10,9},{11,10},{12... | collective-permute-start | bytes 3145736 | tf_op jit(solution)/shard_map/ppermute | solution.py:517
  10.3 1.7 %collective-permute-start.3 = (bf16[2,128,1024]{2,1,0:T(8,128)(2,1)S(1)}, bf16[2,128,1024]{2,1,0:T(8,128)(2,1)S(1)}, u32[]{:S(2)}, u32[]{:S(2)}) collective-permute-start(bf16[2,128,1024]{2,1,0:T(8,128)(2,1)S(1)} %get-tuple-element.38), channel_id=1, source_target_pairs={{0,24},{8,0},{16,8},{24,16},{1,25},{9,1},{17,9},{25,17},{2,26},{10... | collective-permute-start | bytes 1572872 | tf_op jit(solution)/shard_map/ppermute | solution.py:517
  12.0 16.7 %own_project.1 = (bf16[2,24,128,1024]{3,2,1,0:T(8,128)(2,1)}, bf16[2,2,128,1024]{3,2,1,0:T(8,128)(2,1)}, bf16[128,1152]{1,0:T(8,128)(2,1)S(1)}, bf16[128,1152]{1,0:T(8,128)(2,1)S(1)}, f32[8,128]{1,0:T(8,128)S(1)}) custom-call(s32[1]{0:T(128)} %bitcast.1.core_ref.refs_0_, bf16[1024,1024]{1,0:T(8,128)(2,1)} %bitcast.26, bf16[256,1024]{1,0:T(8,128)(2,1)S(1)} %copy-done.2, ...), custom_call_target="tpu_custom_call" | custom-call | flops 1048576 | bytes 65536 | tf_op jit(solution)/shard_map/own_project/pallas_call | solution.py:145
  28.7 1.3 %collective-permute-start.6 = (bf16[128,1152]{1,0:T(8,128)(2,1)S(1)}, bf16[128,1152]{1,0:T(8,128)(2,1)S(1)}, u32[]{:S(2)}, u32[]{:S(2)}) collective-permute-start(bf16[128,1152]{1,0:T(8,128)(2,1)S(1)} %get-tuple-element.25), channel_id=1, source_target_pairs={{0,1},{1,0},{2,3},{3,2},{4,5},{5,4},{6,7},{7,6},{8,9},{9,8},{10,11... | collective-permute-start | bytes 884744 | tf_op jit(solution)/shard_map/ppermute | solution.py:469
  30.0 0.0 collective-permute-done.2.refs_3_
  30.0 0.0 collective-permute-done.3.refs_4_
  30.1 0.8 pad_maximum_fusion
  30.9 1.9 %collective-permute-start.4 = (bf16[2,128,1024]{2,1,0:T(8,128)(2,1)}, bf16[2,128,1024]{2,1,0:T(8,128)(2,1)S(1)}, u32[]{:S(2)}, u32[]{:S(2)}) collective-permute-start(bf16[2,128,1024]{2,1,0:T(8,128)(2,1)} %pad_maximum_fusion), channel_id=1, source_target_pairs={{0,1},{1,2},{2,3},{3,4},{4,5},{5,6},{6,7},{8,9},{9,10},{10,11},{11... | collective-permute-start | bytes 1572872 | tf_op jit(solution)/shard_map/ppermute | solution.py:517
  32.9 0.0 copy-start.4
  32.9 5.5 %query_project.1 = (bf16[1024,1024]{1,0:T(8,128)(2,1)}, f32[8,128]{1,0:T(8,128)S(1)}) custom-call(bf16[1024,1024]{1,0:T(8,128)(2,1)} %bitcast.27, bf16[1024,1024]{1,0:T(8,128)(2,1)} %w_ref.1, f32[8,128]{1,0:T(8,128)S(1)} %get-tuple-element.20.refs_0_, bf16[4,128,1024]{2,1,0:T(8,128)(2,1)} %collective-permute-done.refs_1_, ...), custom_call_target="tpu_custom_call" | custom-call | flops 1048576 | bytes 65536 | tf_op jit(solution)/shard_map/query_project/pallas_call | solution.py:185
  38.4 0.8 register_merge.2
  39.3 2.4 %collective-permute-start.7 = (bf16[128,1152]{1,0:T(8,128)(2,1)S(1)}, bf16[128,1152]{1,0:T(8,128)(2,1)S(1)}, u32[]{:S(2)}, u32[]{:S(2)}) collective-permute-start(bf16[128,1152]{1,0:T(8,128)(2,1)S(1)} %get-tuple-element.30.refs_1_), channel_id=1, source_target_pairs={{0,2},{1,3},{2,0},{3,1},{4,6},{5,7},{6,4},{7,5},{8,10},{9,11},{10,... | collective-permute-start | bytes 884744 | tf_op jit(solution)/shard_map/ppermute | solution.py:469
  41.7 2.6 %collective-permute-start.8 = (bf16[128,1152]{1,0:T(8,128)(2,1)S(1)}, bf16[128,1152]{1,0:T(8,128)(2,1)S(1)}, u32[]{:S(2)}, u32[]{:S(2)}) collective-permute-start(bf16[128,1152]{1,0:T(8,128)(2,1)S(1)} %get-tuple-element.30.refs_1_), channel_id=1, source_target_pairs={{0,4},{1,5},{2,6},{3,7},{4,0},{5,1},{6,2},{7,3},{8,12},{9,13},{10,... | collective-permute-start | bytes 884744 | tf_op jit(solution)/shard_map/ppermute | solution.py:469
  44.3 0.8 pad_maximum_fusion.1
  45.1 1.5 %collective-permute-start.5 = (bf16[2,128,1024]{2,1,0:T(8,128)(2,1)}, bf16[2,128,1024]{2,1,0:T(8,128)(2,1)}, u32[]{:S(2)}, u32[]{:S(2)}) collective-permute-start(bf16[2,128,1024]{2,1,0:T(8,128)(2,1)} %pad_maximum_fusion.1), channel_id=1, source_target_pairs={{1,0},{2,1},{3,2},{4,3},{5,4},{6,5},{7,6},{9,8},{10,9},{11,10},{12... | collective-permute-start | bytes 1572872 | tf_op jit(solution)/shard_map/ppermute | solution.py:517
  46.7 0.1 reshape.42.idx_ref
  46.7 21.0 %attend.2 = (bf16[2,24,128,1024]{3,2,1,0:T(8,128)(2,1)}, bf16[1024,1024]{1,0:T(8,128)(2,1)}, f32[8,128]{1,0:T(8,128)S(1)}) custom-call(s32[40]{0:T(128)S(1)} %reshape.42.idx_ref, bf16[1024,1024]{1,0:T(8,128)(2,1)} %get-tuple-element.21.refs_0_.refs_1_, bf16[1024,1024]{1,0:T(8,128)(2,1)} %get-tuple-element.21.refs_0_.refs_1_, ...), custom_call_target="tpu_custom_call", output_to_operand_aliasing={{0}: (8, {})} | custom-call | flops 1048576 | bytes 65536 | tf_op jit(solution)/shard_map/attend/pallas_call | solution.py:396
  67.8 2.5 %register_merge.3 = (bf16[128,1152]{1,0:T(8,128)(2,1)S(1)}, f32[8,128]{1,0:T(8,128)S(1)}) custom-call(s32[1]{0:T(128)} %bitcast.12.refs_0_, bf16[128,1152]{1,0:T(8,128)(2,1)S(1)} %get-tuple-element.30.refs_1_, bf16[128,1152]{1,0:T(8,128)(2,1)S(1)} %collective-permute-done.7.refs_2_, bf16[128,1152]{1,0:T(8,128)(2,1)S(1)} %collective-permute-done.8.refs_3_, ...), custom_call_target="tpu_custom_call" | custom-call | flops 1048576 | bytes 65536 | tf_op jit(solution)/shard_map/register_merge/pallas_call | solution.py:448
  70.3 0.7 collective-permute-start.10
  71.0 1.5 %collective-permute-start.11 = (bf16[128,1152]{1,0:T(8,128)(2,1)S(1)}, bf16[128,1152]{1,0:T(8,128)(2,1)S(1)}, u32[]{:S(2)}, u32[]{:S(2)}) collective-permute-start(bf16[128,1152]{1,0:T(8,128)(2,1)S(1)} %get-tuple-element.34.refs_1_), channel_id=1, source_target_pairs={{0,16},{8,24},{16,0},{24,8},{1,17},{9,25},{17,1},{25,9},{2,18},{10... | collective-permute-start | bytes 884744 | tf_op jit(solution)/shard_map/ppermute | solution.py:469
  72.5 1.4 %collective-permute-start.12 = (bf16[128,1152]{1,0:T(8,128)(2,1)S(1)}, bf16[128,1152]{1,0:T(8,128)(2,1)S(1)}, u32[]{:S(2)}, u32[]{:S(2)}) collective-permute-start(bf16[128,1152]{1,0:T(8,128)(2,1)S(1)} %get-tuple-element.34.refs_1_), channel_id=1, source_target_pairs={{0,24},{8,16},{16,8},{24,0},{1,25},{9,17},{17,9},{25,1},{2,26},{10... | collective-permute-start | bytes 884744 | tf_op jit(solution)/shard_map/ppermute | solution.py:469
  73.9 21.9 %attend.3 = (bf16[2,24,128,1024]{3,2,1,0:T(8,128)(2,1)}, bf16[1024,1024]{1,0:T(8,128)(2,1)}, f32[8,128]{1,0:T(8,128)S(1)}) custom-call(s32[40]{0:T(128)S(1)} %reshape.42.idx_ref, bf16[1024,1024]{1,0:T(8,128)(2,1)} %get-tuple-element.21.refs_0_.refs_1_, ...), custom_call_target="tpu_custom_call", output_to_operand_aliasing={{0}: (10, {}), {1}: (12, {})} | custom-call | flops 1048576 | bytes 65536 | tf_op jit(solution)/shard_map/attend/pallas_call | solution.py:396
  95.8 1.9 %register_out.1 = (bf16[128,1024]{1,0:T(8,128)(2,1)S(1)}, f32[8,128]{1,0:T(8,128)}) custom-call(s32[1]{0:T(128)} %bitcast.14.refs_0_, bf16[128,1152]{1,0:T(8,128)(2,1)S(1)} %get-tuple-element.34.refs_1_, bf16[128,1152]{1,0:T(8,128)(2,1)S(1)} %collective-permute-done.10.refs_2_, bf16[128,1152]{1,0:T(8,128)(2,1)S(1)} %collective-permute-done.11.refs_3_, ...), custom_call_target="tpu_custom_call" | custom-call | flops 1048576 | bytes 65536 | tf_op jit(solution)/shard_map/register_out/pallas_call | solution.py:448
  97.8 0.4 collective-permute-start.13
  98.2 1.2 %collective-permute-done.13.refs_2_ = bf16[128,1024]{1,0:T(8,128)(2,1)S(1)} collective-permute-done((bf16[128,1024]{1,0:T(8,128)(2,1)S(1)}, bf16[128,1024]{1,0:T(8,128)(2,1)S(1)}, u32[]{:S(2)}, u32[]{:S(2)}) %collective-permute-start.13) | collective-permute-done | bytes 262176 | tf_op jit(solution)/shard_map/ppermute | solution.py:469
  99.4 0.8 register_join.1
  (22 shorter events, 0.2 us)
Async XLA Ops:
  0.6 4.4 %copy-start.3 = (bf16[4,2,128,1024]{3,2,1,0:T(8,128)(2,1)S(1)}, bf16[4,2,128,1024]{3,2,1,0:T(8,128)(2,1)}, u32[]{:S(2)}) copy-start(bf16[4,2,128,1024]{3,2,1,0:T(8,128)(2,1)} %param.7) | copy-start | bytes 6291460
  2.1 10.0 %copy-start.2 = (bf16[256,1024]{1,0:T(8,128)(2,1)S(1)}, bf16[256,1024]{1,0:T(8,128)(2,1)}, u32[]{:S(2)}) copy-start(bf16[256,1024]{1,0:T(8,128)(2,1)} %refs_1_.1) | copy-start | bytes 1572868
  2.1 27.9 %collective-permute-start.2 = (bf16[2,128,1024]{2,1,0:T(8,128)(2,1)S(1)}, bf16[2,128,1024]{2,1,0:T(8,128)(2,1)S(1)}, u32[]{:S(2)}, u32[]{:S(2)}) collective-permute-start(bf16[2,128,1024]{2,1,0:T(8,128)(2,1)S(1)} %get-tuple-element.39), channel_id=1, source_target_pairs={{0,8},{8,16},{16,24},{24,0},{1,9},{9,17},{17,25},{25,1},{2,10},{10... | collective-permute-start | bytes 1572872 | tf_op jit(solution)/shard_map/ppermute | solution.py:517
  6.6 26.3 %collective-permute-start = (bf16[4,128,1024]{2,1,0:T(8,128)(2,1)}, bf16[4,128,1024]{2,1,0:T(8,128)(2,1)}, u32[]{:S(2)}, u32[]{:S(2)}) collective-permute-start(bf16[4,128,1024]{2,1,0:T(8,128)(2,1)} %get-tuple-element.41), channel_id=1, source_target_pairs={{0,1},{1,2},{2,3},{3,4},{4,5},{5,6},{6,7},{8,9},{9,10},{10,11},{11... | collective-permute-start | bytes 3145736 | tf_op jit(solution)/shard_map/ppermute | solution.py:517
  9.1 23.8 %collective-permute-start.1 = (bf16[4,128,1024]{2,1,0:T(8,128)(2,1)}, bf16[4,128,1024]{2,1,0:T(8,128)(2,1)}, u32[]{:S(2)}, u32[]{:S(2)}) collective-permute-start(bf16[4,128,1024]{2,1,0:T(8,128)(2,1)} %get-tuple-element.40), channel_id=1, source_target_pairs={{1,0},{2,1},{3,2},{4,3},{5,4},{6,5},{7,6},{9,8},{10,9},{11,10},{12... | collective-permute-start | bytes 3145736 | tf_op jit(solution)/shard_map/ppermute | solution.py:517
  10.3 19.7 %collective-permute-start.3 = (bf16[2,128,1024]{2,1,0:T(8,128)(2,1)S(1)}, bf16[2,128,1024]{2,1,0:T(8,128)(2,1)S(1)}, u32[]{:S(2)}, u32[]{:S(2)}) collective-permute-start(bf16[2,128,1024]{2,1,0:T(8,128)(2,1)S(1)} %get-tuple-element.38), channel_id=1, source_target_pairs={{0,24},{8,0},{16,8},{24,16},{1,25},{9,1},{17,9},{25,17},{2,26},{10... | collective-permute-start | bytes 1572872 | tf_op jit(solution)/shard_map/ppermute | solution.py:517
  28.7 9.7 %collective-permute-start.6 = (bf16[128,1152]{1,0:T(8,128)(2,1)S(1)}, bf16[128,1152]{1,0:T(8,128)(2,1)S(1)}, u32[]{:S(2)}, u32[]{:S(2)}) collective-permute-start(bf16[128,1152]{1,0:T(8,128)(2,1)S(1)} %get-tuple-element.25), channel_id=1, source_target_pairs={{0,1},{1,0},{2,3},{3,2},{4,5},{5,4},{6,7},{7,6},{8,9},{9,8},{10,11... | collective-permute-start | bytes 884744 | tf_op jit(solution)/shard_map/ppermute | solution.py:469
  30.9 42.9 %collective-permute-start.4 = (bf16[2,128,1024]{2,1,0:T(8,128)(2,1)}, bf16[2,128,1024]{2,1,0:T(8,128)(2,1)S(1)}, u32[]{:S(2)}, u32[]{:S(2)}) collective-permute-start(bf16[2,128,1024]{2,1,0:T(8,128)(2,1)} %pad_maximum_fusion), channel_id=1, source_target_pairs={{0,1},{1,2},{2,3},{3,4},{4,5},{5,6},{6,7},{8,9},{9,10},{10,11},{11... | collective-permute-start | bytes 1572872 | tf_op jit(solution)/shard_map/ppermute | solution.py:517
  32.9 13.7 %copy-start.4 = (s32[4,2,5]{2,1,0:T(2,128)S(1)}, s32[4,2,5]{2,1,0:T(2,128)}, u32[]{:S(2)}) copy-start(s32[4,2,5]{2,1,0:T(2,128)} %param.8) | copy-start | bytes 484
  38.4 8.3 %copy-start.1 = (bf16[2,2,128,1024]{3,2,1,0:T(8,128)(2,1)S(1)}, bf16[2,2,128,1024]{3,2,1,0:T(8,128)(2,1)}, u32[]{:S(2)}) copy-start(bf16[2,2,128,1024]{3,2,1,0:T(8,128)(2,1)} %get-tuple-element.22.refs_2_) | copy-start | bytes 3145732
  39.3 28.5 %collective-permute-start.7 = (bf16[128,1152]{1,0:T(8,128)(2,1)S(1)}, bf16[128,1152]{1,0:T(8,128)(2,1)S(1)}, u32[]{:S(2)}, u32[]{:S(2)}) collective-permute-start(bf16[128,1152]{1,0:T(8,128)(2,1)S(1)} %get-tuple-element.30.refs_1_), channel_id=1, source_target_pairs={{0,2},{1,3},{2,0},{3,1},{4,6},{5,7},{6,4},{7,5},{8,10},{9,11},{10,... | collective-permute-start | bytes 884744 | tf_op jit(solution)/shard_map/ppermute | solution.py:469
  41.7 26.1 %collective-permute-start.8 = (bf16[128,1152]{1,0:T(8,128)(2,1)S(1)}, bf16[128,1152]{1,0:T(8,128)(2,1)S(1)}, u32[]{:S(2)}, u32[]{:S(2)}) collective-permute-start(bf16[128,1152]{1,0:T(8,128)(2,1)S(1)} %get-tuple-element.30.refs_1_), channel_id=1, source_target_pairs={{0,4},{1,5},{2,6},{3,7},{4,0},{5,1},{6,2},{7,3},{8,12},{9,13},{10,... | collective-permute-start | bytes 884744 | tf_op jit(solution)/shard_map/ppermute | solution.py:469
  44.3 23.5 %collective-permute-start.9 = (bf16[128,1152]{1,0:T(8,128)(2,1)S(1)}, bf16[128,1152]{1,0:T(8,128)(2,1)}, u32[]{:S(2)}, u32[]{:S(2)}) collective-permute-start(bf16[128,1152]{1,0:T(8,128)(2,1)S(1)} %get-tuple-element.30.refs_1_), channel_id=1, source_target_pairs={{0,6},{1,7},{2,4},{3,5},{4,2},{5,3},{6,0},{7,1},{8,14},{9,15},{10,... | collective-permute-start | bytes 884744 | tf_op jit(solution)/shard_map/ppermute | solution.py:469
  45.1 28.7 %collective-permute-start.5 = (bf16[2,128,1024]{2,1,0:T(8,128)(2,1)}, bf16[2,128,1024]{2,1,0:T(8,128)(2,1)}, u32[]{:S(2)}, u32[]{:S(2)}) collective-permute-start(bf16[2,128,1024]{2,1,0:T(8,128)(2,1)} %pad_maximum_fusion.1), channel_id=1, source_target_pairs={{1,0},{2,1},{3,2},{4,3},{5,4},{6,5},{7,6},{9,8},{10,9},{11,10},{12... | collective-permute-start | bytes 1572872 | tf_op jit(solution)/shard_map/ppermute | solution.py:517
  70.3 25.5 %collective-permute-start.10 = (bf16[128,1152]{1,0:T(8,128)(2,1)S(1)}, bf16[128,1152]{1,0:T(8,128)(2,1)S(1)}, u32[]{:S(2)}, u32[]{:S(2)}) collective-permute-start(bf16[128,1152]{1,0:T(8,128)(2,1)S(1)} %get-tuple-element.34.refs_1_), channel_id=1, source_target_pairs={{0,8},{8,0},{16,24},{24,16},{1,9},{9,1},{17,25},{25,17},{2,10},{10... | collective-permute-start | bytes 884744 | tf_op jit(solution)/shard_map/ppermute | solution.py:469
  71.0 24.8 %collective-permute-start.11 = (bf16[128,1152]{1,0:T(8,128)(2,1)S(1)}, bf16[128,1152]{1,0:T(8,128)(2,1)S(1)}, u32[]{:S(2)}, u32[]{:S(2)}) collective-permute-start(bf16[128,1152]{1,0:T(8,128)(2,1)S(1)} %get-tuple-element.34.refs_1_), channel_id=1, source_target_pairs={{0,16},{8,24},{16,0},{24,8},{1,17},{9,25},{17,1},{25,9},{2,18},{10... | collective-permute-start | bytes 884744 | tf_op jit(solution)/shard_map/ppermute | solution.py:469
  72.5 23.3 %collective-permute-start.12 = (bf16[128,1152]{1,0:T(8,128)(2,1)S(1)}, bf16[128,1152]{1,0:T(8,128)(2,1)S(1)}, u32[]{:S(2)}, u32[]{:S(2)}) collective-permute-start(bf16[128,1152]{1,0:T(8,128)(2,1)S(1)} %get-tuple-element.34.refs_1_), channel_id=1, source_target_pairs={{0,24},{8,16},{16,8},{24,0},{1,25},{9,17},{17,9},{25,1},{2,26},{10... | collective-permute-start | bytes 884744 | tf_op jit(solution)/shard_map/ppermute | solution.py:469
  73.9 22.0 %copy-start = (bf16[1024,1024]{1,0:T(8,128)(2,1)S(1)}, bf16[1024,1024]{1,0:T(8,128)(2,1)}, u32[]{:S(2)}) copy-start(bf16[1024,1024]{1,0:T(8,128)(2,1)} %refs_5_.3) | copy-start | bytes 6291460
  97.8 1.6 %collective-permute-start.13 = (bf16[128,1024]{1,0:T(8,128)(2,1)S(1)}, bf16[128,1024]{1,0:T(8,128)(2,1)S(1)}, u32[]{:S(2)}, u32[]{:S(2)}) collective-permute-start(bf16[128,1024]{1,0:T(8,128)(2,1)S(1)} %get-tuple-element.36.refs_1_), channel_id=1, source_target_pairs={{0,1},{1,0},{2,3},{3,2},{4,5},{5,4},{6,7},{7,6},{8,9},{9,8},{10,11... | collective-permute-start | bytes 786440 | tf_op jit(solution)/shard_map/ppermute | solution.py:469

commit v6 on v5

--- a/solution.py
+++ b/solution.py
@@ -177,7 +177,9 @@
 
 
 def query_kernel(scale, x_ref, w_ref, *refs):
-    refs[-2][...] = (matmul(x_ref[...], w_ref[...]) * scale).astype(BF16)
+    lanes = refs[-2].shape[1]
+    at = pl.ds(pl.multiple_of(pl.program_id(0) * lanes, lanes), lanes)
+    refs[-2][...] = (matmul(x_ref[...], w_ref[:, at]) * scale).astype(BF16)
 
 
 def query_project(rows, w_query, lanes, scale, deps):
@@ -186,13 +188,13 @@
         functools.partial(query_kernel, scale),
         grid=(width // lanes,),
         in_specs=[
-            pl.BlockSpec((count, width), lambda i: (0, 0)),
-            pl.BlockSpec((width, lanes), lambda i: (0, i)),
+            VMEM,
+            VMEM,
         ]
         + [ANY] * len(deps),
         out_specs=[pl.BlockSpec((count, lanes), lambda i: (0, i)), ANY],
-        out_shape=[jax.ShapeDtypeStruct((count, width), BF16), TOKEN],
-        compiler_params=params(52),
+        out_shape=[pltpu.HBM((count, width), BF16), TOKEN],
+        compiler_params=params(20),
         cost_estimate=cost(),
         name="query_project",
     )(rows, w_query, *deps)

time: 102 us -> 101 us (level)
  Pallas kernels: 71.2 us -> 69.4 us
  local copies, waits for them, and re-layouts: 3.12 us -> 4.19 us
    pallas_call x1, Pallas kernels: 5.5 us -> 3.6 us  [query_project(): pl.pallas_call(functools.partial(query_kernel, scale), grid=(width // lan...]
    ppermute x6, starting transfers between devices: 11.8 us -> 10.4 us  [around(): lax.ppermute(x, axis, [(i, (i + step) % n) for i in range(n) if closed or...]
    ppermute x8, starting transfers between devices: 10.3 us -> 11.6 us  [swap(): lax.ppermute(x, axis, [(i, i ^ n << bit) for i in range(lax.axis_size(axi...]
  transfers between devices with their start and end apart: 14 -> 14, of which waited for: 1 -> 1; matrix products, arithmetic and copies ran while one was open for 3% -> 4% of each run, Pallas kernels for 68% -> 67%
where the time goes in v6:
time: 101 us; the launch traced here: 99.5 us
  Pallas kernels  69.4 us (69%)
  starting transfers between devices  22 us (22%)
  local copies, waits for them, and re-layouts  4.19 us (4%)
  other arithmetic  1.72 us (2%)
  waiting for transfers between devices  1.22 us (1%)
    pallas_call x2, Pallas kernels, attend(): pl.pallas_call(functools.partial(attend_kernel, head_width, phases, loade...  42.9 us
    pallas_call x1, Pallas kernels, own_project(): pl.pallas_call(functools.partial(own_kernel, scale, head_width), grid_spe...  16.8 us
    ppermute x8, starting transfers between devices, swap(): lax.ppermute(x, axis, [(i, i ^ n << bit) for i in range(lax.axis_size(axi...  11.6 us
    ppermute x6, starting transfers between devices, around(): lax.ppermute(x, axis, [(i, (i + step) % n) for i in range(n) if closed or...  10.4 us
    pallas_call x4, Pallas kernels, small_call(): pl.pallas_call(wrapped, in_specs=[pl.BlockSpec(memory_space=pltpu.SMEM)]...  6.14 us
    pallas_call x1, Pallas kernels, query_project(): pl.pallas_call(functools.partial(query_kernel, scale), grid=(width // lan...  3.6 us
    squeeze x1, local copies, waits for them, and re-layouts, shards(): after = around(normed[0], 'phase', -1, True)  2.37 us
  transfers between devices with their start and end apart: 14, of which 1 were waited for; matrix products, arithmetic and copies ran while one was open for 4% of the time, Pallas kernels for 67%

profile of v6, /device:TPU:0, one launch (start us, length us, event | category | flops | bytes accessed | tf_op | source)
XLA Modules:
  0.0 99.5 jit_solution(17961544473545796708)
XLA Ops:
  0.6 0.0 copy-start
  0.6 2.4 %slice_bitcast_fusion.2 = (bf16[2,128,1024]{2,1,0:T(8,128)(2,1)}, bf16[2,128,1024]{2,1,0:T(8,128)(2,1)}) fusion(bf16[4,2,128,1024]{3,2,1,0:T(8,128)(2,1)} %param.7), kind=kLoop, calls=%fused_computation.4 | loop fusion | bytes 2097152 | tf_op jit(solution)/shard_map/squeeze | solution.py:524
  3.0 2.9 %collective-permute-start.2 = (bf16[2,128,1024]{2,1,0:T(8,128)(2,1)}, bf16[2,128,1024]{2,1,0:T(8,128)(2,1)S(1)}, u32[]{:S(2)}, u32[]{:S(2)}) collective-permute-start(bf16[2,128,1024]{2,1,0:T(8,128)(2,1)} %get-tuple-element.39), channel_id=1, source_target_pairs={{0,8},{8,16},{16,24},{24,0},{1,9},{9,17},{17,25},{25,1},{2,10},{10... | collective-permute-start | bytes 1572872 | tf_op jit(solution)/shard_map/ppermute | solution.py:519
  6.0 1.6 %slice_bitcast_fusion = (bf16[4,128,1024]{2,1,0:T(8,128)(2,1)}, bf16[4,128,1024]{2,1,0:T(8,128)(2,1)}) fusion(bf16[4,2,128,1024]{3,2,1,0:T(8,128)(2,1)S(1)} %copy-done), kind=kLoop, calls=%fused_computation | loop fusion | bytes 4194304 | tf_op jit(solution)/shard_map/squeeze | solution.py:526
  7.6 1.5 %collective-permute-start = (bf16[4,128,1024]{2,1,0:T(8,128)(2,1)}, bf16[4,128,1024]{2,1,0:T(8,128)(2,1)S(1)}, u32[]{:S(2)}, u32[]{:S(2)}) collective-permute-start(bf16[4,128,1024]{2,1,0:T(8,128)(2,1)} %get-tuple-element.41), channel_id=1, source_target_pairs={{0,1},{1,2},{2,3},{3,4},{4,5},{5,6},{6,7},{8,9},{9,10},{10,11},{11... | collective-permute-start | bytes 3145736 | tf_op jit(solution)/shard_map/ppermute | solution.py:519
  9.1 1.3 %collective-permute-start.1 = (bf16[4,128,1024]{2,1,0:T(8,128)(2,1)}, bf16[4,128,1024]{2,1,0:T(8,128)(2,1)}, u32[]{:S(2)}, u32[]{:S(2)}) collective-permute-start(bf16[4,128,1024]{2,1,0:T(8,128)(2,1)} %get-tuple-element.40), channel_id=1, source_target_pairs={{1,0},{2,1},{3,2},{4,3},{5,4},{6,5},{7,6},{9,8},{10,9},{11,10},{12... | collective-permute-start | bytes 3145736 | tf_op jit(solution)/shard_map/ppermute | solution.py:519
  10.4 1.3 %collective-permute-start.3 = (bf16[2,128,1024]{2,1,0:T(8,128)(2,1)}, bf16[2,128,1024]{2,1,0:T(8,128)(2,1)S(1)}, u32[]{:S(2)}, u32[]{:S(2)}) collective-permute-start(bf16[2,128,1024]{2,1,0:T(8,128)(2,1)} %get-tuple-element.38), channel_id=1, source_target_pairs={{0,24},{8,0},{16,8},{24,16},{1,25},{9,1},{17,9},{25,17},{2,26},{10... | collective-permute-start | bytes 1572872 | tf_op jit(solution)/shard_map/ppermute | solution.py:519
  11.7 16.8 %own_project.1 = (bf16[2,24,128,1024]{3,2,1,0:T(8,128)(2,1)}, bf16[2,2,128,1024]{3,2,1,0:T(8,128)(2,1)}, bf16[128,1152]{1,0:T(8,128)(2,1)S(1)}, bf16[128,1152]{1,0:T(8,128)(2,1)S(1)}, f32[8,128]{1,0:T(8,128)S(1)}) custom-call(s32[1]{0:T(128)} %bitcast.1.core_ref.refs_0_, bf16[1024,1024]{1,0:T(8,128)(2,1)} %bitcast.23, bf16[256,1024]{1,0:T(8,128)(2,1)S(1)} %copy-done.6, ...), custom_call_target="tpu_custom_call" | custom-call | flops 1048576 | bytes 65536 | tf_op jit(solution)/shard_map/own_project/pallas_call | solution.py:145
  28.5 2.6 %collective-permute-start.6 = (bf16[128,1152]{1,0:T(8,128)(2,1)S(1)}, bf16[128,1152]{1,0:T(8,128)(2,1)S(1)}, u32[]{:S(2)}, u32[]{:S(2)}) collective-permute-start(bf16[128,1152]{1,0:T(8,128)(2,1)S(1)} %get-tuple-element.25), channel_id=1, source_target_pairs={{0,1},{1,0},{2,3},{3,2},{4,5},{5,4},{6,7},{7,6},{8,9},{9,8},{10,11... | collective-permute-start | bytes 884744 | tf_op jit(solution)/shard_map/ppermute | solution.py:471
  31.1 0.0 collective-permute-done.2.refs_3_
  31.1 0.0 collective-permute-done.3.refs_4_
  31.2 0.8 pad_maximum_fusion
  32.0 1.9 %collective-permute-start.4 = (bf16[2,128,1024]{2,1,0:T(8,128)(2,1)}, bf16[2,128,1024]{2,1,0:T(8,128)(2,1)S(1)}, u32[]{:S(2)}, u32[]{:S(2)}) collective-permute-start(bf16[2,128,1024]{2,1,0:T(8,128)(2,1)} %pad_maximum_fusion), channel_id=1, source_target_pairs={{0,1},{1,2},{2,3},{3,4},{4,5},{5,6},{6,7},{8,9},{9,10},{10,11},{11... | collective-permute-start | bytes 1572872 | tf_op jit(solution)/shard_map/ppermute | solution.py:519
  34.0 0.0 collective-permute-done.1.refs_2_
  34.0 0.0 copy-start.7
  34.1 3.6 %query_project.1 = (bf16[1024,1024]{1,0:T(8,128)(2,1)}, f32[8,128]{1,0:T(8,128)S(1)}) custom-call(bf16[1024,1024]{1,0:T(8,128)(2,1)S(1)} %bitcast.24, bf16[1024,1024]{1,0:T(8,128)(2,1)S(1)} %copy-done.3, f32[8,128]{1,0:T(8,128)S(1)} %get-tuple-element.20.refs_0_, bf16[4,128,1024]{2,1,0:T(8,128)(2,1)S(1)} %collective-permute-done.refs_1_, ...), custom_call_target="tpu_custom_call" | custom-call | flops 1048576 | bytes 65536 | tf_op jit(solution)/shard_map/query_project/pallas_call | solution.py:187
  37.7 0.8 register_merge.2
  38.5 2.4 %collective-permute-start.7 = (bf16[128,1152]{1,0:T(8,128)(2,1)S(1)}, bf16[128,1152]{1,0:T(8,128)(2,1)S(1)}, u32[]{:S(2)}, u32[]{:S(2)}) collective-permute-start(bf16[128,1152]{1,0:T(8,128)(2,1)S(1)} %get-tuple-element.30.refs_1_), channel_id=1, source_target_pairs={{0,2},{1,3},{2,0},{3,1},{4,6},{5,7},{6,4},{7,5},{8,10},{9,11},{10,... | collective-permute-start | bytes 884744 | tf_op jit(solution)/shard_map/ppermute | solution.py:471
  40.9 2.6 %collective-permute-start.8 = (bf16[128,1152]{1,0:T(8,128)(2,1)S(1)}, bf16[128,1152]{1,0:T(8,128)(2,1)S(1)}, u32[]{:S(2)}, u32[]{:S(2)}) collective-permute-start(bf16[128,1152]{1,0:T(8,128)(2,1)S(1)} %get-tuple-element.30.refs_1_), channel_id=1, source_target_pairs={{0,4},{1,5},{2,6},{3,7},{4,0},{5,1},{6,2},{7,3},{8,12},{9,13},{10,... | collective-permute-start | bytes 884744 | tf_op jit(solution)/shard_map/ppermute | solution.py:471
  43.5 0.8 pad_maximum_fusion.1
  44.4 1.5 %collective-permute-start.5 = (bf16[2,128,1024]{2,1,0:T(8,128)(2,1)}, bf16[2,128,1024]{2,1,0:T(8,128)(2,1)}, u32[]{:S(2)}, u32[]{:S(2)}) collective-permute-start(bf16[2,128,1024]{2,1,0:T(8,128)(2,1)} %pad_maximum_fusion.1), channel_id=1, source_target_pairs={{1,0},{2,1},{3,2},{4,3},{5,4},{6,5},{7,6},{9,8},{10,9},{11,10},{12... | collective-permute-start | bytes 1572872 | tf_op jit(solution)/shard_map/ppermute | solution.py:519
  45.9 0.1 reshape.42.idx_ref
  46.0 21.0 %attend.2 = (bf16[2,24,128,1024]{3,2,1,0:T(8,128)(2,1)}, bf16[1024,1024]{1,0:T(8,128)(2,1)}, f32[8,128]{1,0:T(8,128)S(1)}) custom-call(s32[40]{0:T(128)S(1)} %reshape.42.idx_ref, bf16[1024,1024]{1,0:T(8,128)(2,1)} %get-tuple-element.21.refs_0_.refs_1_, bf16[1024,1024]{1,0:T(8,128)(2,1)} %get-tuple-element.21.refs_0_.refs_1_, ...), custom_call_target="tpu_custom_call", output_to_operand_aliasing={{0}: (8, {})} | custom-call | flops 1048576 | bytes 65536 | tf_op jit(solution)/shard_map/attend/pallas_call | solution.py:398
  67.0 2.5 %register_merge.3 = (bf16[128,1152]{1,0:T(8,128)(2,1)S(1)}, f32[8,128]{1,0:T(8,128)S(1)}) custom-call(s32[1]{0:T(128)} %bitcast.12.refs_0_, bf16[128,1152]{1,0:T(8,128)(2,1)S(1)} %get-tuple-element.30.refs_1_, bf16[128,1152]{1,0:T(8,128)(2,1)S(1)} %collective-permute-done.7.refs_2_, bf16[128,1152]{1,0:T(8,128)(2,1)S(1)} %collective-permute-done.8.refs_3_, ...), custom_call_target="tpu_custom_call" | custom-call | flops 1048576 | bytes 65536 | tf_op jit(solution)/shard_map/register_merge/pallas_call | solution.py:450
  69.6 0.7 collective-permute-start.10
  70.2 1.5 %collective-permute-start.11 = (bf16[128,1152]{1,0:T(8,128)(2,1)S(1)}, bf16[128,1152]{1,0:T(8,128)(2,1)S(1)}, u32[]{:S(2)}, u32[]{:S(2)}) collective-permute-start(bf16[128,1152]{1,0:T(8,128)(2,1)S(1)} %get-tuple-element.34.refs_1_), channel_id=1, source_target_pairs={{0,16},{8,24},{16,0},{24,8},{1,17},{9,25},{17,1},{25,9},{2,18},{10... | collective-permute-start | bytes 884744 | tf_op jit(solution)/shard_map/ppermute | solution.py:471
  71.7 1.4 %collective-permute-start.12 = (bf16[128,1152]{1,0:T(8,128)(2,1)S(1)}, bf16[128,1152]{1,0:T(8,128)(2,1)S(1)}, u32[]{:S(2)}, u32[]{:S(2)}) collective-permute-start(bf16[128,1152]{1,0:T(8,128)(2,1)S(1)} %get-tuple-element.34.refs_1_), channel_id=1, source_target_pairs={{0,24},{8,16},{16,8},{24,0},{1,25},{9,17},{17,9},{25,1},{2,26},{10... | collective-permute-start | bytes 884744 | tf_op jit(solution)/shard_map/ppermute | solution.py:471
  73.1 21.9 %attend.3 = (bf16[2,24,128,1024]{3,2,1,0:T(8,128)(2,1)}, bf16[1024,1024]{1,0:T(8,128)(2,1)}, f32[8,128]{1,0:T(8,128)S(1)}) custom-call(s32[40]{0:T(128)S(1)} %reshape.42.idx_ref, bf16[1024,1024]{1,0:T(8,128)(2,1)} %get-tuple-element.21.refs_0_.refs_1_, ...), custom_call_target="tpu_custom_call", output_to_operand_aliasing={{0}: (10, {}), {1}: (12, {})} | custom-call | flops 1048576 | bytes 65536 | tf_op jit(solution)/shard_map/attend/pallas_call | solution.py:398
  95.1 1.9 %register_out.1 = (bf16[128,1024]{1,0:T(8,128)(2,1)S(1)}, f32[8,128]{1,0:T(8,128)}) custom-call(s32[1]{0:T(128)} %bitcast.14.refs_0_, bf16[128,1152]{1,0:T(8,128)(2,1)S(1)} %get-tuple-element.34.refs_1_, bf16[128,1152]{1,0:T(8,128)(2,1)S(1)} %collective-permute-done.10.refs_2_, bf16[128,1152]{1,0:T(8,128)(2,1)S(1)} %collective-permute-done.11.refs_3_, ...), custom_call_target="tpu_custom_call" | custom-call | flops 1048576 | bytes 65536 | tf_op jit(solution)/shard_map/register_out/pallas_call | solution.py:450
  97.0 0.4 collective-permute-start.13
  97.5 1.2 %collective-permute-done.13.refs_2_ = bf16[128,1024]{1,0:T(8,128)(2,1)S(1)} collective-permute-done((bf16[128,1024]{1,0:T(8,128)(2,1)S(1)}, bf16[128,1024]{1,0:T(8,128)(2,1)S(1)}, u32[]{:S(2)}, u32[]{:S(2)}) %collective-permute-start.13) | collective-permute-done | bytes 262176 | tf_op jit(solution)/shard_map/ppermute | solution.py:471
  98.6 0.8 register_join.1
  (28 shorter events, 0.2 us)
Async XLA Ops:
  0.6 5.3 %copy-start = (bf16[4,2,128,1024]{3,2,1,0:T(8,128)(2,1)S(1)}, bf16[4,2,128,1024]{3,2,1,0:T(8,128)(2,1)}, u32[]{:S(2)}) copy-start(bf16[4,2,128,1024]{3,2,1,0:T(8,128)(2,1)} %param.7) | copy-start | bytes 6291460
  3.0 8.7 %copy-start.6 = (bf16[256,1024]{1,0:T(8,128)(2,1)S(1)}, bf16[256,1024]{1,0:T(8,128)(2,1)}, u32[]{:S(2)}) copy-start(bf16[256,1024]{1,0:T(8,128)(2,1)} %refs_1_.1) | copy-start | bytes 1572868
  3.0 28.1 %collective-permute-start.2 = (bf16[2,128,1024]{2,1,0:T(8,128)(2,1)}, bf16[2,128,1024]{2,1,0:T(8,128)(2,1)S(1)}, u32[]{:S(2)}, u32[]{:S(2)}) collective-permute-start(bf16[2,128,1024]{2,1,0:T(8,128)(2,1)} %get-tuple-element.39), channel_id=1, source_target_pairs={{0,8},{8,16},{16,24},{24,0},{1,9},{9,17},{17,25},{25,1},{2,10},{10... | collective-permute-start | bytes 1572872 | tf_op jit(solution)/shard_map/ppermute | solution.py:519
  7.6 26.4 %collective-permute-start = (bf16[4,128,1024]{2,1,0:T(8,128)(2,1)}, bf16[4,128,1024]{2,1,0:T(8,128)(2,1)S(1)}, u32[]{:S(2)}, u32[]{:S(2)}) collective-permute-start(bf16[4,128,1024]{2,1,0:T(8,128)(2,1)} %get-tuple-element.41), channel_id=1, source_target_pairs={{0,1},{1,2},{2,3},{3,4},{4,5},{5,6},{6,7},{8,9},{9,10},{10,11},{11... | collective-permute-start | bytes 3145736 | tf_op jit(solution)/shard_map/ppermute | solution.py:519
  9.1 24.9 %collective-permute-start.1 = (bf16[4,128,1024]{2,1,0:T(8,128)(2,1)}, bf16[4,128,1024]{2,1,0:T(8,128)(2,1)}, u32[]{:S(2)}, u32[]{:S(2)}) collective-permute-start(bf16[4,128,1024]{2,1,0:T(8,128)(2,1)} %get-tuple-element.40), channel_id=1, source_target_pairs={{1,0},{2,1},{3,2},{4,3},{5,4},{6,5},{7,6},{9,8},{10,9},{11,10},{12... | collective-permute-start | bytes 3145736 | tf_op jit(solution)/shard_map/ppermute | solution.py:519
  10.4 20.7 %collective-permute-start.3 = (bf16[2,128,1024]{2,1,0:T(8,128)(2,1)}, bf16[2,128,1024]{2,1,0:T(8,128)(2,1)S(1)}, u32[]{:S(2)}, u32[]{:S(2)}) collective-permute-start(bf16[2,128,1024]{2,1,0:T(8,128)(2,1)} %get-tuple-element.38), channel_id=1, source_target_pairs={{0,24},{8,0},{16,8},{24,16},{1,25},{9,1},{17,9},{25,17},{2,26},{10... | collective-permute-start | bytes 1572872 | tf_op jit(solution)/shard_map/ppermute | solution.py:519
  11.7 22.3 %copy-start.3 = (bf16[1024,1024]{1,0:T(8,128)(2,1)S(1)}, bf16[1024,1024]{1,0:T(8,128)(2,1)}, u32[]{:S(2)}) copy-start(bf16[1024,1024]{1,0:T(8,128)(2,1)} %w_ref.1) | copy-start | bytes 6291460
  28.5 5.6 %copy-start.1 = (bf16[4,2,128,1024]{3,2,1,0:T(8,128)(2,1)S(1)}, bf16[4,2,128,1024]{3,2,1,0:T(8,128)(2,1)}, u32[]{:S(2)}) copy-start(bf16[4,2,128,1024]{3,2,1,0:T(8,128)(2,1)} %param.7) | copy-start | bytes 6291460
  28.5 9.2 %collective-permute-start.6 = (bf16[128,1152]{1,0:T(8,128)(2,1)S(1)}, bf16[128,1152]{1,0:T(8,128)(2,1)S(1)}, u32[]{:S(2)}, u32[]{:S(2)}) collective-permute-start(bf16[128,1152]{1,0:T(8,128)(2,1)S(1)} %get-tuple-element.25), channel_id=1, source_target_pairs={{0,1},{1,0},{2,3},{3,2},{4,5},{5,4},{6,7},{7,6},{8,9},{9,8},{10,11... | collective-permute-start | bytes 884744 | tf_op jit(solution)/shard_map/ppermute | solution.py:471
  32.0 41.1 %collective-permute-start.4 = (bf16[2,128,1024]{2,1,0:T(8,128)(2,1)}, bf16[2,128,1024]{2,1,0:T(8,128)(2,1)S(1)}, u32[]{:S(2)}, u32[]{:S(2)}) collective-permute-start(bf16[2,128,1024]{2,1,0:T(8,128)(2,1)} %pad_maximum_fusion), channel_id=1, source_target_pairs={{0,1},{1,2},{2,3},{3,4},{4,5},{5,6},{6,7},{8,9},{9,10},{10,11},{11... | collective-permute-start | bytes 1572872 | tf_op jit(solution)/shard_map/ppermute | solution.py:519
  34.0 3.7 %copy-start.4 = (bf16[4,128,1024]{2,1,0:T(8,128)(2,1)}, bf16[4,128,1024]{2,1,0:T(8,128)(2,1)S(1)}, u32[]{:S(2)}) copy-start(bf16[4,128,1024]{2,1,0:T(8,128)(2,1)S(1)} %collective-permute-done.refs_1_) | copy-start | bytes 3145732
  34.0 11.8 %copy-start.7 = (s32[4,2,5]{2,1,0:T(2,128)S(1)}, s32[4,2,5]{2,1,0:T(2,128)}, u32[]{:S(2)}) copy-start(s32[4,2,5]{2,1,0:T(2,128)} %param.8) | copy-start | bytes 484
  37.7 8.3 %copy-start.5 = (bf16[2,2,128,1024]{3,2,1,0:T(8,128)(2,1)S(1)}, bf16[2,2,128,1024]{3,2,1,0:T(8,128)(2,1)}, u32[]{:S(2)}) copy-start(bf16[2,2,128,1024]{3,2,1,0:T(8,128)(2,1)} %get-tuple-element.22.refs_2_) | copy-start | bytes 3145732
  38.5 28.5 %collective-permute-start.7 = (bf16[128,1152]{1,0:T(8,128)(2,1)S(1)}, bf16[128,1152]{1,0:T(8,128)(2,1)S(1)}, u32[]{:S(2)}, u32[]{:S(2)}) collective-permute-start(bf16[128,1152]{1,0:T(8,128)(2,1)S(1)} %get-tuple-element.30.refs_1_), channel_id=1, source_target_pairs={{0,2},{1,3},{2,0},{3,1},{4,6},{5,7},{6,4},{7,5},{8,10},{9,11},{10,... | collective-permute-start | bytes 884744 | tf_op jit(solution)/shard_map/ppermute | solution.py:471
  40.9 26.1 %collective-permute-start.8 = (bf16[128,1152]{1,0:T(8,128)(2,1)S(1)}, bf16[128,1152]{1,0:T(8,128)(2,1)S(1)}, u32[]{:S(2)}, u32[]{:S(2)}) collective-permute-start(bf16[128,1152]{1,0:T(8,128)(2,1)S(1)} %get-tuple-element.30.refs_1_), channel_id=1, source_target_pairs={{0,4},{1,5},{2,6},{3,7},{4,0},{5,1},{6,2},{7,3},{8,12},{9,13},{10,... | collective-permute-start | bytes 884744 | tf_op jit(solution)/shard_map/ppermute | solution.py:471
  43.5 23.5 %collective-permute-start.9 = (bf16[128,1152]{1,0:T(8,128)(2,1)S(1)}, bf16[128,1152]{1,0:T(8,128)(2,1)}, u32[]{:S(2)}, u32[]{:S(2)}) collective-permute-start(bf16[128,1152]{1,0:T(8,128)(2,1)S(1)} %get-tuple-element.30.refs_1_), channel_id=1, source_target_pairs={{0,6},{1,7},{2,4},{3,5},{4,2},{5,3},{6,0},{7,1},{8,14},{9,15},{10,... | collective-permute-start | bytes 884744 | tf_op jit(solution)/shard_map/ppermute | solution.py:471
  44.4 28.7 %collective-permute-start.5 = (bf16[2,128,1024]{2,1,0:T(8,128)(2,1)}, bf16[2,128,1024]{2,1,0:T(8,128)(2,1)}, u32[]{:S(2)}, u32[]{:S(2)}) collective-permute-start(bf16[2,128,1024]{2,1,0:T(8,128)(2,1)} %pad_maximum_fusion.1), channel_id=1, source_target_pairs={{1,0},{2,1},{3,2},{4,3},{5,4},{6,5},{7,6},{9,8},{10,9},{11,10},{12... | collective-permute-start | bytes 1572872 | tf_op jit(solution)/shard_map/ppermute | solution.py:519
  69.6 25.5 %collective-permute-start.10 = (bf16[128,1152]{1,0:T(8,128)(2,1)S(1)}, bf16[128,1152]{1,0:T(8,128)(2,1)S(1)}, u32[]{:S(2)}, u32[]{:S(2)}) collective-permute-start(bf16[128,1152]{1,0:T(8,128)(2,1)S(1)} %get-tuple-element.34.refs_1_), channel_id=1, source_target_pairs={{0,8},{8,0},{16,24},{24,16},{1,9},{9,1},{17,25},{25,17},{2,10},{10... | collective-permute-start | bytes 884744 | tf_op jit(solution)/shard_map/ppermute | solution.py:471
  70.2 24.8 %collective-permute-start.11 = (bf16[128,1152]{1,0:T(8,128)(2,1)S(1)}, bf16[128,1152]{1,0:T(8,128)(2,1)S(1)}, u32[]{:S(2)}, u32[]{:S(2)}) collective-permute-start(bf16[128,1152]{1,0:T(8,128)(2,1)S(1)} %get-tuple-element.34.refs_1_), channel_id=1, source_target_pairs={{0,16},{8,24},{16,0},{24,8},{1,17},{9,25},{17,1},{25,9},{2,18},{10... | collective-permute-start | bytes 884744 | tf_op jit(solution)/shard_map/ppermute | solution.py:471
  71.7 23.3 %collective-permute-start.12 = (bf16[128,1152]{1,0:T(8,128)(2,1)S(1)}, bf16[128,1152]{1,0:T(8,128)(2,1)S(1)}, u32[]{:S(2)}, u32[]{:S(2)}) collective-permute-start(bf16[128,1152]{1,0:T(8,128)(2,1)S(1)} %get-tuple-element.34.refs_1_), channel_id=1, source_target_pairs={{0,24},{8,16},{16,8},{24,0},{1,25},{9,17},{17,9},{25,1},{2,26},{10... | collective-permute-start | bytes 884744 | tf_op jit(solution)/shard_map/ppermute | solution.py:471
  73.1 22.0 %copy-start.2 = (bf16[1024,1024]{1,0:T(8,128)(2,1)S(1)}, bf16[1024,1024]{1,0:T(8,128)(2,1)}, u32[]{:S(2)}) copy-start(bf16[1024,1024]{1,0:T(8,128)(2,1)} %refs_5_.3) | copy-start | bytes 6291460
  97.0 1.6 %collective-permute-start.13 = (bf16[128,1024]{1,0:T(8,128)(2,1)S(1)}, bf16[128,1024]{1,0:T(8,128)(2,1)S(1)}, u32[]{:S(2)}, u32[]{:S(2)}) collective-permute-start(bf16[128,1024]{1,0:T(8,128)(2,1)S(1)} %get-tuple-element.36.refs_1_), channel_id=1, source_target_pairs={{0,1},{1,0},{2,3},{3,2},{4,5},{5,4},{6,7},{7,6},{8,9},{9,8},{10,11... | collective-permute-start | bytes 786440 | tf_op jit(solution)/shard_map/ppermute | solution.py:471

commit v7 on v6

--- a/solution.py
+++ b/solution.py
@@ -45,19 +45,22 @@
 
 def soften(s):
     peak = jnp.max(s, axis=0, keepdims=True)
-    p = jnp.exp2(s - peak)
-    total = jnp.sum(p, axis=0, keepdims=True)
-    return p.astype(BF16), peak, total
-
-
-def pair_context(v, p, inverse, head_width):
-    o = t_matmul(v, p)
+    return jnp.exp2(s - peak).astype(BF16), peak
+
+
+def pair_context(v, p, head_width):
+    wide = 2 * head_width
+    ones = jnp.ones((16, v.shape[0]), BF16)
+    o = matmul(jnp.concatenate([v.T, ones], axis=0), p)
+    total = o[wide : wide + 1]
+    inverse = 1.0 / total
     count = p.shape[1] // 2
-    return [
+    outs = [
         o[j * head_width : (j + 1) * head_width, j * count : (j + 1) * count]
         * inverse[:, j * count : (j + 1) * count]
         for j in range(2)
     ]
+    return outs, total
 
 
 def pack_levels(level):
@@ -102,9 +105,10 @@
 
     outs, levels = [], []
 
-    def context(pair, p, peak, total):
+    def context(pair, p, peak):
         at = slice(pair[0] * head_width, (pair[1] + 1) * head_width)
-        outs.extend(pair_context(v[:count, at], p, 1.0 / total, head_width))
+        found, total = pair_context(v[:count, at], p, head_width)
+        outs.extend(found)
         level = peak + jnp.log2(total)
         levels.extend([level[:, :regs], level[:, regs:]])
 
@@ -300,14 +304,14 @@
         q = q_refs[block // each][inner : inner + blk, at]
         return matmul_t(gathered(0, block, at), spread_heads(q, head_width, range(QUAD)))
 
-    def context(unit, p, inverse):
+    def context(unit, p):
         block, group = unit
         outs = []
         for h in range(0, QUAD, 2):
             at = slice(h * blk, (h + 2) * blk)
             first = group * quad + h * head_width
             v = gathered(1, block, slice(first, first + 2 * head_width))
-            outs += pair_context(v, p[:, at], inverse[:, at], head_width)
+            outs += pair_context(v, p[:, at], head_width)[0]
         at = pl.ds(pl.multiple_of(step * lanes + group * quad, quad), quad)
         ctx_ref[block * blk : (block + 1) * blk, at] = jnp.concatenate(outs, axis=0).astype(BF16).T
 
@@ -320,8 +324,8 @@
             following = score(*units[n + 1])
         if pending is not None:
             context(*pending)
-        p, _, total = soften(s)
-        pending = (unit, p, 1.0 / total)
+        p, _ = soften(s)
+        pending = (unit, p)
     context(*pending)
     if pieces:
         for c in give(step, buf):

time: 101 us -> 101 us (level)
  the two profiles are of different devices: /device:TPU:0 before, /device:TPU:13 now
where the time goes in v7:
time: 101 us
  Pallas kernels  68.8 us (68%)
  starting transfers between devices  21.2 us (21%)
  local copies, waits for them, and re-layouts  4.19 us (4%)
  waiting for transfers between devices  4.06 us (4%)
  other arithmetic  1.72 us (2%)
    pallas_call x2, Pallas kernels, attend(): pl.pallas_call(functools.partial(attend_kernel, head_width, phases, loade...  42.3 us
    pallas_call x1, Pallas kernels, own_project(): pl.pallas_call(functools.partial(own_kernel, scale, head_width), grid_spe...  16.8 us
    ppermute x6, starting transfers between devices, around(): lax.ppermute(x, axis, [(i, (i + step) % n) for i in range(n) if closed or...  13.7 us
    ppermute x8, starting transfers between devices, swap(): lax.ppermute(x, axis, [(i, i ^ n << bit) for i in range(lax.axis_size(axi...  7.5 us
    pallas_call x4, Pallas kernels, small_call(): pl.pallas_call(wrapped, in_specs=[pl.BlockSpec(memory_space=pltpu.SMEM)]...  6.14 us
    ppermute x8, waiting for transfers between devices, swap(): lax.ppermute(x, axis, [(i, i ^ n << bit) for i in range(lax.axis_size(axi...  3.9 us
    pallas_call x1, Pallas kernels, query_project(): pl.pallas_call(functools.partial(query_kernel, scale), grid=(width // lan...  3.6 us
    squeeze x1, local copies, waits for them, and re-layouts, shards(): after = around(normed[0], 'phase', -1, True)  2.37 us
  transfers between devices with their start and end apart: 14, of which 3 were waited for; matrix products, arithmetic and copies ran while one was open for 3% of the time, Pallas kernels for 66%

profile of v7, /device:TPU:13, one launch (start us, length us, event | category | flops | bytes accessed | tf_op | source)
XLA Modules:
  0.0 100.8 jit_solution(9451393151514845099)
XLA Ops:
  0.6 0.0 copy-start
  0.6 2.4 %slice_bitcast_fusion.2 = (bf16[2,128,1024]{2,1,0:T(8,128)(2,1)}, bf16[2,128,1024]{2,1,0:T(8,128)(2,1)}) fusion(bf16[4,2,128,1024]{3,2,1,0:T(8,128)(2,1)} %param.7), kind=kLoop, calls=%fused_computation.4 | loop fusion | bytes 2097152 | tf_op jit(solution)/shard_map/squeeze | solution.py:528
  3.0 1.2 %collective-permute-start.2 = (bf16[2,128,1024]{2,1,0:T(8,128)(2,1)}, bf16[2,128,1024]{2,1,0:T(8,128)(2,1)S(1)}, u32[]{:S(2)}, u32[]{:S(2)}) collective-permute-start(bf16[2,128,1024]{2,1,0:T(8,128)(2,1)} %get-tuple-element.39), channel_id=1, source_target_pairs={{0,8},{8,16},{16,24},{24,0},{1,9},{9,17},{17,25},{25,1},{2,10},{10... | collective-permute-start | bytes 1572872 | tf_op jit(solution)/shard_map/ppermute | solution.py:523
  4.2 1.6 %slice_bitcast_fusion = (bf16[4,128,1024]{2,1,0:T(8,128)(2,1)}, bf16[4,128,1024]{2,1,0:T(8,128)(2,1)}) fusion(bf16[4,2,128,1024]{3,2,1,0:T(8,128)(2,1)S(1)} %copy-done), kind=kLoop, calls=%fused_computation | loop fusion | bytes 4194304 | tf_op jit(solution)/shard_map/squeeze | solution.py:530
  5.9 4.0 %collective-permute-start = (bf16[4,128,1024]{2,1,0:T(8,128)(2,1)}, bf16[4,128,1024]{2,1,0:T(8,128)(2,1)S(1)}, u32[]{:S(2)}, u32[]{:S(2)}) collective-permute-start(bf16[4,128,1024]{2,1,0:T(8,128)(2,1)} %get-tuple-element.41), channel_id=1, source_target_pairs={{0,1},{1,2},{2,3},{3,4},{4,5},{5,6},{6,7},{8,9},{9,10},{10,11},{11... | collective-permute-start | bytes 3145736 | tf_op jit(solution)/shard_map/ppermute | solution.py:523
  9.9 1.9 %collective-permute-start.1 = (bf16[4,128,1024]{2,1,0:T(8,128)(2,1)}, bf16[4,128,1024]{2,1,0:T(8,128)(2,1)}, u32[]{:S(2)}, u32[]{:S(2)}) collective-permute-start(bf16[4,128,1024]{2,1,0:T(8,128)(2,1)} %get-tuple-element.40), channel_id=1, source_target_pairs={{1,0},{2,1},{3,2},{4,3},{5,4},{6,5},{7,6},{9,8},{10,9},{11,10},{12... | collective-permute-start | bytes 3145736 | tf_op jit(solution)/shard_map/ppermute | solution.py:523
  11.8 1.2 %collective-permute-start.3 = (bf16[2,128,1024]{2,1,0:T(8,128)(2,1)}, bf16[2,128,1024]{2,1,0:T(8,128)(2,1)S(1)}, u32[]{:S(2)}, u32[]{:S(2)}) collective-permute-start(bf16[2,128,1024]{2,1,0:T(8,128)(2,1)} %get-tuple-element.38), channel_id=1, source_target_pairs={{0,24},{8,0},{16,8},{24,16},{1,25},{9,1},{17,9},{25,17},{2,26},{10... | collective-permute-start | bytes 1572872 | tf_op jit(solution)/shard_map/ppermute | solution.py:523
  13.0 16.8 %own_project.1 = (bf16[2,24,128,1024]{3,2,1,0:T(8,128)(2,1)}, bf16[2,2,128,1024]{3,2,1,0:T(8,128)(2,1)}, bf16[128,1152]{1,0:T(8,128)(2,1)S(1)}, bf16[128,1152]{1,0:T(8,128)(2,1)S(1)}, f32[8,128]{1,0:T(8,128)S(1)}) custom-call(s32[1]{0:T(128)} %bitcast.1.core_ref.refs_0_, bf16[1024,1024]{1,0:T(8,128)(2,1)} %bitcast.23, bf16[256,1024]{1,0:T(8,128)(2,1)S(1)} %copy-done.6, ...), custom_call_target="tpu_custom_call" | custom-call | flops 1048576 | bytes 65536 | tf_op jit(solution)/shard_map/own_project/pallas_call | solution.py:149
  29.8 0.8 collective-permute-start.6
  30.8 0.8 pad_maximum_fusion
  31.6 3.1 %collective-permute-start.4 = (bf16[2,128,1024]{2,1,0:T(8,128)(2,1)}, bf16[2,128,1024]{2,1,0:T(8,128)(2,1)S(1)}, u32[]{:S(2)}, u32[]{:S(2)}) collective-permute-start(bf16[2,128,1024]{2,1,0:T(8,128)(2,1)} %pad_maximum_fusion), channel_id=1, source_target_pairs={{0,1},{1,2},{2,3},{3,4},{4,5},{5,6},{6,7},{8,9},{9,10},{10,11},{11... | collective-permute-start | bytes 1572872 | tf_op jit(solution)/shard_map/ppermute | solution.py:523
  34.7 0.0 copy-start.7
  34.8 3.6 %query_project.1 = (bf16[1024,1024]{1,0:T(8,128)(2,1)}, f32[8,128]{1,0:T(8,128)S(1)}) custom-call(bf16[1024,1024]{1,0:T(8,128)(2,1)S(1)} %bitcast.24, bf16[1024,1024]{1,0:T(8,128)(2,1)S(1)} %copy-done.3, f32[8,128]{1,0:T(8,128)S(1)} %get-tuple-element.20.refs_0_, bf16[4,128,1024]{2,1,0:T(8,128)(2,1)S(1)} %collective-permute-done.refs_1_, ...), custom_call_target="tpu_custom_call" | custom-call | flops 1048576 | bytes 65536 | tf_op jit(solution)/shard_map/query_project/pallas_call | solution.py:191
  38.4 0.9 register_merge.2
  39.2 0.2 collective-permute-start.7
  39.5 2.3 %collective-permute-start.8 = (bf16[128,1152]{1,0:T(8,128)(2,1)S(1)}, bf16[128,1152]{1,0:T(8,128)(2,1)S(1)}, u32[]{:S(2)}, u32[]{:S(2)}) collective-permute-start(bf16[128,1152]{1,0:T(8,128)(2,1)S(1)} %get-tuple-element.30.refs_1_), channel_id=1, source_target_pairs={{0,4},{1,5},{2,6},{3,7},{4,0},{5,1},{6,2},{7,3},{8,12},{9,13},{10,... | collective-permute-start | bytes 884744 | tf_op jit(solution)/shard_map/ppermute | solution.py:475
  41.8 0.2 collective-permute-start.9
  41.9 0.8 pad_maximum_fusion.1
  42.8 2.2 %collective-permute-start.5 = (bf16[2,128,1024]{2,1,0:T(8,128)(2,1)}, bf16[2,128,1024]{2,1,0:T(8,128)(2,1)}, u32[]{:S(2)}, u32[]{:S(2)}) collective-permute-start(bf16[2,128,1024]{2,1,0:T(8,128)(2,1)} %pad_maximum_fusion.1), channel_id=1, source_target_pairs={{1,0},{2,1},{3,2},{4,3},{5,4},{6,5},{7,6},{9,8},{10,9},{11,10},{12... | collective-permute-start | bytes 1572872 | tf_op jit(solution)/shard_map/ppermute | solution.py:523
  45.1 0.1 reshape.42.idx_ref
  45.2 20.7 %attend.2 = (bf16[2,24,128,1024]{3,2,1,0:T(8,128)(2,1)}, bf16[1024,1024]{1,0:T(8,128)(2,1)}, f32[8,128]{1,0:T(8,128)S(1)}) custom-call(s32[40]{0:T(128)S(1)} %reshape.42.idx_ref, bf16[1024,1024]{1,0:T(8,128)(2,1)} %get-tuple-element.21.refs_0_.refs_1_, bf16[1024,1024]{1,0:T(8,128)(2,1)} %get-tuple-element.21.refs_0_.refs_1_, ...), custom_call_target="tpu_custom_call", output_to_operand_aliasing={{0}: (8, {})} | custom-call | flops 1048576 | bytes 65536 | tf_op jit(solution)/shard_map/attend/pallas_call | solution.py:402
  65.9 2.7 %collective-permute-done.9.refs_4_ = bf16[128,1152]{1,0:T(8,128)(2,1)} collective-permute-done((bf16[128,1152]{1,0:T(8,128)(2,1)S(1)}, bf16[128,1152]{1,0:T(8,128)(2,1)}, u32[]{:S(2)}, u32[]{:S(2)}) %collective-permute-start.9) | collective-permute-done | bytes 294944 | tf_op jit(solution)/shard_map/ppermute | solution.py:475
  68.6 2.5 %register_merge.3 = (bf16[128,1152]{1,0:T(8,128)(2,1)S(1)}, f32[8,128]{1,0:T(8,128)S(1)}) custom-call(s32[1]{0:T(128)} %bitcast.12.refs_0_, bf16[128,1152]{1,0:T(8,128)(2,1)S(1)} %get-tuple-element.30.refs_1_, bf16[128,1152]{1,0:T(8,128)(2,1)S(1)} %collective-permute-done.7.refs_2_, bf16[128,1152]{1,0:T(8,128)(2,1)S(1)} %collective-permute-done.8.refs_3_, ...), custom_call_target="tpu_custom_call" | custom-call | flops 1048576 | bytes 65536 | tf_op jit(solution)/shard_map/register_merge/pallas_call | solution.py:454
  71.1 0.4 collective-permute-start.10
  71.5 0.2 collective-permute-start.11
  71.7 2.1 %collective-permute-start.12 = (bf16[128,1152]{1,0:T(8,128)(2,1)S(1)}, bf16[128,1152]{1,0:T(8,128)(2,1)S(1)}, u32[]{:S(2)}, u32[]{:S(2)}) collective-permute-start(bf16[128,1152]{1,0:T(8,128)(2,1)S(1)} %get-tuple-element.34.refs_1_), channel_id=1, source_target_pairs={{0,24},{8,16},{16,8},{24,0},{1,25},{9,17},{17,9},{25,1},{2,26},{10... | collective-permute-start | bytes 884744 | tf_op jit(solution)/shard_map/ppermute | solution.py:475
  73.8 0.1 collective-permute-done.5
  74.0 21.6 %attend.3 = (bf16[2,24,128,1024]{3,2,1,0:T(8,128)(2,1)}, bf16[1024,1024]{1,0:T(8,128)(2,1)}, f32[8,128]{1,0:T(8,128)S(1)}) custom-call(s32[40]{0:T(128)S(1)} %reshape.42.idx_ref, bf16[1024,1024]{1,0:T(8,128)(2,1)} %get-tuple-element.21.refs_0_.refs_1_, ...), custom_call_target="tpu_custom_call", output_to_operand_aliasing={{0}: (10, {}), {1}: (12, {})} | custom-call | flops 1048576 | bytes 65536 | tf_op jit(solution)/shard_map/attend/pallas_call | solution.py:402
  95.6 1.9 %register_out.1 = (bf16[128,1024]{1,0:T(8,128)(2,1)S(1)}, f32[8,128]{1,0:T(8,128)}) custom-call(s32[1]{0:T(128)} %bitcast.14.refs_0_, bf16[128,1152]{1,0:T(8,128)(2,1)S(1)} %get-tuple-element.34.refs_1_, bf16[128,1152]{1,0:T(8,128)(2,1)S(1)} %collective-permute-done.10.refs_2_, bf16[128,1152]{1,0:T(8,128)(2,1)S(1)} %collective-permute-done.11.refs_3_, ...), custom_call_target="tpu_custom_call" | custom-call | flops 1048576 | bytes 65536 | tf_op jit(solution)/shard_map/register_out/pallas_call | solution.py:454
  97.6 1.2 %collective-permute-start.13 = (bf16[128,1024]{1,0:T(8,128)(2,1)S(1)}, bf16[128,1024]{1,0:T(8,128)(2,1)S(1)}, u32[]{:S(2)}, u32[]{:S(2)}) collective-permute-start(bf16[128,1024]{1,0:T(8,128)(2,1)S(1)} %get-tuple-element.36.refs_1_), channel_id=1, source_target_pairs={{0,1},{1,0},{2,3},{3,2},{4,5},{5,4},{6,7},{7,6},{8,9},{9,8},{10,11... | collective-permute-start | bytes 786440 | tf_op jit(solution)/shard_map/ppermute | solution.py:475
  98.8 1.2 %collective-permute-done.13.refs_2_ = bf16[128,1024]{1,0:T(8,128)(2,1)S(1)} collective-permute-done((bf16[128,1024]{1,0:T(8,128)(2,1)S(1)}, bf16[128,1024]{1,0:T(8,128)(2,1)S(1)}, u32[]{:S(2)}, u32[]{:S(2)}) %collective-permute-start.13) | collective-permute-done | bytes 262176 | tf_op jit(solution)/shard_map/ppermute | solution.py:475
  100.0 0.8 register_join.1
  (28 shorter events, 0.2 us)
Async XLA Ops:
  0.6 3.6 %copy-start = (bf16[4,2,128,1024]{3,2,1,0:T(8,128)(2,1)S(1)}, bf16[4,2,128,1024]{3,2,1,0:T(8,128)(2,1)}, u32[]{:S(2)}) copy-start(bf16[4,2,128,1024]{3,2,1,0:T(8,128)(2,1)} %param.7) | copy-start | bytes 6291460
  3.0 10.0 %copy-start.6 = (bf16[256,1024]{1,0:T(8,128)(2,1)S(1)}, bf16[256,1024]{1,0:T(8,128)(2,1)}, u32[]{:S(2)}) copy-start(bf16[256,1024]{1,0:T(8,128)(2,1)} %refs_1_.1) | copy-start | bytes 1572868
  3.0 27.6 %collective-permute-start.2 = (bf16[2,128,1024]{2,1,0:T(8,128)(2,1)}, bf16[2,128,1024]{2,1,0:T(8,128)(2,1)S(1)}, u32[]{:S(2)}, u32[]{:S(2)}) collective-permute-start(bf16[2,128,1024]{2,1,0:T(8,128)(2,1)} %get-tuple-element.39), channel_id=1, source_target_pairs={{0,8},{8,16},{16,24},{24,0},{1,9},{9,17},{17,25},{25,1},{2,10},{10... | collective-permute-start | bytes 1572872 | tf_op jit(solution)/shard_map/ppermute | solution.py:523
  5.9 28.8 %collective-permute-start = (bf16[4,128,1024]{2,1,0:T(8,128)(2,1)}, bf16[4,128,1024]{2,1,0:T(8,128)(2,1)S(1)}, u32[]{:S(2)}, u32[]{:S(2)}) collective-permute-start(bf16[4,128,1024]{2,1,0:T(8,128)(2,1)} %get-tuple-element.41), channel_id=1, source_target_pairs={{0,1},{1,2},{2,3},{3,4},{4,5},{5,6},{6,7},{8,9},{9,10},{10,11},{11... | collective-permute-start | bytes 3145736 | tf_op jit(solution)/shard_map/ppermute | solution.py:523
  9.9 24.8 %collective-permute-start.1 = (bf16[4,128,1024]{2,1,0:T(8,128)(2,1)}, bf16[4,128,1024]{2,1,0:T(8,128)(2,1)}, u32[]{:S(2)}, u32[]{:S(2)}) collective-permute-start(bf16[4,128,1024]{2,1,0:T(8,128)(2,1)} %get-tuple-element.40), channel_id=1, source_target_pairs={{1,0},{2,1},{3,2},{4,3},{5,4},{6,5},{7,6},{9,8},{10,9},{11,10},{12... | collective-permute-start | bytes 3145736 | tf_op jit(solution)/shard_map/ppermute | solution.py:523
  11.8 18.9 %collective-permute-start.3 = (bf16[2,128,1024]{2,1,0:T(8,128)(2,1)}, bf16[2,128,1024]{2,1,0:T(8,128)(2,1)S(1)}, u32[]{:S(2)}, u32[]{:S(2)}) collective-permute-start(bf16[2,128,1024]{2,1,0:T(8,128)(2,1)} %get-tuple-element.38), channel_id=1, source_target_pairs={{0,24},{8,0},{16,8},{24,16},{1,25},{9,1},{17,9},{25,17},{2,26},{10... | collective-permute-start | bytes 1572872 | tf_op jit(solution)/shard_map/ppermute | solution.py:523
  13.0 21.7 %copy-start.3 = (bf16[1024,1024]{1,0:T(8,128)(2,1)S(1)}, bf16[1024,1024]{1,0:T(8,128)(2,1)}, u32[]{:S(2)}) copy-start(bf16[1024,1024]{1,0:T(8,128)(2,1)} %w_ref.1) | copy-start | bytes 6291460
  29.8 4.9 %copy-start.1 = (bf16[4,2,128,1024]{3,2,1,0:T(8,128)(2,1)S(1)}, bf16[4,2,128,1024]{3,2,1,0:T(8,128)(2,1)}, u32[]{:S(2)}) copy-start(bf16[4,2,128,1024]{3,2,1,0:T(8,128)(2,1)} %param.7) | copy-start | bytes 6291460
  29.8 8.5 %collective-permute-start.6 = (bf16[128,1152]{1,0:T(8,128)(2,1)S(1)}, bf16[128,1152]{1,0:T(8,128)(2,1)S(1)}, u32[]{:S(2)}, u32[]{:S(2)}) collective-permute-start(bf16[128,1152]{1,0:T(8,128)(2,1)S(1)} %get-tuple-element.25), channel_id=1, source_target_pairs={{0,1},{1,0},{2,3},{3,2},{4,5},{5,4},{6,7},{7,6},{8,9},{9,8},{10,11... | collective-permute-start | bytes 884744 | tf_op jit(solution)/shard_map/ppermute | solution.py:475
  31.6 42.2 %collective-permute-start.4 = (bf16[2,128,1024]{2,1,0:T(8,128)(2,1)}, bf16[2,128,1024]{2,1,0:T(8,128)(2,1)S(1)}, u32[]{:S(2)}, u32[]{:S(2)}) collective-permute-start(bf16[2,128,1024]{2,1,0:T(8,128)(2,1)} %pad_maximum_fusion), channel_id=1, source_target_pairs={{0,1},{1,2},{2,3},{3,4},{4,5},{5,6},{6,7},{8,9},{9,10},{10,11},{11... | collective-permute-start | bytes 1572872 | tf_op jit(solution)/shard_map/ppermute | solution.py:523
  34.7 3.7 %copy-start.4 = (bf16[4,128,1024]{2,1,0:T(8,128)(2,1)}, bf16[4,128,1024]{2,1,0:T(8,128)(2,1)S(1)}, u32[]{:S(2)}) copy-start(bf16[4,128,1024]{2,1,0:T(8,128)(2,1)S(1)} %collective-permute-done.refs_1_) | copy-start | bytes 3145732
  34.7 10.3 %copy-start.7 = (s32[4,2,5]{2,1,0:T(2,128)S(1)}, s32[4,2,5]{2,1,0:T(2,128)}, u32[]{:S(2)}) copy-start(s32[4,2,5]{2,1,0:T(2,128)} %param.8) | copy-start | bytes 484
  38.4 6.8 %copy-start.5 = (bf16[2,2,128,1024]{3,2,1,0:T(8,128)(2,1)S(1)}, bf16[2,2,128,1024]{3,2,1,0:T(8,128)(2,1)}, u32[]{:S(2)}) copy-start(bf16[2,2,128,1024]{3,2,1,0:T(8,128)(2,1)} %get-tuple-element.22.refs_2_) | copy-start | bytes 3145732
  39.2 26.6 %collective-permute-start.7 = (bf16[128,1152]{1,0:T(8,128)(2,1)S(1)}, bf16[128,1152]{1,0:T(8,128)(2,1)S(1)}, u32[]{:S(2)}, u32[]{:S(2)}) collective-permute-start(bf16[128,1152]{1,0:T(8,128)(2,1)S(1)} %get-tuple-element.30.refs_1_), channel_id=1, source_target_pairs={{0,2},{1,3},{2,0},{3,1},{4,6},{5,7},{6,4},{7,5},{8,10},{9,11},{10,... | collective-permute-start | bytes 884744 | tf_op jit(solution)/shard_map/ppermute | solution.py:475
  39.5 26.4 %collective-permute-start.8 = (bf16[128,1152]{1,0:T(8,128)(2,1)S(1)}, bf16[128,1152]{1,0:T(8,128)(2,1)S(1)}, u32[]{:S(2)}, u32[]{:S(2)}) collective-permute-start(bf16[128,1152]{1,0:T(8,128)(2,1)S(1)} %get-tuple-element.30.refs_1_), channel_id=1, source_target_pairs={{0,4},{1,5},{2,6},{3,7},{4,0},{5,1},{6,2},{7,3},{8,12},{9,13},{10,... | collective-permute-start | bytes 884744 | tf_op jit(solution)/shard_map/ppermute | solution.py:475
  41.8 26.8 %collective-permute-start.9 = (bf16[128,1152]{1,0:T(8,128)(2,1)S(1)}, bf16[128,1152]{1,0:T(8,128)(2,1)}, u32[]{:S(2)}, u32[]{:S(2)}) collective-permute-start(bf16[128,1152]{1,0:T(8,128)(2,1)S(1)} %get-tuple-element.30.refs_1_), channel_id=1, source_target_pairs={{0,6},{1,7},{2,4},{3,5},{4,2},{5,3},{6,0},{7,1},{8,14},{9,15},{10,... | collective-permute-start | bytes 884744 | tf_op jit(solution)/shard_map/ppermute | solution.py:475
  42.8 31.2 %collective-permute-start.5 = (bf16[2,128,1024]{2,1,0:T(8,128)(2,1)}, bf16[2,128,1024]{2,1,0:T(8,128)(2,1)}, u32[]{:S(2)}, u32[]{:S(2)}) collective-permute-start(bf16[2,128,1024]{2,1,0:T(8,128)(2,1)} %pad_maximum_fusion.1), channel_id=1, source_target_pairs={{1,0},{2,1},{3,2},{4,3},{5,4},{6,5},{7,6},{9,8},{10,9},{11,10},{12... | collective-permute-start | bytes 1572872 | tf_op jit(solution)/shard_map/ppermute | solution.py:523
  71.1 24.5 %collective-permute-start.10 = (bf16[128,1152]{1,0:T(8,128)(2,1)S(1)}, bf16[128,1152]{1,0:T(8,128)(2,1)S(1)}, u32[]{:S(2)}, u32[]{:S(2)}) collective-permute-start(bf16[128,1152]{1,0:T(8,128)(2,1)S(1)} %get-tuple-element.34.refs_1_), channel_id=1, source_target_pairs={{0,8},{8,0},{16,24},{24,16},{1,9},{9,1},{17,25},{25,17},{2,10},{10... | collective-permute-start | bytes 884744 | tf_op jit(solution)/shard_map/ppermute | solution.py:475
  71.5 24.1 %collective-permute-start.11 = (bf16[128,1152]{1,0:T(8,128)(2,1)S(1)}, bf16[128,1152]{1,0:T(8,128)(2,1)S(1)}, u32[]{:S(2)}, u32[]{:S(2)}) collective-permute-start(bf16[128,1152]{1,0:T(8,128)(2,1)S(1)} %get-tuple-element.34.refs_1_), channel_id=1, source_target_pairs={{0,16},{8,24},{16,0},{24,8},{1,17},{9,25},{17,1},{25,9},{2,18},{10... | collective-permute-start | bytes 884744 | tf_op jit(solution)/shard_map/ppermute | solution.py:475
  71.7 23.9 %collective-permute-start.12 = (bf16[128,1152]{1,0:T(8,128)(2,1)S(1)}, bf16[128,1152]{1,0:T(8,128)(2,1)S(1)}, u32[]{:S(2)}, u32[]{:S(2)}) collective-permute-start(bf16[128,1152]{1,0:T(8,128)(2,1)S(1)} %get-tuple-element.34.refs_1_), channel_id=1, source_target_pairs={{0,24},{8,16},{16,8},{24,0},{1,25},{9,17},{17,9},{25,1},{2,26},{10... | collective-permute-start | bytes 884744 | tf_op jit(solution)/shard_map/ppermute | solution.py:475
  74.0 21.7 %copy-start.2 = (bf16[1024,1024]{1,0:T(8,128)(2,1)S(1)}, bf16[1024,1024]{1,0:T(8,128)(2,1)}, u32[]{:S(2)}) copy-start(bf16[1024,1024]{1,0:T(8,128)(2,1)} %refs_5_.3) | copy-start | bytes 6291460
  97.6 2.4 %collective-permute-start.13 = (bf16[128,1024]{1,0:T(8,128)(2,1)S(1)}, bf16[128,1024]{1,0:T(8,128)(2,1)S(1)}, u32[]{:S(2)}, u32[]{:S(2)}) collective-permute-start(bf16[128,1024]{1,0:T(8,128)(2,1)S(1)} %get-tuple-element.36.refs_1_), channel_id=1, source_target_pairs={{0,1},{1,0},{2,3},{3,2},{4,5},{5,4},{6,7},{7,6},{8,9},{9,8},{10,11... | collective-permute-start | bytes 786440 | tf_op jit(solution)/shard_map/ppermute | solution.py:475
